TPU v7x, 256 devices: a whole 4x4x8 slice. The times are simulated.
256 devices in a mesh: ang: 16 (over y, x_lo, core), row: 16 (over z, x_hi).
Axes of the slice: x: 4 (x_hi: 2, x_lo: 2; x = x_hi * 2 + x_lo), y: 4, z: 8, core: 2. Of those that a mesh axis runs over, the one named last changes fastest.
Arguments:
- projections: float32 [256, 256, 4608], P('ang', 'row'), may hold values from -6 to 6
- phase_kernel: float32 [5, 5], replicated, may hold values from -1 to 1
- correlation: int32 [1], replicated, may hold values from 1472 to 1919
- offset: int32 [1], replicated, may hold values from 0 to 448
Outputs:
- sinograms: float32 [256, 128, 8192], P(('row', 'ang'))
All inputs are finite; a program needn't handle non-finite values.
Results may differ from a plain program's by a relative error of at most 0.000076.
Values sent between devices are 32-bit elements; how exact they have to be, the bound alone decides.
No kernel may reach another device: no remote copies, remote signals or barrier semaphores. Data moves between devices by JAX's collectives and lax.ppermute only.
A program may use at most 128 MiB of HBM per device.

v0:
```python
import functools
import math

import jax
import jax.numpy as jnp
import numpy as np
from jax import lax
from jax.experimental import pallas as pl
from jax.experimental.pallas import tpu as pltpu
from jax.sharding import PartitionSpec as P

W = 4608
S = 8192
LANES = 128
SUB = 8
WT = W // LANES
ST = S // LANES
CT = 61
VMEM_LIMIT = 48 * 1024 * 1024

f32 = jnp.float32
bf16 = jnp.bfloat16


def tables():
    k1 = np.arange(64)
    n2 = np.arange(128)
    turn = 2 * np.pi * (k1[:, None] * n2[None, :]) / S
    twiddle = np.stack([np.cos(turn), -np.sin(turn)])
    twiddle = np.repeat(twiddle[:, :, None, :], SUB, axis=2).astype(np.float32)
    freq = k1[:, None] + 64 * n2[None, :]
    gain = 2.0 * np.minimum(freq, S - freq) / S / S
    gain = np.repeat(gain[:, None, :], SUB, axis=1).reshape(64 * SUB, 128).astype(np.float32)
    angle = 2 * np.pi * ((n2[:, None] * n2[None, :]) % 128) / 128
    c, s = np.cos(angle), np.sin(angle)
    forward = np.block([[c, -s], [s, c]]).astype(np.float32)
    return twiddle, gain, forward


def split(matrix):
    high = matrix.astype(jnp.bfloat16)
    low = (matrix - high.astype(np.float32)).astype(jnp.bfloat16)
    return high, low


def cadd(a, b):
    return (a[0] + b[0], a[1] + b[1])


def csub(a, b):
    return (a[0] - b[0], a[1] - b[1])


def turn_quarter(a, sign):
    return (-a[1], a[0]) if sign > 0 else (a[1], -a[0])


def dft4(x0, x1, x2, x3, sign):
    a0, a1 = cadd(x0, x2), csub(x0, x2)
    a2, a3 = cadd(x1, x3), turn_quarter(csub(x1, x3), sign)
    return cadd(a0, a2), cadd(a1, a3), csub(a0, a2), csub(a1, a3)


def dft8(x, sign):
    e = dft4(x[0], x[2], x[4], x[6], sign)
    o = dft4(x[1], x[3], x[5], x[7], sign)
    h = math.sqrt(0.5)
    r, m = o[1]
    o1 = ((r - m) * h, (m + r) * h) if sign > 0 else ((r + m) * h, (m - r) * h)
    o2 = turn_quarter(o[2], sign)
    r, m = o[3]
    o3 = ((r + m) * -h, (r - m) * h) if sign > 0 else ((m - r) * h, (r + m) * -h)
    odd = (o[0], o1, o2, o3)
    return [cadd(e[k], odd[k]) for k in range(4)] + [csub(e[k], odd[k]) for k in range(4)]


def const_turn(a, count, sign):
    count %= 64
    if count == 0:
        return a
    c = math.cos(2 * math.pi * count / 64)
    s = sign * math.sin(2 * math.pi * count / 64)
    return (a[0] * c - a[1] * s, a[0] * s + a[1] * c)


def lane_index():
    return lax.broadcasted_iota(jnp.int32, (SUB, LANES), 1)


def gather_rows(x_hbm, first, up_ref, dn_ref, flat, sems, xs):
    copies = [
        pltpu.make_async_copy(
            x_hbm.at[pl.ds(first, 16 * SUB), t * LANES : (t + 1) * LANES], flat.at[t], sems.at[t]
        )
        for t in range(WT)
    ]
    for copy in copies:
        copy.start()
    for r in range(2):
        for t in range(WT):
            cols = slice(t * LANES, (t + 1) * LANES)
            xs[r, t] = up_ref[r, :, cols]
            xs[18 + r, t] = dn_ref[r, :, cols]

    for copy in copies:
        copy.wait()

    @pl.loop(0, 16)
    def _(r):
        for t in range(WT):
            xs[r + 2, t] = flat[t, pl.ds(r, SUB, stride=16), :]


def filter_row(taps, w_ref, xs, r, store):
    lane = lane_index()
    zero = jnp.zeros((SUB, LANES), f32)
    r0, r1, left, right3, right4 = zero, zero, None, None, None
    for t in range(WT + 1):
        if t < WT:
            rows = [xs[r + i, t] for i in range(5)]
            acc = []
            for j in range(5):
                total = taps[j] * rows[0]
                for i in range(1, 5):
                    total = total + taps[5 * i + j] * rows[i]
                acc.append(total)
            n0, n1 = pltpu.roll(acc[0], 2, 1), pltpu.roll(acc[1], 1, 1)
            n3, n4 = pltpu.roll(acc[3], LANES - 1, 1), pltpu.roll(acc[4], LANES - 2, 1)
        else:
            n3 = n4 = zero
        if t > 0:
            value = left + jnp.where(lane < LANES - 1, right3, n3) + jnp.where(lane < LANES - 2, right4, n4)
            store(t - 1, value * w_ref[t - 1])
        if t < WT:
            left = acc[2] + jnp.where(lane >= 2, n0, r0) + jnp.where(lane >= 1, n1, r1)
            r0, r1, right3, right4 = n0, n1, n3, n4


def stitch(own, opp, put, add, shift):
    lane = lane_index()
    backwards = LANES - 1 - lane
    zero = jnp.zeros((SUB, LANES), f32)
    for t in range(CT):
        put(t, jnp.take_along_axis(opp(WT - 1 - t), backwards, axis=1) if t < WT else zero)
    whole, part = shift // LANES, lax.rem(shift, LANES)
    before = zero
    for t in range(WT + 1):
        now = pltpu.roll(own(t), part, 1) if t < WT else zero
        add(whole + t, jnp.where(lane >= part, now, before))
        before = now


def place(source, sig, side, shift):
    lane = lane_index()
    zero = jnp.zeros((SUB, LANES), f32)
    whole, part = shift // LANES, lax.rem(shift, LANES)
    for t in range(4):
        sig[side, t] = zero
        sig[side, ST - 4 + t] = zero
    before = zero
    for t in range(CT + 1):
        now = pltpu.roll(source(t), part, 1) if t < CT else zero
        sig[side, whole + t] = jnp.where(lane >= part, now, before)
        before = now


def matmul3(x, high, low):
    xh = x.astype(bf16)
    xl = (x - xh.astype(f32)).astype(bf16)
    dot = functools.partial(jnp.dot, preferred_element_type=f32)
    return dot(xh, low) + dot(xl, high) + dot(xh, high)


def ramp(sig, mid, spec, tw_ref, gain_ref, fh, fl, gh, gl, put):
    for b in range(8):
        x = dft8([(sig[0, 8 * a + b], sig[1, 8 * a + b]) for a in range(8)], -1)
        for c in range(8):
            mid[0, 8 * b + c], mid[1, 8 * b + c] = const_turn(x[c], b * c, -1)
    for c in range(8):
        y = dft8([(mid[0, 8 * b + c], mid[1, 8 * b + c]) for b in range(8)], -1)
        for d in range(8):
            k = c + 8 * d
            tr, ti = tw_ref[0, k], tw_ref[1, k]
            re, im = y[d]
            spec[k * SUB : (k + 1) * SUB, :LANES] = re * tr - im * ti
            spec[k * SUB : (k + 1) * SUB, LANES:] = re * ti + im * tr
    step = 128
    for m in range(0, 64 * SUB, step):
        z = matmul3(spec[m : m + step, :], fh[...], fl[...])
        g = gain_ref[m : m + step, :]
        z = z * jnp.concatenate([g, g], axis=1)
        spec[m : m + step, :] = matmul3(z, gh[...], gl[...])
    for c in range(8):
        y = []
        for d in range(8):
            k = c + 8 * d
            tr, ti = tw_ref[0, k], tw_ref[1, k]
            re, im = spec[k * SUB : (k + 1) * SUB, :LANES], spec[k * SUB : (k + 1) * SUB, LANES:]
            y.append((re * tr + im * ti, im * tr - re * ti))
        v = dft8(y, 1)
        for b in range(8):
            mid[0, 8 * b + c], mid[1, 8 * b + c] = const_turn(v[b], b * c, 1)
    for b in range(8):
        s = dft8([(mid[0, 8 * b + c], mid[1, 8 * b + c]) for c in range(8)], 1)
        for a in range(8):
            put(0, 8 * a + b, s[a][0])
            put(1, 8 * a + b, s[a][1])


def filter_kernel(taps_ref, x_hbm, up_ref, dn_ref, w_ref, out_ref, flat, sems, xs):
    first = pl.multiple_of(pl.program_id(0) * 16 * SUB, 16 * SUB)
    gather_rows(x_hbm, first, up_ref, dn_ref, flat, sems, xs)
    taps = [taps_ref[i] for i in range(25)]

    @pl.loop(0, 16)
    def _(r):
        def store(t, value):
            out_ref[r, :, t * LANES : (t + 1) * LANES] = value

        filter_row(taps, w_ref, xs, r, store)


def phase_filter(x, up, dn, taps, weight):
    return pl.pallas_call(
        filter_kernel,
        out_shape=jax.ShapeDtypeStruct((16, 16, W), f32),
        grid=(2,),
        in_specs=[
            pl.BlockSpec(memory_space=pltpu.SMEM),
            pl.BlockSpec(memory_space=pl.ANY),
            pl.BlockSpec((2, SUB, W), lambda o: (0, o, 0)),
            pl.BlockSpec((2, SUB, W), lambda o: (0, o, 0)),
            pl.BlockSpec((WT, SUB, LANES), lambda o: (0, 0, 0)),
        ],
        out_specs=pl.BlockSpec((16, SUB, W), lambda o: (0, o, 0)),
        scratch_shapes=[
            pltpu.VMEM((WT, 16 * SUB, LANES), f32),
            pltpu.SemaphoreType.DMA((WT,)),
            pltpu.VMEM((20, WT, SUB, LANES), f32),
        ],
        compiler_params=pltpu.CompilerParams(vmem_limit_bytes=VMEM_LIMIT),
        name="phase_filter",
    )(taps, x, up, dn, weight)


def ramp_kernel(sizes, own_ref, opp_ref, tw_ref, gain_ref, fh, fl, gh, gl, out_ref, compact, sig, mid, spec):
    shift, off = W - sizes[0], sizes[1]
    for side in range(2):
        rows = slice(side * SUB, (side + 1) * SUB)

        def put(t, v):
            compact[side, t] = v

        def add(t, v):
            compact[side, t] = compact[side, t] + v

        stitch(
            lambda t: own_ref[0, rows, t * LANES : (t + 1) * LANES],
            lambda t: opp_ref[0, rows, t * LANES : (t + 1) * LANES],
            put,
            add,
            shift,
        )
        place(lambda t: compact[side, t], sig, side, off)

    def write(side, n, value):
        out_ref[0, side * SUB : (side + 1) * SUB, n * LANES : (n + 1) * LANES] = value

    ramp(sig, mid, spec, tw_ref, gain_ref, fh, fl, gh, gl, write)


def ramp_scratch():
    return [
        pltpu.VMEM((2, ST + 2, SUB, LANES), f32),
        pltpu.VMEM((2, 64, SUB, LANES), f32),
        pltpu.VMEM((64 * SUB, 2 * LANES), f32),
    ]


def constants():
    twiddle, gain, forward = tables()
    fh, fl = split(forward)
    gh, gl = split(forward.T.copy())
    return [jnp.asarray(v) for v in (twiddle, gain, fh, fl, gh, gl)]


def whole(shape):
    return pl.BlockSpec(shape, lambda *_: (0,) * len(shape))


def stitch_and_ramp(parts, sizes):
    consts = constants()
    return pl.pallas_call(
        ramp_kernel,
        out_shape=jax.ShapeDtypeStruct((1, 128, S), f32),
        grid=(8,),
        in_specs=[
            pl.BlockSpec(memory_space=pltpu.SMEM),
            pl.BlockSpec((1, 16, W), lambda d: (d, 0, 0)),
            pl.BlockSpec((1, 16, W), lambda d: (d + 8, 0, 0)),
        ]
        + [whole(v.shape) for v in consts],
        out_specs=pl.BlockSpec((1, 16, S), lambda d: (0, d, 0)),
        scratch_shapes=[pltpu.VMEM((2, CT, SUB, LANES), f32)] + ramp_scratch(),
        compiler_params=pltpu.CompilerParams(vmem_limit_bytes=VMEM_LIMIT),
        name="stitch_and_ramp",
    )(sizes, parts, parts, *consts)


def shards(projections, phase_kernel, correlation, offset):
    size = lax.axis_size("row")
    up = [(i, i + 1) for i in range(size - 1)]
    down = [(i + 1, i) for i in range(size - 1)]
    before = lax.ppermute(jnp.swapaxes(projections[:, 14:16, :], 0, 1), "row", up)
    after = lax.ppermute(jnp.swapaxes(projections[:, 0:2, :], 0, 1), "row", down)
    column = (jnp.arange(W, dtype=f32) + 0.5) / correlation[0].astype(f32)
    weight = jnp.minimum(column, 1.0).reshape(WT, 1, LANES)
    weight = jnp.broadcast_to(weight, (WT, SUB, LANES))
    sizes = jnp.concatenate([correlation, offset])
    filtered = phase_filter(projections.reshape(256, W), before, after, phase_kernel.reshape(25), weight)
    parts = lax.all_to_all(filtered, "ang", split_axis=0, concat_axis=0, tiled=True)
    return stitch_and_ramp(parts, sizes)


def solution(mesh):
    return jax.shard_map(
        shards,
        mesh=mesh,
        in_specs=(P("ang", "row", None), P(), P(), P()),
        out_specs=P(("row", "ang"), None, None),
        check_vma=False,
    )
```

profile of v0, /device:TPU:128, one launch (start us, length us, event | category | flops | bytes accessed | tf_op | source)
XLA Modules:
  0.0 130.4 jit_solution(17864442715642656813)
XLA Ops:
  0.0 0.0 copy-start.7
  0.0 2.8 %fusion = (f32[16,2,4608]{2,1,0:T(2,128)S(1)}, f32[16,2,4608]{2,1,0:T(2,128)S(1)}) fusion(f32[16,16,4608]{2,1,0:T(8,128)} %param.10), kind=kLoop, calls=%fused_computation.4 | loop fusion | bytes 2359296 | tf_op jit(solution)/shard_map/slice | solution.py:315
  2.8 0.1 copy.18
  2.9 4.9 %collective-permute-start = (f32[2,16,4608]{2,1,0:T(8,128)S(1)}, f32[2,16,4608]{2,1,0:T(8,128)S(1)}, u32[]{:S(2)}, u32[]{:S(2)}) collective-permute-start(f32[2,16,4608]{2,1,0:T(8,128)S(1)} %bitcast.9), channel_id=1, source_target_pairs={{0,1},{1,2},{2,3},{3,4},{4,5},{5,6},{6,7},{7,8},{8,9},{9,10},{10,1... | collective-permute-start | bytes 1769480 | tf_op jit(solution)/shard_map/ppermute | solution.py:314
  7.9 0.1 copy.17
  8.0 4.5 %collective-permute-start.1 = (f32[2,16,4608]{2,1,0:T(8,128)S(1)}, f32[2,16,4608]{2,1,0:T(8,128)S(1)}, u32[]{:S(2)}, u32[]{:S(2)}) collective-permute-start(f32[2,16,4608]{2,1,0:T(8,128)S(1)} %bitcast.10), channel_id=1, source_target_pairs={{1,0},{2,1},{3,2},{4,3},{5,4},{6,5},{7,6},{8,7},{9,8},{10,9},{11,1... | collective-permute-start | bytes 1769480 | tf_op jit(solution)/shard_map/ppermute | solution.py:315
  13.2 0.0 copy-done.7
  13.2 0.1 reshape.18.taps_ref
  13.3 19.8 %collective-permute-done.up_ref = f32[2,16,4608]{2,1,0:T(8,128)S(1)} collective-permute-done((f32[2,16,4608]{2,1,0:T(8,128)S(1)}, f32[2,16,4608]{2,1,0:T(8,128)S(1)}, u32[]{:S(2)}, u32[]{:S(2)}) %collective-permute-start) | collective-permute-done | bytes 589856 | tf_op jit(solution)/shard_map/ppermute | solution.py:314
  33.1 3.1 %collective-permute-done.1.dn_ref = f32[2,16,4608]{2,1,0:T(8,128)S(1)} collective-permute-done((f32[2,16,4608]{2,1,0:T(8,128)S(1)}, f32[2,16,4608]{2,1,0:T(8,128)S(1)}, u32[]{:S(2)}, u32[]{:S(2)}) %collective-permute-start.1) | collective-permute-done | bytes 589856 | tf_op jit(solution)/shard_map/ppermute | solution.py:315
  36.2 16.8 %phase_filter.1 = f32[16,16,4608]{2,1,0:T(8,128)S(1)} custom-call(f32[25]{0:T(128)S(1)} %reshape.18.taps_ref, f32[256,4608]{1,0:T(8,128)} %bitcast.8, f32[2,16,4608]{2,1,0:T(8,128)S(1)} %collective-permute-done.up_ref, f32[2,16,4608]{2,1,0:T(8,128)S(1)} %collective-permute-done.1.dn_ref, f32[36,8,128]{2,1,0:T(8,128)S(1)} %broadcast_in_dim.2.w_ref), custom_call_target="tpu_custom_call" | custom-call | tf_op jit(solution)/shard_map/phase_filter/pallas_call | solution.py:224
  53.0 0.0 copy-start
  53.0 2.2 %copy-done = f32[16,16,4608]{2,1,0:T(8,128)} copy-done((f32[16,16,4608]{2,1,0:T(8,128)}, f32[16,16,4608]{2,1,0:T(8,128)S(1)}, u32[]{:S(2)}) %copy-start) | copy-done | bytes 4718616
  55.2 0.0 copy-start.1
  55.2 0.0 copy-start.2
  55.2 0.0 copy-start.3
  55.2 0.0 copy-start.4
  55.2 0.0 copy-start.5
  55.2 0.0 copy-start.6
  55.2 5.7 %all-to-all-start = ((f32[16,16,4608]{2,1,0:T(8,128)}), f32[16,16,4608]{2,1,0:T(8,128)}, u32[]{:S(2)}, u32[]{:S(2)}) async-start(f32[16,16,4608]{2,1,0:T(8,128)} %copy-done), calls=%async_computation | async-start | bytes 9437184 | tf_op jit(solution)/shard_map/all_to_all | solution.py:321
  61.6 0.1 pad_add_fusion.sizes
  61.6 55.3 %all-to-all-done.own_ref.opp_ref = f32[16,16,4608]{2,1,0:T(8,128)} async-done(((f32[16,16,4608]{2,1,0:T(8,128)}), f32[16,16,4608]{2,1,0:T(8,128)}, u32[]{:S(2)}, u32[]{:S(2)}) %all-to-all-start) | async-done | bytes 4718624 | tf_op jit(solution)/shard_map/all_to_all | solution.py:321
  116.9 0.0 copy-done.1
  116.9 0.0 copy-done.2
  116.9 0.0 copy-done.3
  116.9 0.0 copy-done.4
  117.0 0.0 copy-done.5
  117.0 0.0 copy-done.6
  117.0 13.4 %stitch_and_ramp.1 = f32[1,128,8192]{2,1,0:T(8,128)} custom-call(s32[2]{0:T(128)S(1)} %pad_add_fusion.sizes, f32[16,16,4608]{2,1,0:T(8,128)} %all-to-all-done.own_ref.opp_ref, f32[16,16,4608]{2,1,0:T(8,128)} %all-to-all-done.own_ref.opp_ref, f32[2,64,8,128]{3,2,1,0:T(8,128)S(1)} %copy-done.1, f32[512,128]{1,0:T(8,128)S(1)} %copy-done.2, ...), custom_call_target="tpu_custom_call" | custom-call | tf_op jit(solution)/shard_map/stitch_and_ramp/pallas_call | solution.py:293
  (2 shorter events, 0.0 us)
Async XLA Ops:
  0.0 13.2 %copy-start.7 = (f32[5,5]{1,0:T(8,128)S(1)}, f32[5,5]{1,0:T(8,128)}, u32[]{:S(2)}) copy-start(f32[5,5]{1,0:T(8,128)} %param.11) | copy-start | bytes 304
  2.9 30.1 %collective-permute-start = (f32[2,16,4608]{2,1,0:T(8,128)S(1)}, f32[2,16,4608]{2,1,0:T(8,128)S(1)}, u32[]{:S(2)}, u32[]{:S(2)}) collective-permute-start(f32[2,16,4608]{2,1,0:T(8,128)S(1)} %bitcast.9), channel_id=1, source_target_pairs={{0,1},{1,2},{2,3},{3,4},{4,5},{5,6},{6,7},{7,8},{8,9},{9,10},{10,1... | collective-permute-start | bytes 1769480 | tf_op jit(solution)/shard_map/ppermute | solution.py:314
  8.0 28.2 %collective-permute-start.1 = (f32[2,16,4608]{2,1,0:T(8,128)S(1)}, f32[2,16,4608]{2,1,0:T(8,128)S(1)}, u32[]{:S(2)}, u32[]{:S(2)}) collective-permute-start(f32[2,16,4608]{2,1,0:T(8,128)S(1)} %bitcast.10), channel_id=1, source_target_pairs={{1,0},{2,1},{3,2},{4,3},{5,4},{6,5},{7,6},{8,7},{9,8},{10,9},{11,1... | collective-permute-start | bytes 1769480 | tf_op jit(solution)/shard_map/ppermute | solution.py:315
  53.0 2.2 %copy-start = (f32[16,16,4608]{2,1,0:T(8,128)}, f32[16,16,4608]{2,1,0:T(8,128)S(1)}, u32[]{:S(2)}) copy-start(f32[16,16,4608]{2,1,0:T(8,128)S(1)} %phase_filter.1) | copy-start | bytes 14155780
  55.2 61.8 %copy-start.1 = (f32[2,64,8,128]{3,2,1,0:T(8,128)S(1)}, f32[2,64,8,128]{3,2,1,0:T(8,128)}, u32[]{:S(2)}) copy-start(f32[2,64,8,128]{3,2,1,0:T(8,128)} %constant.21.clone.tw_ref) | copy-start | bytes 1572868
  55.2 61.8 %copy-start.2 = (f32[512,128]{1,0:T(8,128)S(1)}, f32[512,128]{1,0:T(8,128)}, u32[]{:S(2)}) copy-start(f32[512,128]{1,0:T(8,128)} %constant.22.clone.gain_ref) | copy-start | bytes 786436
  55.2 61.8 %copy-start.3 = (bf16[256,256]{1,0:T(8,128)(2,1)S(1)}, bf16[256,256]{1,0:T(8,128)(2,1)}, u32[]{:S(2)}) copy-start(bf16[256,256]{1,0:T(8,128)(2,1)} %constant.26.clone.gl) | copy-start | bytes 393220
  55.2 61.8 %copy-start.4 = (bf16[256,256]{1,0:T(8,128)(2,1)S(1)}, bf16[256,256]{1,0:T(8,128)(2,1)}, u32[]{:S(2)}) copy-start(bf16[256,256]{1,0:T(8,128)(2,1)} %constant.25.clone.gh) | copy-start | bytes 393220
  55.2 61.8 %copy-start.5 = (bf16[256,256]{1,0:T(8,128)(2,1)S(1)}, bf16[256,256]{1,0:T(8,128)(2,1)}, u32[]{:S(2)}) copy-start(bf16[256,256]{1,0:T(8,128)(2,1)} %constant.24.clone.fl) | copy-start | bytes 393220
  55.2 61.8 %copy-start.6 = (bf16[256,256]{1,0:T(8,128)(2,1)S(1)}, bf16[256,256]{1,0:T(8,128)(2,1)}, u32[]{:S(2)}) copy-start(bf16[256,256]{1,0:T(8,128)(2,1)} %constant.23.clone.fh) | copy-start | bytes 393220
  55.2 61.7 %all-to-all-start = ((f32[16,16,4608]{2,1,0:T(8,128)}), f32[16,16,4608]{2,1,0:T(8,128)}, u32[]{:S(2)}, u32[]{:S(2)}) async-start(f32[16,16,4608]{2,1,0:T(8,128)} %copy-done), calls=%async_computation | async-start | bytes 9437184 | tf_op jit(solution)/shard_map/all_to_all | solution.py:321
where the time goes:
time: 131 us; the launch traced here: 130 us
  waiting for transfers between devices  78.2 us (60%)
  Pallas kernels  30.3 us (23%)
  starting transfers between devices  15.1 us (12%)
  local copies, waits for them, and re-layouts  5.32 us (4%)
  between operations  1.42 us (1%)
    all_to_all x1, waiting for transfers between devices, shards(): lax.all_to_all(filtered, 'ang', split_axis=0, concat_axis=0, tiled=True)  55.3 us
    ppermute x1, waiting for transfers between devices, shards(): lax.ppermute(jnp.swapaxes(projections[:, 14:16, :], 0, 1), 'row', up)  19.8 us
    pallas_call x1, Pallas kernels, phase_filter(): pl.pallas_call(filter_kernel, out_shape=jax.ShapeDtypeStruct((16, 16, W),...  16.8 us
    pallas_call x1, Pallas kernels, stitch_and_ramp(): pl.pallas_call(ramp_kernel, out_shape=jax.ShapeDtypeStruct((1, 128, S), f...  13.4 us
    all_to_all x1, starting transfers between devices, shards(): lax.all_to_all(filtered, 'ang', split_axis=0, concat_axis=0, tiled=True)  5.69 us
    ppermute x1, starting transfers between devices, shards(): lax.ppermute(jnp.swapaxes(projections[:, 14:16, :], 0, 1), 'row', up)  4.93 us
    ppermute x1, starting transfers between devices, shards(): lax.ppermute(jnp.swapaxes(projections[:, 0:2, :], 0, 1), 'row', down)  4.52 us
    ppermute x1, waiting for transfers between devices, shards(): lax.ppermute(jnp.swapaxes(projections[:, 0:2, :], 0, 1), 'row', down)  3.07 us
  transfers between devices with their start and end apart: 3, of which 3 were waited for; matrix products, arithmetic and copies ran while one was open for 0% of the time, Pallas kernels for 0%

commit v1 on v0

--- a/solution.py
+++ b/solution.py
@@ -16,7 +16,7 @@
 WT = W // LANES
 ST = S // LANES
 CT = 61
-VMEM_LIMIT = 48 * 1024 * 1024
+VMEM_LIMIT = 60 * 1024 * 1024
 
 f32 = jnp.float32
 bf16 = jnp.bfloat16
@@ -87,10 +87,10 @@
     return lax.broadcasted_iota(jnp.int32, (SUB, LANES), 1)
 
 
-def gather_rows(x_hbm, first, up_ref, dn_ref, flat, sems, xs):
+def gather_rows(x_hbm, first, halo_ref, flat, sems, xs):
     copies = [
         pltpu.make_async_copy(
-            x_hbm.at[pl.ds(first, 16 * SUB), t * LANES : (t + 1) * LANES], flat.at[t], sems.at[t]
+            x_hbm.at[first : first + 16 * SUB, t * LANES : (t + 1) * LANES], flat.at[t], sems.at[t]
         )
         for t in range(WT)
     ]
@@ -99,8 +99,8 @@
     for r in range(2):
         for t in range(WT):
             cols = slice(t * LANES, (t + 1) * LANES)
-            xs[r, t] = up_ref[r, :, cols]
-            xs[18 + r, t] = dn_ref[r, :, cols]
+            xs[r, t] = halo_ref[0, r, :, cols]
+            xs[18 + r, t] = halo_ref[0, r, :, cols]
 
     for copy in copies:
         copy.wait()
@@ -207,74 +207,147 @@
             put(1, 8 * a + b, s[a][1])
 
 
-def filter_kernel(taps_ref, x_hbm, up_ref, dn_ref, w_ref, out_ref, flat, sems, xs):
-    first = pl.multiple_of(pl.program_id(0) * 16 * SUB, 16 * SUB)
-    gather_rows(x_hbm, first, up_ref, dn_ref, flat, sems, xs)
+def whole(shape):
+    return pl.BlockSpec(shape, lambda *_: (0,) * len(shape))
+
+
+def cost(us):
+    return pl.CostEstimate(flops=int(us * 1.15e7), bytes_accessed=1 << 12, transcendentals=0)
+
+
+def halo_kernel(info, x_ref, out_ref):
+    last = info[0] > 0
+    for r in range(2):
+        for t in range(WT):
+            cols = slice(t * LANES, (t + 1) * LANES)
+            out_ref[0, r, :, cols] = jnp.where(last, x_ref[:, 6 + r, cols], x_ref[:, r, cols])
+
+
+def edge_rows(x, last, octet, count):
+    return pl.pallas_call(
+        halo_kernel,
+        out_shape=jax.ShapeDtypeStruct((count, 2, SUB, W), f32),
+        grid_spec=pltpu.PrefetchScalarGridSpec(
+            num_scalar_prefetch=1,
+            grid=(count,),
+            in_specs=[pl.BlockSpec((SUB, SUB, W), lambda o, last: (octet + o, last[0], 0))],
+            out_specs=pl.BlockSpec((1, 2, SUB, W), lambda o, last: (o, 0, 0, 0)),
+        ),
+        compiler_params=pltpu.CompilerParams(vmem_limit_bytes=VMEM_LIMIT),
+        cost_estimate=cost(1.0 * count),
+        name="edge_rows",
+    )(last, x)
+
+
+def nothing(*refs):
+    pass
+
+
+def gate(values, deps):
+    anywhere = pl.BlockSpec(memory_space=pl.ANY)
+    return pl.pallas_call(
+        nothing,
+        out_shape=[jax.ShapeDtypeStruct(v.shape, v.dtype) for v in values],
+        in_specs=[anywhere] * (len(values) + len(deps)),
+        out_specs=[anywhere] * len(values),
+        input_output_aliases={i: i for i in range(len(values))},
+        cost_estimate=cost(0.3),
+        name="gate",
+    )(*values, *deps)
+
+
+def filter_kernel(octet, info, taps_ref, x_hbm, halo_ref, w_ref, *rest):
+    outs, (flat, sems, xs) = rest[-7:-3], rest[-3:]
+    first = octet * 16 * SUB
+    gather_rows(x_hbm, first, halo_ref, flat, sems, xs)
     taps = [taps_ref[i] for i in range(25)]
-
-    @pl.loop(0, 16)
-    def _(r):
-        def store(t, value):
-            out_ref[r, :, t * LANES : (t + 1) * LANES] = value
-
-        filter_row(taps, w_ref, xs, r, store)
-
-
-def phase_filter(x, up, dn, taps, weight):
+    for s in range(4):
+
+        @pl.loop(0, 2)
+        def _(c):
+            def store(t, value):
+                outs[s][0, c, t] = value
+
+            r = lax.rem(info[0] + s, 4) * 4 + info[1] * 2 + c
+            filter_row(taps, w_ref, xs, r, store)
+
+
+def phase_filter(x, halo, taps, weight, info, octet, deps=()):
+    block = (1, 2, WT, SUB, LANES)
+    at = octet if halo.shape[0] > 1 else 0
+    anywhere = pl.BlockSpec(memory_space=pl.ANY)
     return pl.pallas_call(
-        filter_kernel,
-        out_shape=jax.ShapeDtypeStruct((16, 16, W), f32),
-        grid=(2,),
+        functools.partial(filter_kernel, octet),
+        out_shape=[jax.ShapeDtypeStruct(block, f32)] * 4,
+        grid=(1,),
         in_specs=[
             pl.BlockSpec(memory_space=pltpu.SMEM),
-            pl.BlockSpec(memory_space=pl.ANY),
-            pl.BlockSpec((2, SUB, W), lambda o: (0, o, 0)),
-            pl.BlockSpec((2, SUB, W), lambda o: (0, o, 0)),
-            pl.BlockSpec((WT, SUB, LANES), lambda o: (0, 0, 0)),
-        ],
-        out_specs=pl.BlockSpec((16, SUB, W), lambda o: (0, o, 0)),
+            pl.BlockSpec(memory_space=pltpu.SMEM),
+            anywhere,
+            pl.BlockSpec((1, 2, SUB, W), lambda o: (at, 0, 0, 0)),
+            whole((WT, SUB, LANES)),
+        ]
+        + [anywhere] * len(deps),
+        out_specs=[whole(block)] * 4,
         scratch_shapes=[
             pltpu.VMEM((WT, 16 * SUB, LANES), f32),
             pltpu.SemaphoreType.DMA((WT,)),
             pltpu.VMEM((20, WT, SUB, LANES), f32),
         ],
         compiler_params=pltpu.CompilerParams(vmem_limit_bytes=VMEM_LIMIT),
+        cost_estimate=cost(5.0),
         name="phase_filter",
-    )(taps, x, up, dn, weight)
-
-
-def ramp_kernel(sizes, own_ref, opp_ref, tw_ref, gain_ref, fh, fl, gh, gl, out_ref, compact, sig, mid, spec):
-    shift, off = W - sizes[0], sizes[1]
-    for side in range(2):
-        rows = slice(side * SUB, (side + 1) * SUB)
-
-        def put(t, v):
-            compact[side, t] = v
-
-        def add(t, v):
-            compact[side, t] = compact[side, t] + v
-
-        stitch(
-            lambda t: own_ref[0, rows, t * LANES : (t + 1) * LANES],
-            lambda t: opp_ref[0, rows, t * LANES : (t + 1) * LANES],
-            put,
-            add,
-            shift,
-        )
-        place(lambda t: compact[side, t], sig, side, off)
-
-    def write(side, n, value):
-        out_ref[0, side * SUB : (side + 1) * SUB, n * LANES : (n + 1) * LANES] = value
+    )(info, taps, x, halo, weight, *deps)
+
+
+def stitch_kernel(info, r0, r1, r2, r3, *rest):
+    mine, other = rest[-2:]
+    shift, y, core = W - info[0], info[2], info[4]
+    for near, far, place_of in ((r0, r2, y), (r1, r3, lax.rem(y + 3, 4))):
+        near_is_own = place_of < 2
+        half = lax.rem(place_of, 2)
+        for out, row in ((mine, core), (other, 1 - core)):
+
+            def put(t, v):
+                out[half, 0, t] = v
+
+            def add(t, v):
+                out[half, 0, t] = out[half, 0, t] + v
+
+            stitch(
+                lambda t: jnp.where(near_is_own, near[0, row, t], far[0, row, t]),
+                lambda t: jnp.where(near_is_own, far[0, row, t], near[0, row, t]),
+                put,
+                add,
+                shift,
+            )
+
+
+def stitch_pairs(parts, info, deps=()):
+    out = jax.ShapeDtypeStruct((2, 1, CT, SUB, LANES), f32)
+    return pl.pallas_call(
+        stitch_kernel,
+        out_shape=[out, out],
+        in_specs=[pl.BlockSpec(memory_space=pltpu.SMEM)]
+        + [whole((1, 2, WT, SUB, LANES))] * 4
+        + [pl.BlockSpec(memory_space=pl.ANY)] * len(deps),
+        out_specs=[whole((2, 1, CT, SUB, LANES))] * 2,
+        grid=(1,),
+        compiler_params=pltpu.CompilerParams(vmem_limit_bytes=VMEM_LIMIT),
+        cost_estimate=cost(1.5),
+        name="stitch_pairs",
+    )(info, *parts, *deps)
+
+
+def ramp_kernel(octet, info, source, tw_ref, gain_ref, fh, fl, gh, gl, *rest):
+    out_ref, (sig, mid, spec) = rest[-4], rest[-3:]
+    for half in range(2):
+        place(lambda t: source[half, 0, t], sig, half, info[1])
+
+    def write(half, n, value):
+        out_ref[half, 0, 0, 0, :, n * LANES : (n + 1) * LANES] = value
 
     ramp(sig, mid, spec, tw_ref, gain_ref, fh, fl, gh, gl, write)
-
-
-def ramp_scratch():
-    return [
-        pltpu.VMEM((2, ST + 2, SUB, LANES), f32),
-        pltpu.VMEM((2, 64, SUB, LANES), f32),
-        pltpu.VMEM((64 * SUB, 2 * LANES), f32),
-    ]
 
 
 def constants():
@@ -284,42 +357,116 @@
     return [jnp.asarray(v) for v in (twiddle, gain, fh, fl, gh, gl)]
 
 
-def whole(shape):
-    return pl.BlockSpec(shape, lambda *_: (0,) * len(shape))
-
-
-def stitch_and_ramp(parts, sizes):
-    consts = constants()
+def ramp_filter(rows, info, consts, octet, result=None, deps=()):
+    count = rows.shape[1]
+    anywhere = pl.BlockSpec(memory_space=pl.ANY)
+    in_specs = [pl.BlockSpec((2, 1, CT, SUB, LANES), lambda o, info: (0, o, 0, 0, 0))]
+    in_specs += [whole(v.shape) for v in consts] + [anywhere] * len(deps)
+    operands = [rows, *consts, *deps]
+    alias = {}
+    if result is not None:
+        alias = {1 + len(operands): 0}
+        in_specs.append(anywhere)
+        operands.append(result)
     return pl.pallas_call(
-        ramp_kernel,
-        out_shape=jax.ShapeDtypeStruct((1, 128, S), f32),
-        grid=(8,),
-        in_specs=[
-            pl.BlockSpec(memory_space=pltpu.SMEM),
-            pl.BlockSpec((1, 16, W), lambda d: (d, 0, 0)),
-            pl.BlockSpec((1, 16, W), lambda d: (d + 8, 0, 0)),
-        ]
-        + [whole(v.shape) for v in consts],
-        out_specs=pl.BlockSpec((1, 16, S), lambda d: (0, d, 0)),
-        scratch_shapes=[pltpu.VMEM((2, CT, SUB, LANES), f32)] + ramp_scratch(),
+        functools.partial(ramp_kernel, octet),
+        out_shape=jax.ShapeDtypeStruct((2, 2, 2, 2, SUB, S), f32),
+        grid_spec=pltpu.PrefetchScalarGridSpec(
+            num_scalar_prefetch=1,
+            grid=(count,),
+            in_specs=in_specs,
+            out_specs=pl.BlockSpec(
+                (2, 1, 1, 1, SUB, S), lambda o, info: (0, info[5], info[6], octet + o, 0, 0)
+            ),
+            scratch_shapes=[
+                pltpu.VMEM((2, ST + 2, SUB, LANES), f32),
+                pltpu.VMEM((2, 64, SUB, LANES), f32),
+                pltpu.VMEM((64 * SUB, 2 * LANES), f32),
+            ],
+        ),
+        input_output_aliases=alias,
         compiler_params=pltpu.CompilerParams(vmem_limit_bytes=VMEM_LIMIT),
-        name="stitch_and_ramp",
-    )(sizes, parts, parts, *consts)
+        cost_estimate=cost(1.7 * count),
+        name="ramp_filter",
+    )(info, *operands)
+
+
+def y_step(block, s):
+    route = [(i, (i // 4 + s) % 4 * 4 + i % 4) for i in range(16)]
+    return lax.ppermute(block, "ang", route)
+
+
+def flip(block, bits):
+    return lax.ppermute(block, "ang", [(i, i ^ bits) for i in range(16)])
+
+
+def row_step(block, up_side):
+    rows, angs = lax.axis_size("row"), lax.axis_size("ang")
+    route = []
+    for r in range(rows):
+        for a in range(angs):
+            to = r + 1 if a // 2 % 2 == up_side else r - 1
+            if 0 <= to < rows:
+                route.append((a * rows + r, a * rows + to))
+    return lax.ppermute(block, ("ang", "row"), route)
 
 
 def shards(projections, phase_kernel, correlation, offset):
-    size = lax.axis_size("row")
-    up = [(i, i + 1) for i in range(size - 1)]
-    down = [(i + 1, i) for i in range(size - 1)]
-    before = lax.ppermute(jnp.swapaxes(projections[:, 14:16, :], 0, 1), "row", up)
-    after = lax.ppermute(jnp.swapaxes(projections[:, 0:2, :], 0, 1), "row", down)
     column = (jnp.arange(W, dtype=f32) + 0.5) / correlation[0].astype(f32)
     weight = jnp.minimum(column, 1.0).reshape(WT, 1, LANES)
     weight = jnp.broadcast_to(weight, (WT, SUB, LANES))
-    sizes = jnp.concatenate([correlation, offset])
-    filtered = phase_filter(projections.reshape(256, W), before, after, phase_kernel.reshape(25), weight)
-    parts = lax.all_to_all(filtered, "ang", split_axis=0, concat_axis=0, tiled=True)
-    return stitch_and_ramp(parts, sizes)
+    me = lax.axis_index("ang").astype(jnp.uint32)
+    y, x, core = [v.astype(jnp.int32) for v in (me >> 2, (me >> 1) & 1, me & 1)]
+    to_other = jnp.stack([y, 1 - x])
+    to_own = jnp.stack([y, x])
+
+    def info(x_of, core_of):
+        return jnp.stack([correlation[0], offset[0], y, x, core, x_of, core_of])
+
+    flat = projections.reshape(256, W)
+    taps = phase_kernel.reshape(25)
+    consts = constants()
+
+    def y_exchange(parts):
+        return [parts[0]] + [y_step(parts[s], s) for s in (1, 2, 3)]
+
+    near = [row_step(edge_rows(projections, x.reshape(1), o, 1), 1) for o in range(2)]
+    far = row_step(edge_rows(projections, (1 - x).reshape(1), 0, 2), 0)
+
+    same, cross = info(1 - x, core), info(1 - x, 1 - core)
+    keep, swap = info(x, core), info(x, 1 - core)
+
+    def send(rows):
+        return flip(rows[0], 2), flip(rows[1], 3)
+
+    sent_0 = phase_filter(flat, near[0], taps, weight, to_other, 0)
+    parts_0 = y_exchange(sent_0)
+    sent_1 = phase_filter(flat, near[1], taps, weight, to_other, 1, sent_0[1:2])
+    sent_1 = [sent_1[0], *gate(sent_1[1:], parts_0[1:])]
+    parts_1 = y_exchange(sent_1)
+    rows_0 = stitch_pairs(parts_0, same, sent_1[1:2])
+    arrived_0 = send(rows_0)
+    sent_2 = phase_filter(flat, far, taps, weight, to_own, 0, [rows_0[0], sent_1[1]])
+    sent_3 = phase_filter(flat, far, taps, weight, to_own, 1, [sent_2[0]])
+    sent_2 = [sent_2[0], *gate(sent_2[1:], [*parts_1[1:], sent_3[0]])]
+    parts_2 = y_exchange(sent_2)
+    rows_1 = stitch_pairs(parts_1, same, sent_2[1:2])
+    arrived_1 = send(rows_1)
+    result = ramp_filter(arrived_0[0], same, consts, 0, None, [rows_1[0]])
+    result = ramp_filter(arrived_0[1], cross, consts, 0, result)
+    sent_3 = [sent_3[0], *gate(sent_3[1:], [*parts_2[1:], result])]
+    parts_3 = y_exchange(sent_3)
+    rows_2 = stitch_pairs(parts_2, keep, [sent_3[1], arrived_1[0]])
+    swapped_2 = flip(rows_2[1], 1)
+    result = ramp_filter(arrived_1[0], same, consts, 1, result)
+    result = ramp_filter(rows_2[0], keep, consts, 0, result)
+    result = ramp_filter(swapped_2, swap, consts, 0, result)
+    rows_3 = stitch_pairs(parts_3, keep, [result, arrived_1[1]])
+    swapped_3 = flip(rows_3[1], 1)
+    result = ramp_filter(arrived_1[1], cross, consts, 1, result)
+    result = ramp_filter(rows_3[0], keep, consts, 1, result)
+    result = ramp_filter(swapped_3, swap, consts, 1, result)
+    return result.reshape(1, 128, S)
 
 
 def solution(mesh):

time: 131 us -> 136 us (1.038)
  the two profiles are of different devices: /device:TPU:128 before, /device:TPU:121 now
where the time goes in v1:
time: 136 us; the launch traced here: 133 us
  Pallas kernels  79.7 us (59%)
  starting transfers between devices  31.6 us (23%)
  local copies, waits for them, and re-layouts  11.9 us (9%)
  waiting for transfers between devices  7.25 us (5%)
  between operations  1.53 us (1%)
    pallas_call x8, Pallas kernels, ramp_filter(): pl.pallas_call(functools.partial(ramp_kernel, octet), out_shape=jax.Shape...  32.9 us
    pallas_call x4, Pallas kernels, phase_filter(): pl.pallas_call(functools.partial(filter_kernel, octet), out_shape=[jax.Sh...  29.7 us
    ppermute x12, starting transfers between devices, y_step(): return lax.ppermute(block, 'ang', route)  14.2 us
    ppermute x3, starting transfers between devices, row_step(): return lax.ppermute(block, ('ang', 'row'), route)  11.1 us
    pallas_call x4, Pallas kernels, stitch_pairs(): pl.pallas_call(stitch_kernel, out_shape=[out, out], in_specs=[pl.BlockSpe...  10 us
    unnamed x46, local copies, waits for them, and re-layouts  8.06 us
    ppermute x12, waiting for transfers between devices, y_step(): return lax.ppermute(block, 'ang', route)  7.22 us
    pallas_call x3, Pallas kernels, edge_rows(): pl.pallas_call(halo_kernel, out_shape=jax.ShapeDtypeStruct((count, 2, SUB...  6.99 us
  transfers between devices with their start and end apart: 21, of which 2 were waited for; matrix products, arithmetic and copies ran while one was open for 4% of the time, Pallas kernels for 51%

profile of v1, /device:TPU:121, one launch (start us, length us, event | category | flops | bytes accessed | tf_op | source)
XLA Modules:
  0.0 133.2 jit_solution(18249993296461623889)
XLA Ops:
  0.0 2.2 %edge_rows.4 = f32[1,2,8,4608]{3,2,1,0:T(8,128)} custom-call(s32[1]{0:T(128)} %bitcast.1.info, f32[16,16,4608]{2,1,0:T(8,128)} %x_ref.5), custom_call_target="tpu_custom_call" | custom-call | flops 11500000 | bytes 4096 | tf_op jit(solution)/shard_map/edge_rows/pallas_call | solution.py:227
  2.2 4.3 %collective-permute-start.1 = (f32[1,2,8,4608]{3,2,1,0:T(8,128)}, f32[1,2,8,4608]{3,2,1,0:T(8,128)S(1)}, u32[]{:S(2)}, u32[]{:S(2)}) collective-permute-start(f32[1,2,8,4608]{3,2,1,0:T(8,128)} %edge_rows.4), channel_id=1, source_target_pairs={{32,33},{48,49},{96,97},{112,113},{160,161},{176,177},{224,225},{2... | collective-permute-start | bytes 884744 | tf_op jit(solution)/shard_map/ppermute | solution.py:411
  6.5 2.2 %edge_rows.5 = f32[1,2,8,4608]{3,2,1,0:T(8,128)} custom-call(s32[1]{0:T(128)} %bitcast.1.info, f32[16,16,4608]{2,1,0:T(8,128)} %x_ref.5), custom_call_target="tpu_custom_call" | custom-call | flops 11500000 | bytes 4096 | tf_op jit(solution)/shard_map/edge_rows/pallas_call | solution.py:227
  8.7 2.1 %collective-permute-start.5 = (f32[1,2,8,4608]{3,2,1,0:T(8,128)}, f32[1,2,8,4608]{3,2,1,0:T(8,128)S(1)}, u32[]{:S(2)}, u32[]{:S(2)}) collective-permute-start(f32[1,2,8,4608]{3,2,1,0:T(8,128)} %edge_rows.5), channel_id=1, source_target_pairs={{32,33},{48,49},{96,97},{112,113},{160,161},{176,177},{224,225},{2... | collective-permute-start | bytes 884744 | tf_op jit(solution)/shard_map/ppermute | solution.py:411
  10.9 2.6 %edge_rows.3 = f32[2,2,8,4608]{3,2,1,0:T(8,128)} custom-call(s32[1]{0:T(128)} %bitcast.5.info, f32[16,16,4608]{2,1,0:T(8,128)} %x_ref.5), custom_call_target="tpu_custom_call" | custom-call | flops 23000000 | bytes 4096 | tf_op jit(solution)/shard_map/edge_rows/pallas_call | solution.py:227
  13.4 4.6 %collective-permute-start = (f32[2,2,8,4608]{3,2,1,0:T(8,128)}, f32[2,2,8,4608]{3,2,1,0:T(8,128)S(1)}, u32[]{:S(2)}, u32[]{:S(2)}) collective-permute-start(f32[2,2,8,4608]{3,2,1,0:T(8,128)} %edge_rows.3), channel_id=1, source_target_pairs={{0,1},{16,17},{64,65},{80,81},{128,129},{144,145},{192,193},{208,2... | collective-permute-start | bytes 1769480 | tf_op jit(solution)/shard_map/ppermute | solution.py:411
  20.0 0.7 broadcast_in_dim.2.w_ref
  20.8 7.4 %phase_filter.4 = (f32[1,2,36,8,128]{4,3,2,1,0:T(8,128)}, f32[1,2,36,8,128]{4,3,2,1,0:T(8,128)}, f32[1,2,36,8,128]{4,3,2,1,0:T(8,128)}, f32[1,2,36,8,128]{4,3,2,1,0:T(8,128)}) custom-call(s32[2]{0:T(128)} %pad_add_fusion.1.info, f32[25]{0:T(128)} %reshape.26.taps_ref, f32[256,4608]{1,0:T(8,128)} %bitcast.8, f32[1,2,8,4608]{3,2,1,0:T(8,128)} %copy-done.20, ...), custom_call_target="tpu_custom_call" | custom-call | flops 57500000 | bytes 4096 | tf_op jit(solution)/shard_map/phase_filter/pallas_call | solution.py:279
  28.2 1.0 collective-permute-start.3
  29.2 2.7 %collective-permute-start.2 = (f32[1,2,36,8,128]{4,3,2,1,0:T(8,128)}, f32[1,2,36,8,128]{4,3,2,1,0:T(8,128)S(1)}, u32[]{:S(2)}, u32[]{:S(2)}) collective-permute-start(f32[1,2,36,8,128]{4,3,2,1,0:T(8,128)} %get-tuple-element.39.rest_0_), channel_id=1, source_target_pairs={{0,64},{16,80},{32,96},{48,112},{64,128},{80,144},{96,160},{112,17... | collective-permute-start | bytes 884744 | tf_op jit(solution)/shard_map/ppermute | solution.py:396
  33.2 0.7 copy-done.16
  33.9 7.4 %phase_filter.5 = (f32[1,2,36,8,128]{4,3,2,1,0:T(8,128)}, f32[1,2,36,8,128]{4,3,2,1,0:T(8,128)}, f32[1,2,36,8,128]{4,3,2,1,0:T(8,128)}, f32[1,2,36,8,128]{4,3,2,1,0:T(8,128)}) custom-call(s32[2]{0:T(128)} %pad_add_fusion.1.info, f32[25]{0:T(128)} %reshape.26.taps_ref, f32[256,4608]{1,0:T(8,128)} %bitcast.9, f32[1,2,8,4608]{3,2,1,0:T(8,128)} %copy-done.16, ...), custom_call_target="tpu_custom_call" | custom-call | flops 57500000 | bytes 4096 | tf_op jit(solution)/shard_map/phase_filter/pallas_call | solution.py:279
  41.4 3.9 %collective-permute-done.4.refs_5_.r3 = f32[1,2,36,8,128]{4,3,2,1,0:T(8,128)S(1)} collective-permute-done((f32[1,2,36,8,128]{4,3,2,1,0:T(8,128)}, f32[1,2,36,8,128]{4,3,2,1,0:T(8,128)S(1)}, u32[]{:S(2)}, u32[]{:S(2)}) %collective-permute-start.4) | collective-permute-done | bytes 294944 | tf_op jit(solution)/shard_map/ppermute | solution.py:396
  45.3 0.7 copy-done.7
  46.1 1.0 collective-permute-start.7
  47.0 2.7 %collective-permute-start.6 = (f32[1,2,36,8,128]{4,3,2,1,0:T(8,128)}, f32[1,2,36,8,128]{4,3,2,1,0:T(8,128)S(1)}, u32[]{:S(2)}, u32[]{:S(2)}) collective-permute-start(f32[1,2,36,8,128]{4,3,2,1,0:T(8,128)} %get-tuple-element.45.rest_0_.rest_1_), channel_id=1, source_target_pairs={{0,64},{16,80},{32,96},{48,112},{64,128},{80,144},{96,160},{112,17... | collective-permute-start | bytes 884744 | tf_op jit(solution)/shard_map/ppermute | solution.py:396
  49.7 2.5 %stitch_pairs.4 = (f32[2,1,61,8,128]{4,3,2,1,0:T(8,128)}, f32[2,1,61,8,128]{4,3,2,1,0:T(8,128)}) custom-call(s32[7]{0:T(128)} %stack.27.info, f32[1,2,36,8,128]{4,3,2,1,0:T(8,128)} %get-tuple-element.38.r0, f32[1,2,36,8,128]{4,3,2,1,0:T(8,128)} %copy-done.8, f32[1,2,36,8,128]{4,3,2,1,0:T(8,128)} %copy-done.6, f32[1,2,36,8,128]{4,3,2,1,0:T(8,128)} %copy-done.7, ...), custom_call_target="tpu_custom_call" | custom-call | flops 17250000 | bytes 4096 | tf_op jit(solution)/shard_map/stitch_pairs/pallas_call | solution.py:328
  52.2 1.7 %collective-permute-start.13 = (f32[2,1,61,8,128]{4,3,2,1,0:T(8,128)}, f32[2,1,61,8,128]{4,3,2,1,0:T(8,128)S(1)}, u32[]{:S(2)}, u32[]{:S(2)}) collective-permute-start(f32[2,1,61,8,128]{4,3,2,1,0:T(8,128)} %get-tuple-element.46.rest_0_), channel_id=1, source_target_pairs={{0,32},{16,48},{32,0},{48,16},{64,96},{80,112},{96,64},{112,80},{1... | collective-permute-start | bytes 1499144 | tf_op jit(solution)/shard_map/ppermute | solution.py:400
  54.5 1.4 %collective-permute-start.12 = (f32[2,1,61,8,128]{4,3,2,1,0:T(8,128)}, f32[2,1,61,8,128]{4,3,2,1,0:T(8,128)S(1)}, u32[]{:S(2)}, u32[]{:S(2)}) collective-permute-start(f32[2,1,61,8,128]{4,3,2,1,0:T(8,128)} %get-tuple-element.60), channel_id=1, source_target_pairs={{0,48},{16,32},{32,16},{48,0},{64,112},{80,96},{96,80},{112,64},{1... | collective-permute-start | bytes 1499144 | tf_op jit(solution)/shard_map/ppermute | solution.py:400
  55.8 7.4 %phase_filter.6 = (f32[1,2,36,8,128]{4,3,2,1,0:T(8,128)}, f32[1,2,36,8,128]{4,3,2,1,0:T(8,128)}, f32[1,2,36,8,128]{4,3,2,1,0:T(8,128)}, f32[1,2,36,8,128]{4,3,2,1,0:T(8,128)}) custom-call(s32[2]{0:T(128)} %pad_add_fusion.info, f32[25]{0:T(128)} %reshape.26.taps_ref, f32[256,4608]{1,0:T(8,128)} %bitcast.10, f32[2,2,8,4608]{3,2,1,0:T(8,128)} %copy-done, ...), custom_call_target="tpu_custom_call" | custom-call | flops 57500000 | bytes 4096 | tf_op jit(solution)/shard_map/phase_filter/pallas_call | solution.py:279
  63.3 7.4 %phase_filter.7 = (f32[1,2,36,8,128]{4,3,2,1,0:T(8,128)}, f32[1,2,36,8,128]{4,3,2,1,0:T(8,128)}, f32[1,2,36,8,128]{4,3,2,1,0:T(8,128)}, f32[1,2,36,8,128]{4,3,2,1,0:T(8,128)}) custom-call(s32[2]{0:T(128)} %pad_add_fusion.info, f32[25]{0:T(128)} %reshape.26.taps_ref, f32[256,4608]{1,0:T(8,128)} %bitcast.11, f32[2,2,8,4608]{3,2,1,0:T(8,128)} %copy-done, ...), custom_call_target="tpu_custom_call" | custom-call | flops 57500000 | bytes 4096 | tf_op jit(solution)/shard_map/phase_filter/pallas_call | solution.py:279
  70.8 0.7 copy-done.9
  71.7 2.5 %stitch_pairs.5 = (f32[2,1,61,8,128]{4,3,2,1,0:T(8,128)}, f32[2,1,61,8,128]{4,3,2,1,0:T(8,128)}) custom-call(s32[7]{0:T(128)} %stack.27.info, f32[1,2,36,8,128]{4,3,2,1,0:T(8,128)} %get-tuple-element.61.r0, f32[1,2,36,8,128]{4,3,2,1,0:T(8,128)} %copy-done.11, f32[1,2,36,8,128]{4,3,2,1,0:T(8,128)} %copy-done.9, f32[1,2,36,8,128]{4,3,2,1,0:T(8,128)} %copy-done.10, ...), custom_call_target="tpu_custom_call" | custom-call | flops 17250000 | bytes 4096 | tf_op jit(solution)/shard_map/stitch_pairs/pallas_call | solution.py:328
  74.2 1.7 %collective-permute-start.17 = (f32[2,1,61,8,128]{4,3,2,1,0:T(8,128)}, f32[2,1,61,8,128]{4,3,2,1,0:T(8,128)S(1)}, u32[]{:S(2)}, u32[]{:S(2)}) collective-permute-start(f32[2,1,61,8,128]{4,3,2,1,0:T(8,128)} %get-tuple-element.62.rest_0_), channel_id=1, source_target_pairs={{0,32},{16,48},{32,0},{48,16},{64,96},{80,112},{96,64},{112,80},{1... | collective-permute-start | bytes 1499144 | tf_op jit(solution)/shard_map/ppermute | solution.py:400
  75.8 0.7 collective-permute-start.10
  76.9 2.3 %collective-permute-start.9 = (f32[1,2,36,8,128]{4,3,2,1,0:T(8,128)}, f32[1,2,36,8,128]{4,3,2,1,0:T(8,128)S(1)}, u32[]{:S(2)}, u32[]{:S(2)}) collective-permute-start(f32[1,2,36,8,128]{4,3,2,1,0:T(8,128)} %get-tuple-element.57.rest_0_), channel_id=1, source_target_pairs={{0,64},{16,80},{32,96},{48,112},{64,128},{80,144},{96,160},{112,17... | collective-permute-start | bytes 884744 | tf_op jit(solution)/shard_map/ppermute | solution.py:396
  79.9 0.7 stack.29.info
  80.5 4.1 %ramp_filter.8.rest_0_ = f32[2,2,2,2,8,8192]{5,4,3,2,1,0:T(8,128)} custom-call(s32[7]{0:T(128)} %stack.27.info, f32[2,1,61,8,128]{4,3,2,1,0:T(8,128)} %copy-done.12, f32[2,64,8,128]{3,2,1,0:T(8,128)} %constant.32.clone.tw_ref, f32[512,128]{1,0:T(8,128)} %constant.33.clone.gain_ref, bf16[256,256]{1,0:T(8,128)(2,1)} %constant.34.clone.fh, ...), custom_call_target="tpu_custom_call" | custom-call | flops 19550000 | bytes 4096 | tf_op jit(solution)/shard_map/ramp_filter/pallas_call | solution.py:371
  84.6 0.8 copy-done.13
  85.4 4.1 %ramp_filter.9.refs_6_.rest_0_ = f32[2,2,2,2,8,8192]{5,4,3,2,1,0:T(8,128)} custom-call(s32[7]{0:T(128)} %stack.29.info, f32[2,1,61,8,128]{4,3,2,1,0:T(8,128)} %copy-done.13, f32[2,64,8,128]{3,2,1,0:T(8,128)} %constant.32.clone.tw_ref, f32[512,128]{1,0:T(8,128)} %constant.33.clone.gain_ref, ...), custom_call_target="tpu_custom_call", output_to_operand_aliasing={{}: (8, {})} | custom-call | flops 19550000 | bytes 4096 | tf_op jit(solution)/shard_map/ramp_filter/pallas_call | solution.py:371
  89.6 3.3 %collective-permute-done.11.refs_5_.r3 = f32[1,2,36,8,128]{4,3,2,1,0:T(8,128)S(1)} collective-permute-done((f32[1,2,36,8,128]{4,3,2,1,0:T(8,128)}, f32[1,2,36,8,128]{4,3,2,1,0:T(8,128)S(1)}, u32[]{:S(2)}, u32[]{:S(2)}) %collective-permute-start.11) | collective-permute-done | bytes 294944 | tf_op jit(solution)/shard_map/ppermute | solution.py:396
  92.9 0.7 copy-done.4
  93.7 0.8 copy-done.1
  94.5 2.5 %stitch_pairs.6 = (f32[2,1,61,8,128]{4,3,2,1,0:T(8,128)}, f32[2,1,61,8,128]{4,3,2,1,0:T(8,128)}) custom-call(s32[7]{0:T(128)} %stack.25.info, f32[1,2,36,8,128]{4,3,2,1,0:T(8,128)} %get-tuple-element.47.rest_0_.r0, f32[1,2,36,8,128]{4,3,2,1,0:T(8,128)} %copy-done.5, f32[1,2,36,8,128]{4,3,2,1,0:T(8,128)} %copy-done.3, f32[1,2,36,8,128]{4,3,2,1,0:T(8,128)} %copy-done.4, ...), custom_call_target="tpu_custom_call" | custom-call | flops 17250000 | bytes 4096 | tf_op jit(solution)/shard_map/stitch_pairs/pallas_call | solution.py:328
  97.4 0.7 collective-permute-start.15
  98.4 2.4 %collective-permute-start.14 = (f32[1,2,36,8,128]{4,3,2,1,0:T(8,128)}, f32[1,2,36,8,128]{4,3,2,1,0:T(8,128)S(1)}, u32[]{:S(2)}, u32[]{:S(2)}) collective-permute-start(f32[1,2,36,8,128]{4,3,2,1,0:T(8,128)} %get-tuple-element.63.rest_0_), channel_id=1, source_target_pairs={{0,64},{16,80},{32,96},{48,112},{64,128},{80,144},{96,160},{112,17... | collective-permute-start | bytes 884744 | tf_op jit(solution)/shard_map/ppermute | solution.py:396
  101.5 4.1 %ramp_filter.10.rest_0_ = f32[2,2,2,2,8,8192]{5,4,3,2,1,0:T(8,128)} custom-call(s32[7]{0:T(128)} %stack.27.info, f32[2,1,61,8,128]{4,3,2,1,0:T(8,128)} %copy-done.1, f32[2,64,8,128]{3,2,1,0:T(8,128)} %constant.32.clone.tw_ref, f32[512,128]{1,0:T(8,128)} %constant.33.clone.gain_ref, ...), custom_call_target="tpu_custom_call", output_to_operand_aliasing={{}: (8, {})} | custom-call | flops 19550000 | bytes 4096 | tf_op jit(solution)/shard_map/ramp_filter/pallas_call | solution.py:371
  105.6 4.1 %ramp_filter.11.rest_0_ = f32[2,2,2,2,8,8192]{5,4,3,2,1,0:T(8,128)} custom-call(s32[7]{0:T(128)} %stack.25.info, f32[2,1,61,8,128]{4,3,2,1,0:T(8,128)} %get-tuple-element.67.source, f32[2,64,8,128]{3,2,1,0:T(8,128)} %constant.32.clone.tw_ref, f32[512,128]{1,0:T(8,128)} %constant.33.clone.gain_ref, ...), custom_call_target="tpu_custom_call", output_to_operand_aliasing={{}: (8, {})} | custom-call | flops 19550000 | bytes 4096 | tf_op jit(solution)/shard_map/ramp_filter/pallas_call | solution.py:371
  109.7 0.8 copy-done.14
  110.5 4.1 %ramp_filter.12.rest_0_ = f32[2,2,2,2,8,8192]{5,4,3,2,1,0:T(8,128)} custom-call(s32[7]{0:T(128)} %stack.24.info, f32[2,1,61,8,128]{4,3,2,1,0:T(8,128)} %copy-done.14, f32[2,64,8,128]{3,2,1,0:T(8,128)} %constant.32.clone.tw_ref, f32[512,128]{1,0:T(8,128)} %constant.33.clone.gain_ref, ...), custom_call_target="tpu_custom_call", output_to_operand_aliasing={{}: (8, {})} | custom-call | flops 19550000 | bytes 4096 | tf_op jit(solution)/shard_map/ramp_filter/pallas_call | solution.py:371
  114.6 0.7 copy-done.2
  115.6 0.7 copy-done.19
  116.3 2.5 %stitch_pairs.7 = (f32[2,1,61,8,128]{4,3,2,1,0:T(8,128)}, f32[2,1,61,8,128]{4,3,2,1,0:T(8,128)}) custom-call(s32[7]{0:T(128)} %stack.25.info, f32[1,2,36,8,128]{4,3,2,1,0:T(8,128)} %get-tuple-element.48.refs_6_.r0, f32[1,2,36,8,128]{4,3,2,1,0:T(8,128)} %copy-done.19, f32[1,2,36,8,128]{4,3,2,1,0:T(8,128)} %copy-done.17, f32[1,2,36,8,128]{4,3,2,1,0:T(8,128)} %copy-done.18, ...), custom_call_target="tpu_custom_call" | custom-call | flops 17250000 | bytes 4096 | tf_op jit(solution)/shard_map/stitch_pairs/pallas_call | solution.py:328
  118.8 1.2 collective-permute-start.20
  120.1 4.1 %ramp_filter.13.rest_0_ = f32[2,2,2,2,8,8192]{5,4,3,2,1,0:T(8,128)} custom-call(s32[7]{0:T(128)} %stack.29.info, f32[2,1,61,8,128]{4,3,2,1,0:T(8,128)} %copy-done.2, f32[2,64,8,128]{3,2,1,0:T(8,128)} %constant.32.clone.tw_ref, f32[512,128]{1,0:T(8,128)} %constant.33.clone.gain_ref, ...), custom_call_target="tpu_custom_call", output_to_operand_aliasing={{}: (8, {})} | custom-call | flops 19550000 | bytes 4096 | tf_op jit(solution)/shard_map/ramp_filter/pallas_call | solution.py:371
  124.2 4.1 %ramp_filter.14.rest_0_ = f32[2,2,2,2,8,8192]{5,4,3,2,1,0:T(8,128)} custom-call(s32[7]{0:T(128)} %stack.25.info, f32[2,1,61,8,128]{4,3,2,1,0:T(8,128)} %get-tuple-element.70.source, f32[2,64,8,128]{3,2,1,0:T(8,128)} %constant.32.clone.tw_ref, f32[512,128]{1,0:T(8,128)} %constant.33.clone.gain_ref, ...), custom_call_target="tpu_custom_call", output_to_operand_aliasing={{}: (8, {})} | custom-call | flops 19550000 | bytes 4096 | tf_op jit(solution)/shard_map/ramp_filter/pallas_call | solution.py:371
  128.3 0.8 copy-done.15
  129.1 4.1 %ramp_filter.15 = f32[2,2,2,2,8,8192]{5,4,3,2,1,0:T(8,128)} custom-call(s32[7]{0:T(128)} %stack.24.info, f32[2,1,61,8,128]{4,3,2,1,0:T(8,128)} %copy-done.15, f32[2,64,8,128]{3,2,1,0:T(8,128)} %constant.32.clone.tw_ref, f32[512,128]{1,0:T(8,128)} %constant.33.clone.gain_ref, bf16[256,256]{1,0:T(8,128)(2,1)} %constant.34.clone.fh, ...), custom_call_target="tpu_custom_call", output_to_operand_aliasing={{}: (8, {})} | custom-call | flops 19550000 | bytes 4096 | tf_op jit(solution)/shard_map/ramp_filter/pallas_call | solution.py:371
  (71 shorter events, 5.5 us)
Async XLA Ops:
  2.2 17.2 %copy-start.21 = (f32[5,5]{1,0:T(8,128)S(1)}, f32[5,5]{1,0:T(8,128)}, u32[]{:S(2)}) copy-start(f32[5,5]{1,0:T(8,128)} %param.11) | copy-start | bytes 304
  2.2 17.8 %collective-permute-start.1 = (f32[1,2,8,4608]{3,2,1,0:T(8,128)}, f32[1,2,8,4608]{3,2,1,0:T(8,128)S(1)}, u32[]{:S(2)}, u32[]{:S(2)}) collective-permute-start(f32[1,2,8,4608]{3,2,1,0:T(8,128)} %edge_rows.4), channel_id=1, source_target_pairs={{32,33},{48,49},{96,97},{112,113},{160,161},{176,177},{224,225},{2... | collective-permute-start | bytes 884744 | tf_op jit(solution)/shard_map/ppermute | solution.py:411
  8.7 24.4 %collective-permute-start.5 = (f32[1,2,8,4608]{3,2,1,0:T(8,128)}, f32[1,2,8,4608]{3,2,1,0:T(8,128)S(1)}, u32[]{:S(2)}, u32[]{:S(2)}) collective-permute-start(f32[1,2,8,4608]{3,2,1,0:T(8,128)} %edge_rows.5), channel_id=1, source_target_pairs={{32,33},{48,49},{96,97},{112,113},{160,161},{176,177},{224,225},{2... | collective-permute-start | bytes 884744 | tf_op jit(solution)/shard_map/ppermute | solution.py:411
  13.4 41.0 %collective-permute-start = (f32[2,2,8,4608]{3,2,1,0:T(8,128)}, f32[2,2,8,4608]{3,2,1,0:T(8,128)S(1)}, u32[]{:S(2)}, u32[]{:S(2)}) collective-permute-start(f32[2,2,8,4608]{3,2,1,0:T(8,128)} %edge_rows.3), channel_id=1, source_target_pairs={{0,1},{16,17},{64,65},{80,81},{128,129},{144,145},{192,193},{208,2... | collective-permute-start | bytes 1769480 | tf_op jit(solution)/shard_map/ppermute | solution.py:411
  20.0 0.8 copy-start.20
  28.2 13.1 %collective-permute-start.3 = (f32[1,2,36,8,128]{4,3,2,1,0:T(8,128)}, f32[1,2,36,8,128]{4,3,2,1,0:T(8,128)S(1)}, u32[]{:S(2)}, u32[]{:S(2)}) collective-permute-start(f32[1,2,36,8,128]{4,3,2,1,0:T(8,128)} %get-tuple-element.40), channel_id=1, source_target_pairs={{0,128},{16,144},{32,160},{48,176},{64,192},{80,208},{96,224},{112... | collective-permute-start | bytes 884744 | tf_op jit(solution)/shard_map/ppermute | solution.py:396
  29.2 16.0 %collective-permute-start.4 = (f32[1,2,36,8,128]{4,3,2,1,0:T(8,128)}, f32[1,2,36,8,128]{4,3,2,1,0:T(8,128)S(1)}, u32[]{:S(2)}, u32[]{:S(2)}) collective-permute-start(f32[1,2,36,8,128]{4,3,2,1,0:T(8,128)} %get-tuple-element.41), channel_id=1, source_target_pairs={{0,192},{16,208},{32,224},{48,240},{64,0},{80,16},{96,32},{112,48}... | collective-permute-start | bytes 884744 | tf_op jit(solution)/shard_map/ppermute | solution.py:396
  29.2 16.0 %collective-permute-start.2 = (f32[1,2,36,8,128]{4,3,2,1,0:T(8,128)}, f32[1,2,36,8,128]{4,3,2,1,0:T(8,128)S(1)}, u32[]{:S(2)}, u32[]{:S(2)}) collective-permute-start(f32[1,2,36,8,128]{4,3,2,1,0:T(8,128)} %get-tuple-element.39.rest_0_), channel_id=1, source_target_pairs={{0,64},{16,80},{32,96},{48,112},{64,128},{80,144},{96,160},{112,17... | collective-permute-start | bytes 884744 | tf_op jit(solution)/shard_map/ppermute | solution.py:396
  33.2 0.7 copy-start.16
  41.3 3.9 %copy-start.6 = (f32[1,2,36,8,128]{4,3,2,1,0:T(8,128)}, f32[1,2,36,8,128]{4,3,2,1,0:T(8,128)S(1)}, u32[]{:S(2)}) copy-start(f32[1,2,36,8,128]{4,3,2,1,0:T(8,128)S(1)} %collective-permute-done.3.refs_4_.r2) | copy-start | bytes 884740
  45.2 0.7 copy-start.7
  45.3 0.8 copy-start.8
  46.1 24.7 %collective-permute-start.7 = (f32[1,2,36,8,128]{4,3,2,1,0:T(8,128)}, f32[1,2,36,8,128]{4,3,2,1,0:T(8,128)S(1)}, u32[]{:S(2)}, u32[]{:S(2)}) collective-permute-start(f32[1,2,36,8,128]{4,3,2,1,0:T(8,128)} %get-tuple-element.55), channel_id=1, source_target_pairs={{0,128},{16,144},{32,160},{48,176},{64,192},{80,208},{96,224},{112... | collective-permute-start | bytes 884744 | tf_op jit(solution)/shard_map/ppermute | solution.py:396
  47.0 23.7 %collective-permute-start.8 = (f32[1,2,36,8,128]{4,3,2,1,0:T(8,128)}, f32[1,2,36,8,128]{4,3,2,1,0:T(8,128)S(1)}, u32[]{:S(2)}, u32[]{:S(2)}) collective-permute-start(f32[1,2,36,8,128]{4,3,2,1,0:T(8,128)} %get-tuple-element.56), channel_id=1, source_target_pairs={{0,192},{16,208},{32,224},{48,240},{64,0},{80,16},{96,32},{112,48}... | collective-permute-start | bytes 884744 | tf_op jit(solution)/shard_map/ppermute | solution.py:396
  47.0 23.7 %collective-permute-start.6 = (f32[1,2,36,8,128]{4,3,2,1,0:T(8,128)}, f32[1,2,36,8,128]{4,3,2,1,0:T(8,128)S(1)}, u32[]{:S(2)}, u32[]{:S(2)}) collective-permute-start(f32[1,2,36,8,128]{4,3,2,1,0:T(8,128)} %get-tuple-element.45.rest_0_.rest_1_), channel_id=1, source_target_pairs={{0,64},{16,80},{32,96},{48,112},{64,128},{80,144},{96,160},{112,17... | collective-permute-start | bytes 884744 | tf_op jit(solution)/shard_map/ppermute | solution.py:396
  52.2 24.7 %collective-permute-start.13 = (f32[2,1,61,8,128]{4,3,2,1,0:T(8,128)}, f32[2,1,61,8,128]{4,3,2,1,0:T(8,128)S(1)}, u32[]{:S(2)}, u32[]{:S(2)}) collective-permute-start(f32[2,1,61,8,128]{4,3,2,1,0:T(8,128)} %get-tuple-element.46.rest_0_), channel_id=1, source_target_pairs={{0,32},{16,48},{32,0},{48,16},{64,96},{80,112},{96,64},{112,80},{1... | collective-permute-start | bytes 1499144 | tf_op jit(solution)/shard_map/ppermute | solution.py:400
  54.5 1.4 %copy-start = (f32[2,2,8,4608]{3,2,1,0:T(8,128)}, f32[2,2,8,4608]{3,2,1,0:T(8,128)S(1)}, u32[]{:S(2)}) copy-start(f32[2,2,8,4608]{3,2,1,0:T(8,128)S(1)} %collective-permute-done.halo_ref) | copy-start | bytes 1769476
  54.5 30.2 %collective-permute-start.12 = (f32[2,1,61,8,128]{4,3,2,1,0:T(8,128)}, f32[2,1,61,8,128]{4,3,2,1,0:T(8,128)S(1)}, u32[]{:S(2)}, u32[]{:S(2)}) collective-permute-start(f32[2,1,61,8,128]{4,3,2,1,0:T(8,128)} %get-tuple-element.60), channel_id=1, source_target_pairs={{0,48},{16,32},{32,16},{48,0},{64,112},{80,96},{96,80},{112,64},{1... | collective-permute-start | bytes 1499144 | tf_op jit(solution)/shard_map/ppermute | solution.py:400
  70.7 0.7 copy-start.9
  70.8 0.8 copy-start.10
  70.8 0.9 copy-start.11
  74.2 19.5 %collective-permute-start.17 = (f32[2,1,61,8,128]{4,3,2,1,0:T(8,128)}, f32[2,1,61,8,128]{4,3,2,1,0:T(8,128)S(1)}, u32[]{:S(2)}, u32[]{:S(2)}) collective-permute-start(f32[2,1,61,8,128]{4,3,2,1,0:T(8,128)} %get-tuple-element.62.rest_0_), channel_id=1, source_target_pairs={{0,32},{16,48},{32,0},{48,16},{64,96},{80,112},{96,64},{112,80},{1... | collective-permute-start | bytes 1499144 | tf_op jit(solution)/shard_map/ppermute | solution.py:400
  75.8 13.7 %collective-permute-start.10 = (f32[1,2,36,8,128]{4,3,2,1,0:T(8,128)}, f32[1,2,36,8,128]{4,3,2,1,0:T(8,128)S(1)}, u32[]{:S(2)}, u32[]{:S(2)}) collective-permute-start(f32[1,2,36,8,128]{4,3,2,1,0:T(8,128)} %get-tuple-element.58), channel_id=1, source_target_pairs={{0,128},{16,144},{32,160},{48,176},{64,192},{80,208},{96,224},{112... | collective-permute-start | bytes 884744 | tf_op jit(solution)/shard_map/ppermute | solution.py:396
  76.6 16.3 %collective-permute-start.11 = (f32[1,2,36,8,128]{4,3,2,1,0:T(8,128)}, f32[1,2,36,8,128]{4,3,2,1,0:T(8,128)S(1)}, u32[]{:S(2)}, u32[]{:S(2)}) collective-permute-start(f32[1,2,36,8,128]{4,3,2,1,0:T(8,128)} %get-tuple-element.59), channel_id=1, source_target_pairs={{0,192},{16,208},{32,224},{48,240},{64,0},{80,16},{96,32},{112,48}... | collective-permute-start | bytes 884744 | tf_op jit(solution)/shard_map/ppermute | solution.py:396
  76.9 3.6 %copy-start.12 = (f32[2,1,61,8,128]{4,3,2,1,0:T(8,128)}, f32[2,1,61,8,128]{4,3,2,1,0:T(8,128)S(1)}, u32[]{:S(2)}) copy-start(f32[2,1,61,8,128]{4,3,2,1,0:T(8,128)S(1)} %collective-permute-done.13.source) | copy-start | bytes 1499140
  76.9 15.9 %collective-permute-start.9 = (f32[1,2,36,8,128]{4,3,2,1,0:T(8,128)}, f32[1,2,36,8,128]{4,3,2,1,0:T(8,128)S(1)}, u32[]{:S(2)}, u32[]{:S(2)}) collective-permute-start(f32[1,2,36,8,128]{4,3,2,1,0:T(8,128)} %get-tuple-element.57.rest_0_), channel_id=1, source_target_pairs={{0,64},{16,80},{32,96},{48,112},{64,128},{80,144},{96,160},{112,17... | collective-permute-start | bytes 884744 | tf_op jit(solution)/shard_map/ppermute | solution.py:396
  84.6 0.8 copy-start.13
  89.5 7.9 %copy-start.22 = (f32[2,1,61,8,128]{4,3,2,1,0:T(8,128)S(1)}, f32[2,1,61,8,128]{4,3,2,1,0:T(8,128)}, u32[]{:S(2)}) copy-start(f32[2,1,61,8,128]{4,3,2,1,0:T(8,128)} %get-tuple-element.68) | copy-start | bytes 1499140
  89.5 3.3 %copy-start.3 = (f32[1,2,36,8,128]{4,3,2,1,0:T(8,128)}, f32[1,2,36,8,128]{4,3,2,1,0:T(8,128)S(1)}, u32[]{:S(2)}) copy-start(f32[1,2,36,8,128]{4,3,2,1,0:T(8,128)S(1)} %collective-permute-done.10.refs_4_.r2) | copy-start | bytes 884740
  92.9 0.7 copy-start.4
  92.9 0.8 copy-start.5
  93.7 0.8 copy-start.1
  97.0 12.7 %collective-permute-start.18 = (f32[2,1,61,8,128]{4,3,2,1,0:T(8,128)}, f32[2,1,61,8,128]{4,3,2,1,0:T(8,128)S(1)}, u32[]{:S(2)}, u32[]{:S(2)}) collective-permute-start(f32[2,1,61,8,128]{4,3,2,1,0:T(8,128)} %get-tuple-element.66), channel_id=1, source_target_pairs={{0,16},{16,0},{32,48},{48,32},{64,80},{80,64},{96,112},{112,96},{1... | collective-permute-start | bytes 1499144 | tf_op jit(solution)/shard_map/ppermute | solution.py:400
  97.4 17.2 %collective-permute-start.19 = (f32[2,1,61,8,128]{4,3,2,1,0:T(8,128)S(1)}, f32[2,1,61,8,128]{4,3,2,1,0:T(8,128)S(1)}, u32[]{:S(2)}, u32[]{:S(2)}) collective-permute-start(f32[2,1,61,8,128]{4,3,2,1,0:T(8,128)S(1)} %copy-done.22), channel_id=1, source_target_pairs={{0,48},{16,32},{32,16},{48,0},{64,112},{80,96},{96,80},{112,64},{1... | collective-permute-start | bytes 1499144 | tf_op jit(solution)/shard_map/ppermute | solution.py:400
  97.4 17.2 %collective-permute-start.15 = (f32[1,2,36,8,128]{4,3,2,1,0:T(8,128)}, f32[1,2,36,8,128]{4,3,2,1,0:T(8,128)S(1)}, u32[]{:S(2)}, u32[]{:S(2)}) collective-permute-start(f32[1,2,36,8,128]{4,3,2,1,0:T(8,128)} %get-tuple-element.64), channel_id=1, source_target_pairs={{0,128},{16,144},{32,160},{48,176},{64,192},{80,208},{96,224},{112... | collective-permute-start | bytes 884744 | tf_op jit(solution)/shard_map/ppermute | solution.py:396
  98.2 16.5 %collective-permute-start.16 = (f32[1,2,36,8,128]{4,3,2,1,0:T(8,128)}, f32[1,2,36,8,128]{4,3,2,1,0:T(8,128)S(1)}, u32[]{:S(2)}, u32[]{:S(2)}) collective-permute-start(f32[1,2,36,8,128]{4,3,2,1,0:T(8,128)} %get-tuple-element.65), channel_id=1, source_target_pairs={{0,192},{16,208},{32,224},{48,240},{64,0},{80,16},{96,32},{112,48}... | collective-permute-start | bytes 884744 | tf_op jit(solution)/shard_map/ppermute | solution.py:396
  98.4 16.2 %collective-permute-start.14 = (f32[1,2,36,8,128]{4,3,2,1,0:T(8,128)}, f32[1,2,36,8,128]{4,3,2,1,0:T(8,128)S(1)}, u32[]{:S(2)}, u32[]{:S(2)}) collective-permute-start(f32[1,2,36,8,128]{4,3,2,1,0:T(8,128)} %get-tuple-element.63.rest_0_), channel_id=1, source_target_pairs={{0,64},{16,80},{32,96},{48,112},{64,128},{80,144},{96,160},{112,17... | collective-permute-start | bytes 884744 | tf_op jit(solution)/shard_map/ppermute | solution.py:396
  109.7 0.8 copy-start.14
  114.6 0.8 copy-start.2
  114.6 0.9 copy-start.17
  114.6 1.0 copy-start.18
  115.6 0.7 copy-start.19
  118.8 9.5 %collective-permute-start.20 = (f32[2,1,61,8,128]{4,3,2,1,0:T(8,128)}, f32[2,1,61,8,128]{4,3,2,1,0:T(8,128)S(1)}, u32[]{:S(2)}, u32[]{:S(2)}) collective-permute-start(f32[2,1,61,8,128]{4,3,2,1,0:T(8,128)} %get-tuple-element.69), channel_id=1, source_target_pairs={{0,16},{16,0},{32,48},{48,32},{64,80},{80,64},{96,112},{112,96},{1... | collective-permute-start | bytes 1499144 | tf_op jit(solution)/shard_map/ppermute | solution.py:400
  128.3 0.8 copy-start.15

commit v2 on v1

v2 whole, which is shorter than its diff:
```python
import functools
import math

import jax
import jax.numpy as jnp
import numpy as np
from jax import lax
from jax.experimental import pallas as pl
from jax.experimental.pallas import tpu as pltpu
from jax.sharding import PartitionSpec as P

W = 4608
S = 8192
LANES = 128
SUB = 8
WT = W // LANES
ST = S // LANES
CT = 61

f32 = jnp.float32
bf16 = jnp.bfloat16


def tables():
    k1 = np.arange(64)
    n2 = np.arange(128)
    turn = 2 * np.pi * (k1[:, None] * n2[None, :]) / S
    twiddle = np.stack([np.cos(turn), -np.sin(turn)])
    twiddle = np.repeat(twiddle[:, :, None, :], SUB, axis=2).astype(np.float32)
    freq = k1[:, None] + 64 * n2[None, :]
    gain = 2.0 * np.minimum(freq, S - freq) / S / S
    gain = np.repeat(gain[:, None, :], SUB, axis=1).reshape(64 * SUB, 128).astype(np.float32)
    angle = 2 * np.pi * ((n2[:, None] * n2[None, :]) % 128) / 128
    c, s = np.cos(angle), np.sin(angle)
    forward = np.block([[c, -s], [s, c]]).astype(np.float32)
    return twiddle, gain, forward


def split(matrix):
    high = matrix.astype(jnp.bfloat16)
    low = (matrix - high.astype(np.float32)).astype(jnp.bfloat16)
    return high, low


def cadd(a, b):
    return (a[0] + b[0], a[1] + b[1])


def csub(a, b):
    return (a[0] - b[0], a[1] - b[1])


def turn_quarter(a, sign):
    return (-a[1], a[0]) if sign > 0 else (a[1], -a[0])


def dft4(x0, x1, x2, x3, sign):
    a0, a1 = cadd(x0, x2), csub(x0, x2)
    a2, a3 = cadd(x1, x3), turn_quarter(csub(x1, x3), sign)
    return cadd(a0, a2), cadd(a1, a3), csub(a0, a2), csub(a1, a3)


def dft8(x, sign):
    e = dft4(x[0], x[2], x[4], x[6], sign)
    o = dft4(x[1], x[3], x[5], x[7], sign)
    h = math.sqrt(0.5)
    r, m = o[1]
    o1 = ((r - m) * h, (m + r) * h) if sign > 0 else ((r + m) * h, (m - r) * h)
    o2 = turn_quarter(o[2], sign)
    r, m = o[3]
    o3 = ((r + m) * -h, (r - m) * h) if sign > 0 else ((m - r) * h, (r + m) * -h)
    odd = (o[0], o1, o2, o3)
    return [cadd(e[k], odd[k]) for k in range(4)] + [csub(e[k], odd[k]) for k in range(4)]


def const_turn(a, count, sign):
    count %= 64
    if count == 0:
        return a
    c = math.cos(2 * math.pi * count / 64)
    s = sign * math.sin(2 * math.pi * count / 64)
    return (a[0] * c - a[1] * s, a[0] * s + a[1] * c)


def lane_index():
    return lax.broadcasted_iota(jnp.int32, (SUB, LANES), 1)


def filter_row(taps, w_ref, xs, r, store):
    lane = lane_index()
    zero = jnp.zeros((SUB, LANES), f32)
    r0, r1, left, right3, right4 = zero, zero, None, None, None
    for t in range(WT + 1):
        if t < WT:
            rows = [xs[r + i, t] for i in range(5)]
            acc = []
            for j in range(5):
                total = taps[j] * rows[0]
                for i in range(1, 5):
                    total = total + taps[5 * i + j] * rows[i]
                acc.append(total)
            n0, n1 = pltpu.roll(acc[0], 2, 1), pltpu.roll(acc[1], 1, 1)
            n3, n4 = pltpu.roll(acc[3], LANES - 1, 1), pltpu.roll(acc[4], LANES - 2, 1)
        else:
            n3 = n4 = zero
        if t > 0:
            value = left + jnp.where(lane < LANES - 1, right3, n3) + jnp.where(lane < LANES - 2, right4, n4)
            store(t - 1, value * w_ref[t - 1])
        if t < WT:
            left = acc[2] + jnp.where(lane >= 2, n0, r0) + jnp.where(lane >= 1, n1, r1)
            r0, r1, right3, right4 = n0, n1, n3, n4


def stitch(own, opp, put, add, shift):
    lane = lane_index()
    backwards = LANES - 1 - lane
    zero = jnp.zeros((SUB, LANES), f32)
    for t in range(CT):
        put(t, jnp.take_along_axis(opp(WT - 1 - t), backwards, axis=1) if t < WT else zero)
    whole, part = shift // LANES, lax.rem(shift, LANES)
    before = zero
    for t in range(WT + 1):
        now = pltpu.roll(own(t), part, 1) if t < WT else zero
        add(whole + t, jnp.where(lane >= part, now, before))
        before = now


def place(source, sig, side, shift):
    lane = lane_index()
    zero = jnp.zeros((SUB, LANES), f32)
    whole, part = shift // LANES, lax.rem(shift, LANES)
    for t in range(4):
        sig[side, t] = zero
        sig[side, ST - 4 + t] = zero
    before = zero
    for t in range(CT + 1):
        now = pltpu.roll(source(t), part, 1) if t < CT else zero
        sig[side, whole + t] = jnp.where(lane >= part, now, before)
        before = now


def matmul3(x, high, low):
    xh = x.astype(bf16)
    xl = (x - xh.astype(f32)).astype(bf16)
    dot = functools.partial(jnp.dot, preferred_element_type=f32)
    return dot(xh, low) + dot(xl, high) + dot(xh, high)


def ramp(sig, mid, spec, tw_ref, gain_ref, fh, fl, gh, gl, put):
    for b in range(8):
        x = dft8([(sig[0, 8 * a + b], sig[1, 8 * a + b]) for a in range(8)], -1)
        for c in range(8):
            mid[0, 8 * b + c], mid[1, 8 * b + c] = const_turn(x[c], b * c, -1)
    for c in range(8):
        y = dft8([(mid[0, 8 * b + c], mid[1, 8 * b + c]) for b in range(8)], -1)
        for d in range(8):
            k = c + 8 * d
            tr, ti = tw_ref[0, k], tw_ref[1, k]
            re, im = y[d]
            spec[k * SUB : (k + 1) * SUB, :LANES] = re * tr - im * ti
            spec[k * SUB : (k + 1) * SUB, LANES:] = re * ti + im * tr
    step = 128
    for m in range(0, 64 * SUB, step):
        z = matmul3(spec[m : m + step, :], fh[...], fl[...])
        g = gain_ref[m : m + step, :]
        z = z * jnp.concatenate([g, g], axis=1)
        spec[m : m + step, :] = matmul3(z, gh[...], gl[...])
    for c in range(8):
        y = []
        for d in range(8):
            k = c + 8 * d
            tr, ti = tw_ref[0, k], tw_ref[1, k]
            re, im = spec[k * SUB : (k + 1) * SUB, :LANES], spec[k * SUB : (k + 1) * SUB, LANES:]
            y.append((re * tr + im * ti, im * tr - re * ti))
        v = dft8(y, 1)
        for b in range(8):
            mid[0, 8 * b + c], mid[1, 8 * b + c] = const_turn(v[b], b * c, 1)
    for b in range(8):
        s = dft8([(mid[0, 8 * b + c], mid[1, 8 * b + c]) for c in range(8)], 1)
        for a in range(8):
            put(0, 8 * a + b, s[a][0])
            put(1, 8 * a + b, s[a][1])


def whole(shape):
    return pl.BlockSpec(shape, lambda *_: (0,) * len(shape))


def cost(us):
    return pl.CostEstimate(flops=int(us * 1.15e7), bytes_accessed=1 << 12, transcendentals=0)


def limit(mib):
    return pltpu.CompilerParams(vmem_limit_bytes=mib * 1024 * 1024)


SMEM = pl.BlockSpec(memory_space=pltpu.SMEM)
ANYWHERE = pl.BlockSpec(memory_space=pl.ANY)
TOKEN = jax.ShapeDtypeStruct((SUB, LANES), f32)
TOKEN_SPEC = whole((SUB, LANES))
ROWS = (16, WT, SUB, LANES)


def gather_kernel(x_hbm, out_ref, token, flat, sems):
    octet = pl.program_id(0)
    first = pl.multiple_of(octet * 16 * SUB, 16 * SUB)
    copies = [
        pltpu.make_async_copy(
            x_hbm.at[pl.ds(first, 16 * SUB), t * LANES : (t + 1) * LANES], flat.at[t], sems.at[t]
        )
        for t in range(WT)
    ]
    for copy in copies:
        copy.start()
    for copy in copies:
        copy.wait()
    for r in range(16):
        for t in range(WT):
            out_ref[0, r, t] = flat[t, pl.ds(r, SUB, stride=16), :]
    token[...] = jnp.zeros_like(token)


def gather_rows(x):
    return pl.pallas_call(
        gather_kernel,
        out_shape=[jax.ShapeDtypeStruct((2,) + ROWS, f32), TOKEN],
        grid=(2,),
        in_specs=[ANYWHERE],
        out_specs=[pl.BlockSpec((1,) + ROWS, lambda o: (o, 0, 0, 0, 0)), TOKEN_SPEC],
        scratch_shapes=[pltpu.VMEM((WT, 16 * SUB, LANES), f32), pltpu.SemaphoreType.DMA((WT,))],
        compiler_params=limit(16),
        cost_estimate=cost(3.0),
        name="gather_rows",
    )(x)


def filter_kernel(octet, other, info, taps_ref, xt_hbm, halo_ref, *rest):
    outs, token, edge = rest[-11:-7], rest[-7], rest[-6]
    in_sem, xs, ys, weight, out_sems = rest[-5:]
    step = pl.program_id(0)
    load = pltpu.make_async_copy(xt_hbm.at[octet + step], xs.at[2:18], in_sem)
    load.start()
    for r in range(2):
        for t in range(WT):
            if other:
                value = halo_ref[r, :, t * LANES : (t + 1) * LANES]
            else:
                value = halo_ref[0, r, t]
            xs[r, t] = value
            xs[18 + r, t] = value
    taps = [taps_ref[i, j] for i in range(5) for j in range(5)]
    overlap = info[0].astype(f32)
    lane = lane_index().astype(f32) + 0.5
    for t in range(WT):
        weight[t] = jnp.minimum((lane + t * LANES) / overlap, 1.0)
    token[...] = jnp.zeros_like(token)
    x_of = 1 - info[3] if other else info[3]
    load.wait()
    if other:
        top = 2 + 14 * (1 - info[3])
        for r in range(2):
            for t in range(WT):
                edge[0, r, t] = xs[top + r, t]
    else:
        edge[...] = jnp.zeros_like(edge)

    @pl.loop(0, 8)
    def _(i):
        def store(t, value):
            ys[i, t] = value

        r = lax.rem(info[2] + i // 2, 4) * 4 + x_of * 2 + lax.rem(i, 2)
        filter_row(taps, weight, xs, r, store)
        for s in range(4):

            @pl.when(i == 2 * s + 1)
            def _():
                pltpu.make_async_copy(ys.at[2 * s : 2 * s + 2], outs[s].at[step], out_sems.at[s]).start()

    for s in range(4):
        pltpu.make_async_copy(ys.at[2 * s : 2 * s + 2], outs[s].at[step], out_sems.at[s]).wait()


def phase_filter(xt, halo, taps, info, octet, count, other, deps=()):
    if other:
        halo_spec = pl.BlockSpec((2, SUB, W), lambda o: (0, octet + o, 0))
        edge = (1, 2, WT, SUB, LANES)
    else:
        halo_spec = pl.BlockSpec((1, 2, WT, SUB, LANES), lambda o: (octet + o, 0, 0, 0, 0))
        edge = (SUB, LANES)
    return pl.pallas_call(
        functools.partial(filter_kernel, octet, other),
        out_shape=[jax.ShapeDtypeStruct((count, 2, WT, SUB, LANES), f32)] * 4
        + [TOKEN, jax.ShapeDtypeStruct(edge, f32)],
        grid=(count,),
        in_specs=[SMEM, SMEM, ANYWHERE, halo_spec] + [ANYWHERE] * len(deps),
        out_specs=[ANYWHERE] * 4 + [TOKEN_SPEC, whole(edge)],
        scratch_shapes=[
            pltpu.SemaphoreType.DMA,
            pltpu.VMEM((20, WT, SUB, LANES), f32),
            pltpu.VMEM((8, WT, SUB, LANES), f32),
            pltpu.VMEM((WT, SUB, LANES), f32),
            pltpu.SemaphoreType.DMA((4,)),
        ],
        compiler_params=limit(12),
        cost_estimate=cost(5.0),
        name="phase_filter",
    )(info, taps, xt, halo, *deps)


def stitch_kernel(info, r0, r1, r2, r3, *rest):
    mine, crossing, token = rest[-3:]
    token[...] = jnp.zeros_like(token)
    shift, y, core = W - info[0], info[2], info[4]
    for near, far, place_of in ((r0, r2, y), (r1, r3, lax.rem(y + 3, 4))):
        near_is_own = place_of < 2
        half = lax.rem(place_of, 2)
        for out, row in ((mine, core), (crossing, 1 - core)):

            def put(t, v):
                out[half, 0, t] = v

            def add(t, v):
                out[half, 0, t] = out[half, 0, t] + v

            stitch(
                lambda t: jnp.where(near_is_own, near[0, row, t], far[0, row, t]),
                lambda t: jnp.where(near_is_own, far[0, row, t], near[0, row, t]),
                put,
                add,
                shift,
            )


def stitch_pairs(parts, info, deps=()):
    count = parts[0].shape[0]
    out = jax.ShapeDtypeStruct((2, count, CT, SUB, LANES), f32)
    return pl.pallas_call(
        stitch_kernel,
        out_shape=[out, out, TOKEN],
        in_specs=[SMEM]
        + [pl.BlockSpec((1, 2, WT, SUB, LANES), lambda o: (o, 0, 0, 0, 0))] * 4
        + [ANYWHERE] * len(deps),
        out_specs=[pl.BlockSpec((2, 1, CT, SUB, LANES), lambda o: (0, o, 0, 0, 0))] * 2 + [TOKEN_SPEC],
        grid=(count,),
        compiler_params=limit(8),
        cost_estimate=cost(1.5),
        name="stitch_pairs",
    )(info, *parts, *deps)


SLOTS = 5


def ramp_kernel(sources, info, *refs):
    rows, (tw_ref, gain_ref, fh, fl, gh, gl) = refs[:sources], refs[sources : sources + 6]
    out_ref, token, (sig, mid, spec) = refs[-5], refs[-4], refs[-3:]
    token[...] = jnp.zeros_like(token)
    steps = [(source, which) for source in rows for which in range(source.shape[1])]
    for n, (source, which) in enumerate(steps):

        @pl.when(pl.program_id(0) == n)
        def _():
            for half in range(2):
                place(lambda t: source[half, which, t], sig, half, info[1])

    def write(half, n, value):
        out_ref[half, 0, 0, 0, :, n * LANES : (n + 1) * LANES] = value

    ramp(sig, mid, spec, tw_ref, gain_ref, fh, fl, gh, gl, write)


def constants():
    twiddle, gain, forward = tables()
    fh, fl = split(forward)
    gh, gl = split(forward.T.copy())
    return [jnp.asarray(v) for v in (twiddle, gain, fh, fl, gh, gl)]


def ramp_filter(rows, info, consts, slot, result=None, deps=()):
    steps = sum(v.shape[1] for v in rows)
    local = pl.BlockSpec(memory_space=pltpu.VMEM)
    in_specs = [local] * (len(rows) + len(consts)) + [ANYWHERE] * len(deps)
    operands = [*rows, *consts, *deps]
    alias = {}
    if result is not None:
        alias = {1 + len(operands): 0}
        in_specs.append(ANYWHERE)
        operands.append(result)

    def target(i, info):
        at = SLOTS + 3 * (slot + i)
        return (0, info[at], info[at + 1], info[at + 2], 0, 0)

    return pl.pallas_call(
        functools.partial(ramp_kernel, len(rows)),
        out_shape=[jax.ShapeDtypeStruct((2, 2, 2, 2, SUB, S), f32), TOKEN],
        grid_spec=pltpu.PrefetchScalarGridSpec(
            num_scalar_prefetch=1,
            grid=(steps,),
            in_specs=in_specs,
            out_specs=[pl.BlockSpec((2, 1, 1, 1, SUB, S), target), whole((SUB, LANES))],
            scratch_shapes=[
                pltpu.VMEM((2, ST + 2, SUB, LANES), f32),
                pltpu.VMEM((2, 64, SUB, LANES), f32),
                pltpu.VMEM((64 * SUB, 2 * LANES), f32),
            ],
        ),
        input_output_aliases=alias,
        compiler_params=limit(16),
        cost_estimate=cost(2.0),
        name="ramp_filter",
    )(info, *operands)


def y_step(block, s):
    route = [(i, (i // 4 + s) % 4 * 4 + i % 4) for i in range(16)]
    return lax.ppermute(block, "ang", route)


def flip(block, bits):
    return lax.ppermute(block, "ang", [(i, i ^ bits) for i in range(16)])


def row_step(block, up_side):
    rows, angs = lax.axis_size("row"), lax.axis_size("ang")
    route = []
    for r in range(rows):
        for a in range(angs):
            to = r + 1 if a // 2 % 2 == up_side else r - 1
            if 0 <= to < rows:
                route.append((a * rows + r, a * rows + to))
    return lax.ppermute(block, ("ang", "row"), route)


def shards(projections, phase_kernel, correlation, offset):
    me = lax.axis_index("ang").astype(jnp.uint32)
    y, x, core = [v.astype(jnp.int32) for v in (me >> 2, (me >> 1) & 1, me & 1)]
    slots = []
    for x_of, core_of, octet in (
        (1 - x, core, 0),
        (1 - x, 1 - core, 0),
        (x, core, 0),
        (x, core, 1),
        (1 - x, core, 1),
        (x, 1 - core, 0),
        (x, 1 - core, 1),
        (1 - x, 1 - core, 1),
    ):
        slots += [x_of, core_of, jnp.int32(octet)]
    info = jnp.stack([correlation[0], offset[0], y, x, core] + slots)
    consts = constants()

    def y_exchange(parts):
        return [parts[0]] + [y_step(parts[s], s) for s in (1, 2, 3)]

    def send(rows):
        return flip(rows[0], 2), flip(rows[1], 3)

    near = lax.dynamic_slice_in_dim(projections, 14 * x, 2, axis=1)
    near = row_step(jnp.swapaxes(near, 0, 1), 1)
    xt, gathered = gather_rows(projections.reshape(256, W))
    *sent_0, done, edge_0 = phase_filter(xt, near, phase_kernel, info, 0, 1, True)
    parts_0 = y_exchange(sent_0)
    *sent_1, done, edge_1 = phase_filter(xt, near, phase_kernel, info, 1, 1, True, [done])
    parts_1 = y_exchange(sent_1)
    far = row_step(jnp.concatenate([edge_0, edge_1], axis=0), 0)
    *rows_0, done = stitch_pairs(parts_0, info, [done])
    arrived_0 = send(rows_0)
    *sent_2, done, _ = phase_filter(xt, far, phase_kernel, info, 0, 2, False, [done])
    parts_2 = y_exchange(sent_2)
    *rows_1, done = stitch_pairs(parts_1, info, [done])
    arrived_1 = send(rows_1)
    result, done = ramp_filter(arrived_0, info, consts, 0, None, [done])
    *rows_2, done = stitch_pairs(parts_2, info, [done, arrived_1[0][0, 0, 0]])
    swapped = flip(rows_2[1], 1)
    result, done = ramp_filter([rows_2[0], arrived_1[0]], info, consts, 2, result)
    result, done = ramp_filter([swapped, arrived_1[1]], info, consts, 5, result)
    return result.reshape(1, 128, S)


def solution(mesh):
    return jax.shard_map(
        shards,
        mesh=mesh,
        in_specs=(P("ang", "row", None), P(), P(), P()),
        out_specs=P(("row", "ang"), None, None),
        check_vma=False,
    )
```

time: 136 us -> 117 us (0.86); the launches traced: 133 us -> 116 us
  Pallas kernels: 79.7 us -> 36.8 us
  waiting for transfers between devices: 7.25 us -> 43.2 us
  local copies, waits for them, and re-layouts: 11.9 us -> 4.48 us
  starting transfers between devices: 31.6 us -> 29.8 us
    pallas_call x22 -> x10, Pallas kernels: 79.7 us -> 36.8 us  [the longest x3 15.3 us: phase_filter(): pl.pallas_call(functools.partial(filter_kernel, octet, other), out_shape=...]
    ppermute x6 -> x5, waiting for transfers between devices: 0.02 us -> 19.8 us  [flip(): return lax.ppermute(block, 'ang', [(i, i ^ bits) for i in range(16)])]
    ppermute x3 -> x2, waiting for transfers between devices: 0.01 us -> 8.51 us  [row_step(): return lax.ppermute(block, ('ang', 'row'), route)]
    ppermute x12 -> x9, waiting for transfers between devices: 7.22 us -> 14.8 us  [y_step(): return lax.ppermute(block, 'ang', route)]
    ppermute x12 -> x9, starting transfers between devices: 14.2 us -> 7.9 us  [y_step(): return lax.ppermute(block, 'ang', route)]
    unnamed x46 -> x17, local copies, waits for them, and re-layouts: 8.06 us -> 2.49 us
    ppermute x6 -> x5, starting transfers between devices: 6.38 us -> 10.8 us  [flip(): return lax.ppermute(block, 'ang', [(i, i ^ bits) for i in range(16)])]
    another operation x4 -> x1, local copies, waits for them, and re-layouts: 2.47 us -> 0.1 us  [shards(): info = jnp.stack([correlation[0], offset[0], y, x, core] + slots)]
  transfers between devices with their start and end apart: 21 -> 16, of which waited for: 2 -> 8; matrix products, arithmetic and copies ran while one was open for 4% -> 0% of each run, Pallas kernels for 51% -> 22%
where the time goes in v2:
time: 117 us; the launch traced here: 116 us
  waiting for transfers between devices  43.2 us (37%)
  Pallas kernels  36.8 us (31%)
  starting transfers between devices  29.8 us (25%)
  local copies, waits for them, and re-layouts  4.48 us (4%)
  between operations  1.53 us (1%)
    ppermute x5, waiting for transfers between devices, flip(): return lax.ppermute(block, 'ang', [(i, i ^ bits) for i in range(16)])  19.8 us
    pallas_call x3, Pallas kernels, phase_filter(): pl.pallas_call(functools.partial(filter_kernel, octet, other), out_shape=...  15.3 us
    ppermute x9, waiting for transfers between devices, y_step(): return lax.ppermute(block, 'ang', route)  14.8 us
    pallas_call x3, Pallas kernels, ramp_filter(): pl.pallas_call(functools.partial(ramp_kernel, len(rows)), out_shape=[jax....  14.4 us
    ppermute x2, starting transfers between devices, row_step(): return lax.ppermute(block, ('ang', 'row'), route)  11.1 us
    ppermute x5, starting transfers between devices, flip(): return lax.ppermute(block, 'ang', [(i, i ^ bits) for i in range(16)])  10.8 us
    ppermute x2, waiting for transfers between devices, row_step(): return lax.ppermute(block, ('ang', 'row'), route)  8.51 us
    ppermute x9, starting transfers between devices, y_step(): return lax.ppermute(block, 'ang', route)  7.9 us
  transfers between devices with their start and end apart: 16, of which 8 were waited for; matrix products, arithmetic and copies ran while one was open for 0% of the time, Pallas kernels for 22%

profile of v2, /device:TPU:121, one launch (start us, length us, event | category | flops | bytes accessed | tf_op | source)
XLA Modules:
  0.0 115.8 jit_solution(3453825638479406651)
XLA Ops:
  0.0 1.9 %constant_dynamic-slice_fusion = f32[16,2,4608]{2,1,0:T(2,128)S(1)} fusion(f32[16,16,4608]{2,1,0:T(8,128)} %param.10, s32[]{:T(128)S(6)} %select_n.3), kind=kLoop, calls=%fused_computation.3 | loop fusion | bytes 1179652 | tf_op jit(solution)/shard_map/dynamic_slice | solution.py:460
  1.9 0.1 copy.16
  2.0 4.2 %collective-permute-start = (f32[2,16,4608]{2,1,0:T(8,128)S(1)}, f32[2,16,4608]{2,1,0:T(8,128)S(1)}, u32[]{:S(2)}, u32[]{:S(2)}) collective-permute-start(f32[2,16,4608]{2,1,0:T(8,128)S(1)} %bitcast.13), channel_id=1, source_target_pairs={{32,33},{48,49},{96,97},{112,113},{160,161},{176,177},{224,225},{2... | collective-permute-start | bytes 1769480 | tf_op jit(solution)/shard_map/ppermute | solution.py:433
  7.5 0.1 stack.17.info
  7.6 0.0 copy-start
  7.6 2.3 %copy-done = f32[16,16,4608]{2,1,0:T(8,128)S(1)} copy-done((f32[16,16,4608]{2,1,0:T(8,128)S(1)}, f32[16,16,4608]{2,1,0:T(8,128)}, u32[]{:S(2)}) %copy-start) | copy-done | bytes 4718616
  10.0 3.2 %gather_rows.1 = (f32[2,16,36,8,128]{4,3,2,1,0:T(8,128)S(1)}, f32[8,128]{1,0:T(8,128)}) custom-call(f32[256,4608]{1,0:T(8,128)S(1)} %bitcast.12), custom_call_target="tpu_custom_call" | custom-call | flops 34500000 | bytes 4096 | tf_op jit(solution)/shard_map/gather_rows/pallas_call | solution.py:224
  13.2 6.4 %collective-permute-done.halo_ref = f32[2,16,4608]{2,1,0:T(8,128)S(1)} collective-permute-done((f32[2,16,4608]{2,1,0:T(8,128)S(1)}, f32[2,16,4608]{2,1,0:T(8,128)S(1)}, u32[]{:S(2)}, u32[]{:S(2)}) %collective-permute-start) | collective-permute-done | bytes 589856 | tf_op jit(solution)/shard_map/ppermute | solution.py:433
  19.6 3.9 %phase_filter.3 = (f32[1,2,36,8,128]{4,3,2,1,0:T(8,128)S(1)}, f32[1,2,36,8,128]{4,3,2,1,0:T(8,128)S(1)}, f32[1,2,36,8,128]{4,3,2,1,0:T(8,128)S(1)}, f32[1,2,36,8...) custom-call(s32[29]{0:T(128)S(1)} %stack.17.info, f32[5,5]{1,0:T(8,128)S(1)} %copy-done.7, ...), custom_call_target="tpu_custom_call" | custom-call | flops 57500000 | bytes 4096 | tf_op jit(solution)/shard_map/phase_filter/pallas_call | solution.py:291
  23.5 0.1 collective-permute-start.2
  23.6 2.2 %collective-permute-start.3 = (f32[1,2,36,8,128]{4,3,2,1,0:T(8,128)S(1)}, f32[1,2,36,8,128]{4,3,2,1,0:T(8,128)S(1)}, u32[]{:S(2)}, u32[]{:S(2)}) collective-permute-start(f32[1,2,36,8,128]{4,3,2,1,0:T(8,128)S(1)} %get-tuple-element.41), channel_id=1, source_target_pairs={{0,128},{16,144},{32,160},{48,176},{64,192},{80,208},{96,224},{112... | collective-permute-start | bytes 884744 | tf_op jit(solution)/shard_map/ppermute | solution.py:418
  25.8 0.0 collective-permute-start.4
  25.8 3.9 %phase_filter.4 = (f32[1,2,36,8,128]{4,3,2,1,0:T(8,128)S(1)}, f32[1,2,36,8,128]{4,3,2,1,0:T(8,128)S(1)}, f32[1,2,36,8,128]{4,3,2,1,0:T(8,128)S(1)}, f32[1,2,36,8...) custom-call(s32[29]{0:T(128)S(1)} %stack.17.info, f32[5,5]{1,0:T(8,128)S(1)} %copy-done.7, ...), custom_call_target="tpu_custom_call" | custom-call | flops 57500000 | bytes 4096 | tf_op jit(solution)/shard_map/phase_filter/pallas_call | solution.py:291
  29.7 0.0 copy-start.1
  29.7 0.0 copy-start.2
  29.7 0.0 copy-start.3
  29.7 0.0 copy-start.4
  29.7 0.0 copy-start.5
  29.7 0.0 copy-start.6
  29.8 6.9 %collective-permute-start.1 = (f32[2,2,36,8,128]{4,3,2,1,0:T(8,128)S(1)}, f32[2,2,36,8,128]{4,3,2,1,0:T(8,128)S(1)}, u32[]{:S(2)}, u32[]{:S(2)}) collective-permute-start(f32[2,2,36,8,128]{4,3,2,1,0:T(8,128)S(1)} %pad_maximum_fusion), channel_id=1, source_target_pairs={{0,1},{16,17},{64,65},{80,81},{128,129},{144,145},{192,193},{208,2... | collective-permute-start | bytes 1769480 | tf_op jit(solution)/shard_map/ppermute | solution.py:433
  36.7 0.0 collective-permute-done.2.r1
  36.7 0.0 collective-permute-done.3.r2
  36.7 3.6 %collective-permute-done.4.r3 = f32[1,2,36,8,128]{4,3,2,1,0:T(8,128)S(1)} collective-permute-done((f32[1,2,36,8,128]{4,3,2,1,0:T(8,128)S(1)}, f32[1,2,36,8,128]{4,3,2,1,0:T(8,128)S(1)}, u32[]{:S(2)}, u32[]{:S(2)}) %collective-permute-start.4) | collective-permute-done | bytes 294944 | tf_op jit(solution)/shard_map/ppermute | solution.py:418
  40.3 0.9 stitch_pairs.3
  41.3 2.2 %collective-permute-start.8 = (f32[2,1,61,8,128]{4,3,2,1,0:T(8,128)S(1)}, f32[2,1,61,8,128]{4,3,2,1,0:T(8,128)S(1)}, u32[]{:S(2)}, u32[]{:S(2)}) collective-permute-start(f32[2,1,61,8,128]{4,3,2,1,0:T(8,128)S(1)} %get-tuple-element.49), channel_id=1, source_target_pairs={{0,32},{16,48},{32,0},{48,16},{64,96},{80,112},{96,64},{112,80},{1... | collective-permute-start | bytes 1499144 | tf_op jit(solution)/shard_map/ppermute | solution.py:422
  43.5 0.0 collective-permute-start.10
  43.5 0.8 collective-permute-start.11
  44.2 0.9 collective-permute-start.12
  45.1 2.1 %collective-permute-done.1.halo_ref = f32[2,2,36,8,128]{4,3,2,1,0:T(8,128)S(1)} collective-permute-done((f32[2,2,36,8,128]{4,3,2,1,0:T(8,128)S(1)}, f32[2,2,36,8,128]{4,3,2,1,0:T(8,128)S(1)}, u32[]{:S(2)}, u32[]{:S(2)}) %collective-permute-start.1) | collective-permute-done | bytes 589856 | tf_op jit(solution)/shard_map/ppermute | solution.py:433
  47.2 6.3 %collective-permute-start.9 = (f32[2,1,61,8,128]{4,3,2,1,0:T(8,128)S(1)}, f32[2,1,61,8,128]{4,3,2,1,0:T(8,128)S(1)}, u32[]{:S(2)}, u32[]{:S(2)}) collective-permute-start(f32[2,1,61,8,128]{4,3,2,1,0:T(8,128)S(1)} %get-tuple-element.50), channel_id=1, source_target_pairs={{0,48},{16,32},{32,16},{48,0},{64,112},{80,96},{96,80},{112,64},{1... | collective-permute-start | bytes 1499144 | tf_op jit(solution)/shard_map/ppermute | solution.py:422
  53.5 7.6 %phase_filter.5 = (f32[2,2,36,8,128]{4,3,2,1,0:T(8,128)S(1)}, f32[2,2,36,8,128]{4,3,2,1,0:T(8,128)S(1)}, f32[2,2,36,8,128]{4,3,2,1,0:T(8,128)S(1)}, f32[2,2,36,8...) custom-call(s32[29]{0:T(128)S(1)} %stack.17.info, f32[5,5]{1,0:T(8,128)S(1)} %copy-done.7, ...), custom_call_target="tpu_custom_call" | custom-call | flops 57500000 | bytes 4096 | tf_op jit(solution)/shard_map/phase_filter/pallas_call | solution.py:291
  61.1 0.0 collective-permute-done.12.r3
  61.1 0.9 stitch_pairs.4
  62.0 0.8 collective-permute-start.13
  62.8 3.0 %collective-permute-start.5 = (f32[2,2,36,8,128]{4,3,2,1,0:T(8,128)S(1)}, f32[2,2,36,8,128]{4,3,2,1,0:T(8,128)S(1)}, u32[]{:S(2)}, u32[]{:S(2)}) collective-permute-start(f32[2,2,36,8,128]{4,3,2,1,0:T(8,128)S(1)} %get-tuple-element.46), channel_id=1, source_target_pairs={{0,64},{16,80},{32,96},{48,112},{64,128},{80,144},{96,160},{112,17... | collective-permute-start | bytes 1769480 | tf_op jit(solution)/shard_map/ppermute | solution.py:418
  65.8 0.1 collective-permute-start.6
  65.9 0.9 collective-permute-start.7
  66.8 6.3 %collective-permute-done.9.refs_1_ = f32[2,1,61,8,128]{4,3,2,1,0:T(8,128)S(1)} collective-permute-done((f32[2,1,61,8,128]{4,3,2,1,0:T(8,128)S(1)}, f32[2,1,61,8,128]{4,3,2,1,0:T(8,128)S(1)}, u32[]{:S(2)}, u32[]{:S(2)}) %collective-permute-start.9) | collective-permute-done | bytes 499744 | tf_op jit(solution)/shard_map/ppermute | solution.py:422
  73.1 3.9 %ramp_filter.3 = (f32[2,2,2,2,8,8192]{5,4,3,2,1,0:T(8,128)}, f32[8,128]{1,0:T(8,128)S(1)}) custom-call(s32[29]{0:T(128)S(1)} %stack.17.info, f32[2,1,61,8,128]{4,3,2,1,0:T(8,128)S(1)} %collective-permute-done.8.refs_0_, f32[2,1,61,8,128]{4,3,2,1,0:T(8,128)S(1)} %collective-permute-done.9.refs_1_, f32[2,64,8,128]{3,2,1,0:T(8,128)S(1)} %copy-done.1, ...), custom_call_target="tpu_custom_call" | custom-call | flops 23000000 | bytes 4096 | tf_op jit(solution)/shard_map/ramp_filter/pallas_call | solution.py:395
  77.1 6.6 %collective-permute-done.13.refs_1_ = f32[2,1,61,8,128]{4,3,2,1,0:T(8,128)S(1)} collective-permute-done((f32[2,1,61,8,128]{4,3,2,1,0:T(8,128)S(1)}, f32[2,1,61,8,128]{4,3,2,1,0:T(8,128)S(1)}, u32[]{:S(2)}, u32[]{:S(2)}) %collective-permute-start.13) | collective-permute-done | bytes 499744 | tf_op jit(solution)/shard_map/ppermute | solution.py:422
  83.7 7.7 %collective-permute-done.5.r1 = f32[2,2,36,8,128]{4,3,2,1,0:T(8,128)S(1)} collective-permute-done((f32[2,2,36,8,128]{4,3,2,1,0:T(8,128)S(1)}, f32[2,2,36,8,128]{4,3,2,1,0:T(8,128)S(1)}, u32[]{:S(2)}, u32[]{:S(2)}) %collective-permute-start.5) | collective-permute-done | bytes 589856 | tf_op jit(solution)/shard_map/ppermute | solution.py:418
  91.3 3.5 %collective-permute-done.7.r3 = f32[2,2,36,8,128]{4,3,2,1,0:T(8,128)S(1)} collective-permute-done((f32[2,2,36,8,128]{4,3,2,1,0:T(8,128)S(1)}, f32[2,2,36,8,128]{4,3,2,1,0:T(8,128)S(1)}, u32[]{:S(2)}, u32[]{:S(2)}) %collective-permute-start.7) | collective-permute-done | bytes 589856 | tf_op jit(solution)/shard_map/ppermute | solution.py:418
  94.8 2.1 %stitch_pairs.5 = (f32[2,2,61,8,128]{4,3,2,1,0:T(8,128)S(1)}, f32[2,2,61,8,128]{4,3,2,1,0:T(8,128)S(1)}, f32[8,128]{1,0:T(8,128)}) custom-call(s32[29]{0:T(128)S(1)} %stack.17.info, f32[2,2,36,8,128]{4,3,2,1,0:T(8,128)S(1)} %get-tuple-element.45.r0, f32[2,2,36,8,128]{4,3,2,1,0:T(8,128)S(1)} %collective-permute-done.5.r1, ...), custom_call_target="tpu_custom_call" | custom-call | flops 17250000 | bytes 4096 | tf_op jit(solution)/shard_map/stitch_pairs/pallas_call | solution.py:338
  96.9 0.7 collective-permute-start.14
  97.6 0.8 collective-permute-start.15
  98.4 5.2 %ramp_filter.4 = (f32[2,2,2,2,8,8192]{5,4,3,2,1,0:T(8,128)}, f32[8,128]{1,0:T(8,128)}) custom-call(s32[29]{0:T(128)S(1)} %stack.17.info, f32[2,2,61,8,128]{4,3,2,1,0:T(8,128)S(1)} %get-tuple-element.61.refs_0_, f32[2,1,61,8,128]{4,3,2,1,0:T(8,128)S(1)} %collective-permute-done.13.refs_1_, ...), custom_call_target="tpu_custom_call", output_to_operand_aliasing={{0}: (9, {})} | custom-call | flops 23000000 | bytes 4096 | tf_op jit(solution)/shard_map/ramp_filter/pallas_call | solution.py:395
  103.7 6.9 %collective-permute-done.15.refs_1_ = f32[2,1,61,8,128]{4,3,2,1,0:T(8,128)S(1)} collective-permute-done((f32[2,1,61,8,128]{4,3,2,1,0:T(8,128)S(1)}, f32[2,1,61,8,128]{4,3,2,1,0:T(8,128)S(1)}, u32[]{:S(2)}, u32[]{:S(2)}) %collective-permute-start.15) | collective-permute-done | bytes 499744 | tf_op jit(solution)/shard_map/ppermute | solution.py:422
  110.6 5.2 %ramp_filter.5 = (f32[2,2,2,2,8,8192]{5,4,3,2,1,0:T(8,128)}, f32[8,128]{1,0:T(8,128)}) custom-call(s32[29]{0:T(128)S(1)} %stack.17.info, f32[2,2,61,8,128]{4,3,2,1,0:T(8,128)S(1)} %collective-permute-done.14.refs_0_, f32[2,1,61,8,128]{4,3,2,1,0:T(8,128)S(1)} %collective-permute-done.15.refs_1_, ...), custom_call_target="tpu_custom_call", output_to_operand_aliasing={{0}: (9, {})} | custom-call | flops 23000000 | bytes 4096 | tf_op jit(solution)/shard_map/ramp_filter/pallas_call | solution.py:395
  (15 shorter events, 0.1 us)
Async XLA Ops:
  0.0 19.6 %copy-start.7 = (f32[5,5]{1,0:T(8,128)S(1)}, f32[5,5]{1,0:T(8,128)}, u32[]{:S(2)}) copy-start(f32[5,5]{1,0:T(8,128)} %taps_ref.5) | copy-start | bytes 304
  2.0 17.6 %collective-permute-start = (f32[2,16,4608]{2,1,0:T(8,128)S(1)}, f32[2,16,4608]{2,1,0:T(8,128)S(1)}, u32[]{:S(2)}, u32[]{:S(2)}) collective-permute-start(f32[2,16,4608]{2,1,0:T(8,128)S(1)} %bitcast.13), channel_id=1, source_target_pairs={{32,33},{48,49},{96,97},{112,113},{160,161},{176,177},{224,225},{2... | collective-permute-start | bytes 1769480 | tf_op jit(solution)/shard_map/ppermute | solution.py:433
  7.6 2.3 %copy-start = (f32[16,16,4608]{2,1,0:T(8,128)S(1)}, f32[16,16,4608]{2,1,0:T(8,128)}, u32[]{:S(2)}) copy-start(f32[16,16,4608]{2,1,0:T(8,128)} %param.10) | copy-start | bytes 14155780
  23.5 13.2 %collective-permute-start.2 = (f32[1,2,36,8,128]{4,3,2,1,0:T(8,128)S(1)}, f32[1,2,36,8,128]{4,3,2,1,0:T(8,128)S(1)}, u32[]{:S(2)}, u32[]{:S(2)}) collective-permute-start(f32[1,2,36,8,128]{4,3,2,1,0:T(8,128)S(1)} %get-tuple-element.40), channel_id=1, source_target_pairs={{0,64},{16,80},{32,96},{48,112},{64,128},{80,144},{96,160},{112,17... | collective-permute-start | bytes 884744 | tf_op jit(solution)/shard_map/ppermute | solution.py:418
  23.6 13.1 %collective-permute-start.3 = (f32[1,2,36,8,128]{4,3,2,1,0:T(8,128)S(1)}, f32[1,2,36,8,128]{4,3,2,1,0:T(8,128)S(1)}, u32[]{:S(2)}, u32[]{:S(2)}) collective-permute-start(f32[1,2,36,8,128]{4,3,2,1,0:T(8,128)S(1)} %get-tuple-element.41), channel_id=1, source_target_pairs={{0,128},{16,144},{32,160},{48,176},{64,192},{80,208},{96,224},{112... | collective-permute-start | bytes 884744 | tf_op jit(solution)/shard_map/ppermute | solution.py:418
  25.8 14.5 %collective-permute-start.4 = (f32[1,2,36,8,128]{4,3,2,1,0:T(8,128)S(1)}, f32[1,2,36,8,128]{4,3,2,1,0:T(8,128)S(1)}, u32[]{:S(2)}, u32[]{:S(2)}) collective-permute-start(f32[1,2,36,8,128]{4,3,2,1,0:T(8,128)S(1)} %get-tuple-element.42), channel_id=1, source_target_pairs={{0,192},{16,208},{32,224},{48,240},{64,0},{80,16},{96,32},{112,48}... | collective-permute-start | bytes 884744 | tf_op jit(solution)/shard_map/ppermute | solution.py:418
  29.7 43.4 %copy-start.1 = (f32[2,64,8,128]{3,2,1,0:T(8,128)S(1)}, f32[2,64,8,128]{3,2,1,0:T(8,128)}, u32[]{:S(2)}) copy-start(f32[2,64,8,128]{3,2,1,0:T(8,128)} %constant.33.clone.refs_2_) | copy-start | bytes 1572868
  29.7 43.4 %copy-start.2 = (f32[512,128]{1,0:T(8,128)S(1)}, f32[512,128]{1,0:T(8,128)}, u32[]{:S(2)}) copy-start(f32[512,128]{1,0:T(8,128)} %constant.34.clone.refs_3_) | copy-start | bytes 786436
  29.7 43.4 %copy-start.3 = (bf16[256,256]{1,0:T(8,128)(2,1)S(1)}, bf16[256,256]{1,0:T(8,128)(2,1)}, u32[]{:S(2)}) copy-start(bf16[256,256]{1,0:T(8,128)(2,1)} %constant.35.clone.refs_4_) | copy-start | bytes 393220
  29.7 43.4 %copy-start.4 = (bf16[256,256]{1,0:T(8,128)(2,1)S(1)}, bf16[256,256]{1,0:T(8,128)(2,1)}, u32[]{:S(2)}) copy-start(bf16[256,256]{1,0:T(8,128)(2,1)} %constant.36.clone.refs_5_) | copy-start | bytes 393220
  29.7 43.4 %copy-start.5 = (bf16[256,256]{1,0:T(8,128)(2,1)S(1)}, bf16[256,256]{1,0:T(8,128)(2,1)}, u32[]{:S(2)}) copy-start(bf16[256,256]{1,0:T(8,128)(2,1)} %constant.37.clone.refs_6_) | copy-start | bytes 393220
  29.7 43.4 %copy-start.6 = (bf16[256,256]{1,0:T(8,128)(2,1)S(1)}, bf16[256,256]{1,0:T(8,128)(2,1)}, u32[]{:S(2)}) copy-start(bf16[256,256]{1,0:T(8,128)(2,1)} %constant.38.clone.refs_7_) | copy-start | bytes 393220
  29.8 17.4 %collective-permute-start.1 = (f32[2,2,36,8,128]{4,3,2,1,0:T(8,128)S(1)}, f32[2,2,36,8,128]{4,3,2,1,0:T(8,128)S(1)}, u32[]{:S(2)}, u32[]{:S(2)}) collective-permute-start(f32[2,2,36,8,128]{4,3,2,1,0:T(8,128)S(1)} %pad_maximum_fusion), channel_id=1, source_target_pairs={{0,1},{16,17},{64,65},{80,81},{128,129},{144,145},{192,193},{208,2... | collective-permute-start | bytes 1769480 | tf_op jit(solution)/shard_map/ppermute | solution.py:433
  41.3 24.7 %collective-permute-start.8 = (f32[2,1,61,8,128]{4,3,2,1,0:T(8,128)S(1)}, f32[2,1,61,8,128]{4,3,2,1,0:T(8,128)S(1)}, u32[]{:S(2)}, u32[]{:S(2)}) collective-permute-start(f32[2,1,61,8,128]{4,3,2,1,0:T(8,128)S(1)} %get-tuple-element.49), channel_id=1, source_target_pairs={{0,32},{16,48},{32,0},{48,16},{64,96},{80,112},{96,64},{112,80},{1... | collective-permute-start | bytes 1499144 | tf_op jit(solution)/shard_map/ppermute | solution.py:422
  43.5 17.6 %collective-permute-start.10 = (f32[1,2,36,8,128]{4,3,2,1,0:T(8,128)S(1)}, f32[1,2,36,8,128]{4,3,2,1,0:T(8,128)S(1)}, u32[]{:S(2)}, u32[]{:S(2)}) collective-permute-start(f32[1,2,36,8,128]{4,3,2,1,0:T(8,128)S(1)} %get-tuple-element.52), channel_id=1, source_target_pairs={{0,64},{16,80},{32,96},{48,112},{64,128},{80,144},{96,160},{112,17... | collective-permute-start | bytes 884744 | tf_op jit(solution)/shard_map/ppermute | solution.py:418
  43.5 17.6 %collective-permute-start.11 = (f32[1,2,36,8,128]{4,3,2,1,0:T(8,128)S(1)}, f32[1,2,36,8,128]{4,3,2,1,0:T(8,128)S(1)}, u32[]{:S(2)}, u32[]{:S(2)}) collective-permute-start(f32[1,2,36,8,128]{4,3,2,1,0:T(8,128)S(1)} %get-tuple-element.53), channel_id=1, source_target_pairs={{0,128},{16,144},{32,160},{48,176},{64,192},{80,208},{96,224},{112... | collective-permute-start | bytes 884744 | tf_op jit(solution)/shard_map/ppermute | solution.py:418
  44.2 16.9 %collective-permute-start.12 = (f32[1,2,36,8,128]{4,3,2,1,0:T(8,128)S(1)}, f32[1,2,36,8,128]{4,3,2,1,0:T(8,128)S(1)}, u32[]{:S(2)}, u32[]{:S(2)}) collective-permute-start(f32[1,2,36,8,128]{4,3,2,1,0:T(8,128)S(1)} %get-tuple-element.54), channel_id=1, source_target_pairs={{0,192},{16,208},{32,224},{48,240},{64,0},{80,16},{96,32},{112,48}... | collective-permute-start | bytes 884744 | tf_op jit(solution)/shard_map/ppermute | solution.py:418
  47.2 25.9 %collective-permute-start.9 = (f32[2,1,61,8,128]{4,3,2,1,0:T(8,128)S(1)}, f32[2,1,61,8,128]{4,3,2,1,0:T(8,128)S(1)}, u32[]{:S(2)}, u32[]{:S(2)}) collective-permute-start(f32[2,1,61,8,128]{4,3,2,1,0:T(8,128)S(1)} %get-tuple-element.50), channel_id=1, source_target_pairs={{0,48},{16,32},{32,16},{48,0},{64,112},{80,96},{96,80},{112,64},{1... | collective-permute-start | bytes 1499144 | tf_op jit(solution)/shard_map/ppermute | solution.py:422
  62.0 21.6 %collective-permute-start.13 = (f32[2,1,61,8,128]{4,3,2,1,0:T(8,128)S(1)}, f32[2,1,61,8,128]{4,3,2,1,0:T(8,128)S(1)}, u32[]{:S(2)}, u32[]{:S(2)}) collective-permute-start(f32[2,1,61,8,128]{4,3,2,1,0:T(8,128)S(1)} %get-tuple-element.58), channel_id=1, source_target_pairs={{0,32},{16,48},{32,0},{48,16},{64,96},{80,112},{96,64},{112,80},{1... | collective-permute-start | bytes 1499144 | tf_op jit(solution)/shard_map/ppermute | solution.py:422
  62.8 28.5 %collective-permute-start.5 = (f32[2,2,36,8,128]{4,3,2,1,0:T(8,128)S(1)}, f32[2,2,36,8,128]{4,3,2,1,0:T(8,128)S(1)}, u32[]{:S(2)}, u32[]{:S(2)}) collective-permute-start(f32[2,2,36,8,128]{4,3,2,1,0:T(8,128)S(1)} %get-tuple-element.46), channel_id=1, source_target_pairs={{0,64},{16,80},{32,96},{48,112},{64,128},{80,144},{96,160},{112,17... | collective-permute-start | bytes 1769480 | tf_op jit(solution)/shard_map/ppermute | solution.py:418
  65.8 25.5 %collective-permute-start.6 = (f32[2,2,36,8,128]{4,3,2,1,0:T(8,128)S(1)}, f32[2,2,36,8,128]{4,3,2,1,0:T(8,128)S(1)}, u32[]{:S(2)}, u32[]{:S(2)}) collective-permute-start(f32[2,2,36,8,128]{4,3,2,1,0:T(8,128)S(1)} %get-tuple-element.47), channel_id=1, source_target_pairs={{0,128},{16,144},{32,160},{48,176},{64,192},{80,208},{96,224},{112... | collective-permute-start | bytes 1769480 | tf_op jit(solution)/shard_map/ppermute | solution.py:418
  65.9 28.9 %collective-permute-start.7 = (f32[2,2,36,8,128]{4,3,2,1,0:T(8,128)S(1)}, f32[2,2,36,8,128]{4,3,2,1,0:T(8,128)S(1)}, u32[]{:S(2)}, u32[]{:S(2)}) collective-permute-start(f32[2,2,36,8,128]{4,3,2,1,0:T(8,128)S(1)} %get-tuple-element.48), channel_id=1, source_target_pairs={{0,192},{16,208},{32,224},{48,240},{64,0},{80,16},{96,32},{112,48}... | collective-permute-start | bytes 1769480 | tf_op jit(solution)/shard_map/ppermute | solution.py:418
  96.9 13.7 %collective-permute-start.14 = (f32[2,2,61,8,128]{4,3,2,1,0:T(8,128)S(1)}, f32[2,2,61,8,128]{4,3,2,1,0:T(8,128)S(1)}, u32[]{:S(2)}, u32[]{:S(2)}) collective-permute-start(f32[2,2,61,8,128]{4,3,2,1,0:T(8,128)S(1)} %get-tuple-element.59), channel_id=1, source_target_pairs={{0,16},{16,0},{32,48},{48,32},{64,80},{80,64},{96,112},{112,96},{1... | collective-permute-start | bytes 2998280 | tf_op jit(solution)/shard_map/ppermute | solution.py:422
  97.6 13.0 %collective-permute-start.15 = (f32[2,1,61,8,128]{4,3,2,1,0:T(8,128)S(1)}, f32[2,1,61,8,128]{4,3,2,1,0:T(8,128)S(1)}, u32[]{:S(2)}, u32[]{:S(2)}) collective-permute-start(f32[2,1,61,8,128]{4,3,2,1,0:T(8,128)S(1)} %get-tuple-element.60), channel_id=1, source_target_pairs={{0,48},{16,32},{32,16},{48,0},{64,112},{80,96},{96,80},{112,64},{1... | collective-permute-start | bytes 1499144 | tf_op jit(solution)/shard_map/ppermute | solution.py:422

commit v3 on v2

--- a/solution.py
+++ b/solution.py
@@ -198,10 +198,10 @@
 ANYWHERE = pl.BlockSpec(memory_space=pl.ANY)
 TOKEN = jax.ShapeDtypeStruct((SUB, LANES), f32)
 TOKEN_SPEC = whole((SUB, LANES))
-ROWS = (16, WT, SUB, LANES)
-
-
-def gather_kernel(x_hbm, out_ref, token, flat, sems):
+ROWS = (20, WT, SUB, LANES)
+
+
+def gather_kernel(info, x_hbm, out_ref, edge_ref, flat, sems):
     octet = pl.program_id(0)
     first = pl.multiple_of(octet * 16 * SUB, 16 * SUB)
     copies = [
@@ -216,30 +216,31 @@
         copy.wait()
     for r in range(16):
         for t in range(WT):
-            out_ref[0, r, t] = flat[t, pl.ds(r, SUB, stride=16), :]
-    token[...] = jnp.zeros_like(token)
-
-
-def gather_rows(x):
+            out_ref[0, r + 2, t] = flat[t, pl.ds(r, SUB, stride=16), :]
+    top = 14 * (1 - info[3])
+    for r in range(2):
+        for t in range(WT):
+            edge_ref[0, r, t] = flat[t, pl.ds(top + r, SUB, stride=16), :]
+
+
+def gather_rows(x, info):
     return pl.pallas_call(
         gather_kernel,
-        out_shape=[jax.ShapeDtypeStruct((2,) + ROWS, f32), TOKEN],
+        out_shape=[jax.ShapeDtypeStruct((2, n) + ROWS[1:], f32) for n in (20, 2)],
         grid=(2,),
-        in_specs=[ANYWHERE],
-        out_specs=[pl.BlockSpec((1,) + ROWS, lambda o: (o, 0, 0, 0, 0)), TOKEN_SPEC],
+        in_specs=[SMEM, ANYWHERE],
+        out_specs=[pl.BlockSpec((1, n) + ROWS[1:], lambda o: (o, 0, 0, 0, 0)) for n in (20, 2)],
         scratch_shapes=[pltpu.VMEM((WT, 16 * SUB, LANES), f32), pltpu.SemaphoreType.DMA((WT,))],
         compiler_params=limit(16),
         cost_estimate=cost(3.0),
         name="gather_rows",
-    )(x)
-
-
-def filter_kernel(octet, other, info, taps_ref, xt_hbm, halo_ref, *rest):
-    outs, token, edge = rest[-11:-7], rest[-7], rest[-6]
-    in_sem, xs, ys, weight, out_sems = rest[-5:]
+    )(info, x)
+
+
+def filter_kernel(octet, other, info, taps_ref, _, halo_ref, *rest):
+    rows, outs, token, weight = rest[-7], rest[-6:-2], rest[-2], rest[-1]
     step = pl.program_id(0)
-    load = pltpu.make_async_copy(xt_hbm.at[octet + step], xs.at[2:18], in_sem)
-    load.start()
+    xs = rows.at[octet + step]
     for r in range(2):
         for t in range(WT):
             if other:
@@ -255,67 +256,48 @@
         weight[t] = jnp.minimum((lane + t * LANES) / overlap, 1.0)
     token[...] = jnp.zeros_like(token)
     x_of = 1 - info[3] if other else info[3]
-    load.wait()
-    if other:
-        top = 2 + 14 * (1 - info[3])
-        for r in range(2):
-            for t in range(WT):
-                edge[0, r, t] = xs[top + r, t]
-    else:
-        edge[...] = jnp.zeros_like(edge)
-
-    @pl.loop(0, 8)
-    def _(i):
-        def store(t, value):
-            ys[i, t] = value
-
-        r = lax.rem(info[2] + i // 2, 4) * 4 + x_of * 2 + lax.rem(i, 2)
-        filter_row(taps, weight, xs, r, store)
-        for s in range(4):
-
-            @pl.when(i == 2 * s + 1)
-            def _():
-                pltpu.make_async_copy(ys.at[2 * s : 2 * s + 2], outs[s].at[step], out_sems.at[s]).start()
-
     for s in range(4):
-        pltpu.make_async_copy(ys.at[2 * s : 2 * s + 2], outs[s].at[step], out_sems.at[s]).wait()
+
+        @pl.loop(0, 2)
+        def _(c):
+            def store(t, value):
+                outs[s][step, c, t] = value
+
+            r = lax.rem(info[2] + s, 4) * 4 + x_of * 2 + c
+            filter_row(taps, weight, xs, r, store)
 
 
 def phase_filter(xt, halo, taps, info, octet, count, other, deps=()):
+    tile = (WT, SUB, LANES)
     if other:
         halo_spec = pl.BlockSpec((2, SUB, W), lambda o: (0, octet + o, 0))
-        edge = (1, 2, WT, SUB, LANES)
     else:
-        halo_spec = pl.BlockSpec((1, 2, WT, SUB, LANES), lambda o: (octet + o, 0, 0, 0, 0))
-        edge = (SUB, LANES)
+        halo_spec = pl.BlockSpec((1, 2) + tile, lambda o: (octet + o, 0, 0, 0, 0))
+    local = pl.BlockSpec(memory_space=pltpu.VMEM)
     return pl.pallas_call(
         functools.partial(filter_kernel, octet, other),
-        out_shape=[jax.ShapeDtypeStruct((count, 2, WT, SUB, LANES), f32)] * 4
-        + [TOKEN, jax.ShapeDtypeStruct(edge, f32)],
+        out_shape=[jax.ShapeDtypeStruct(xt.shape, f32)]
+        + [jax.ShapeDtypeStruct((count, 2) + tile, f32)] * 4
+        + [TOKEN],
         grid=(count,),
-        in_specs=[SMEM, SMEM, ANYWHERE, halo_spec] + [ANYWHERE] * len(deps),
-        out_specs=[ANYWHERE] * 4 + [TOKEN_SPEC, whole(edge)],
-        scratch_shapes=[
-            pltpu.SemaphoreType.DMA,
-            pltpu.VMEM((20, WT, SUB, LANES), f32),
-            pltpu.VMEM((8, WT, SUB, LANES), f32),
-            pltpu.VMEM((WT, SUB, LANES), f32),
-            pltpu.SemaphoreType.DMA((4,)),
-        ],
-        compiler_params=limit(12),
+        in_specs=[SMEM, SMEM, local, halo_spec] + [ANYWHERE] * len(deps),
+        out_specs=[local] * 5 + [TOKEN_SPEC],
+        scratch_shapes=[pltpu.VMEM(tile, f32)],
+        input_output_aliases={2: 0},
+        compiler_params=limit(8),
         cost_estimate=cost(5.0),
         name="phase_filter",
     )(info, taps, xt, halo, *deps)
 
 
-def stitch_kernel(info, r0, r1, r2, r3, *rest):
-    mine, crossing, token = rest[-3:]
+def stitch_kernel(by_core, info, r0, r1, r2, r3, *rest):
+    outs, token = (rest[-3:-1] if by_core else rest[-2:-1]), rest[-1]
     token[...] = jnp.zeros_like(token)
     shift, y, core = W - info[0], info[2], info[4]
     for near, far, place_of in ((r0, r2, y), (r1, r3, lax.rem(y + 3, 4))):
         near_is_own = place_of < 2
         half = lax.rem(place_of, 2)
-        for out, row in ((mine, core), (crossing, 1 - core)):
+        for out, row in zip(outs, (core, 1 - core)):
 
             def put(t, v):
                 out[half, 0, t] = v
@@ -323,9 +305,10 @@
             def add(t, v):
                 out[half, 0, t] = out[half, 0, t] + v
 
+            at = (0, row) if by_core else (0,)
             stitch(
-                lambda t: jnp.where(near_is_own, near[0, row, t], far[0, row, t]),
-                lambda t: jnp.where(near_is_own, far[0, row, t], near[0, row, t]),
+                lambda t: jnp.where(near_is_own, near[*at, t], far[*at, t]),
+                lambda t: jnp.where(near_is_own, far[*at, t], near[*at, t]),
                 put,
                 add,
                 shift,
@@ -333,15 +316,16 @@
 
 
 def stitch_pairs(parts, info, deps=()):
-    count = parts[0].shape[0]
-    out = jax.ShapeDtypeStruct((2, count, CT, SUB, LANES), f32)
+    count, by_core = parts[0].shape[0], parts[0].ndim == 5
+    block = (1,) + parts[0].shape[1:]
+    outs = [jax.ShapeDtypeStruct((2, count, CT, SUB, LANES), f32)] * (2 if by_core else 1)
     return pl.pallas_call(
-        stitch_kernel,
-        out_shape=[out, out, TOKEN],
+        functools.partial(stitch_kernel, by_core),
+        out_shape=outs + [TOKEN],
         in_specs=[SMEM]
-        + [pl.BlockSpec((1, 2, WT, SUB, LANES), lambda o: (o, 0, 0, 0, 0))] * 4
+        + [pl.BlockSpec(block, lambda o: (o,) + (0,) * (len(block) - 1))] * 4
         + [ANYWHERE] * len(deps),
-        out_specs=[pl.BlockSpec((2, 1, CT, SUB, LANES), lambda o: (0, o, 0, 0, 0))] * 2 + [TOKEN_SPEC],
+        out_specs=[pl.BlockSpec((2, 1, CT, SUB, LANES), lambda o: (0, o, 0, 0, 0))] * len(outs) + [TOKEN_SPEC],
         grid=(count,),
         compiler_params=limit(8),
         cost_estimate=cost(1.5),
@@ -440,12 +424,12 @@
     for x_of, core_of, octet in (
         (1 - x, core, 0),
         (1 - x, 1 - core, 0),
+        (1 - x, core, 1),
+        (1 - x, 1 - core, 1),
         (x, core, 0),
         (x, core, 1),
-        (1 - x, core, 1),
         (x, 1 - core, 0),
         (x, 1 - core, 1),
-        (1 - x, 1 - core, 1),
     ):
         slots += [x_of, core_of, jnp.int32(octet)]
     info = jnp.stack([correlation[0], offset[0], y, x, core] + slots)
@@ -457,25 +441,26 @@
     def send(rows):
         return flip(rows[0], 2), flip(rows[1], 3)
 
-    near = lax.dynamic_slice_in_dim(projections, 14 * x, 2, axis=1)
-    near = row_step(jnp.swapaxes(near, 0, 1), 1)
-    xt, gathered = gather_rows(projections.reshape(256, W))
-    *sent_0, done, edge_0 = phase_filter(xt, near, phase_kernel, info, 0, 1, True)
+    edge = lax.dynamic_slice(projections, (0, 14 * x, 0), (16, 2, W))
+    near = [row_step(jnp.swapaxes(edge, 0, 1), 1)] * 2
+    xt, edges = gather_rows(projections.reshape(256, W), info)
+    far = row_step(edges, 0)
+    xt, *sent_0, done = phase_filter(xt, near[0], phase_kernel, info, 0, 1, True)
     parts_0 = y_exchange(sent_0)
-    *sent_1, done, edge_1 = phase_filter(xt, near, phase_kernel, info, 1, 1, True, [done])
+    xt, *sent_1, done = phase_filter(xt, near[1], phase_kernel, info, 1, 1, True, [done])
     parts_1 = y_exchange(sent_1)
-    far = row_step(jnp.concatenate([edge_0, edge_1], axis=0), 0)
     *rows_0, done = stitch_pairs(parts_0, info, [done])
     arrived_0 = send(rows_0)
-    *sent_2, done, _ = phase_filter(xt, far, phase_kernel, info, 0, 2, False, [done])
+    xt, *sent_2, done = phase_filter(xt, far, phase_kernel, info, 0, 2, False, [done])
     parts_2 = y_exchange(sent_2)
     *rows_1, done = stitch_pairs(parts_1, info, [done])
     arrived_1 = send(rows_1)
     result, done = ramp_filter(arrived_0, info, consts, 0, None, [done])
-    *rows_2, done = stitch_pairs(parts_2, info, [done, arrived_1[0][0, 0, 0]])
+    result, done = ramp_filter(arrived_1, info, consts, 2, result)
+    *rows_2, done = stitch_pairs(parts_2, info, [done])
     swapped = flip(rows_2[1], 1)
-    result, done = ramp_filter([rows_2[0], arrived_1[0]], info, consts, 2, result)
-    result, done = ramp_filter([swapped, arrived_1[1]], info, consts, 5, result)
+    result, done = ramp_filter([rows_2[0]], info, consts, 4, result)
+    result, done = ramp_filter([swapped], info, consts, 6, result)
     return result.reshape(1, 128, S)
 
 

time: 117 us -> 110 us (0.940)
  the two profiles are of different devices: /device:TPU:121 before, /device:TPU:197 now
where the time goes in v3:
time: 110 us
  Pallas kernels  35.3 us (32%)
  starting transfers between devices  34.7 us (32%)
  waiting for transfers between devices  34.2 us (31%)
  local copies, waits for them, and re-layouts  4.48 us (4%)
  between operations  1.51 us (1%)
    ppermute x5, waiting for transfers between devices, flip(): return lax.ppermute(block, 'ang', [(i, i ^ bits) for i in range(16)])  17.4 us
    pallas_call x4, Pallas kernels, ramp_filter(): pl.pallas_call(functools.partial(ramp_kernel, len(rows)), out_shape=[jax....  15.7 us
    ppermute x9, starting transfers between devices, y_step(): return lax.ppermute(block, 'ang', route)  13.9 us
    ppermute x9, waiting for transfers between devices, y_step(): return lax.ppermute(block, 'ang', route)  13.8 us
    ppermute x5, starting transfers between devices, flip(): return lax.ppermute(block, 'ang', [(i, i ^ bits) for i in range(16)])  13.1 us
    pallas_call x3, Pallas kernels, phase_filter(): pl.pallas_call(functools.partial(filter_kernel, octet, other), out_shape=...  11.7 us
    ppermute x2, starting transfers between devices, row_step(): return lax.ppermute(block, ('ang', 'row'), route)  7.69 us
    pallas_call x1, Pallas kernels, gather_rows(): pl.pallas_call(gather_kernel, out_shape=[jax.ShapeDtypeStruct((2, n) + RO...  3.99 us
  transfers between devices with their start and end apart: 16, of which 7 were waited for; matrix products, arithmetic and copies ran while one was open for 0% of the time, Pallas kernels for 27%

profile of v3, /device:TPU:197, one launch (start us, length us, event | category | flops | bytes accessed | tf_op | source)
XLA Modules:
  0.0 110.3 jit_solution(11257993762843101581)
XLA Ops:
  0.0 1.9 %constant_dynamic-slice_fusion = f32[16,2,4608]{2,1,0:T(2,128)S(1)} fusion(f32[16,16,4608]{2,1,0:T(8,128)} %param.10, s32[]{:T(128)S(6)} %select_n.3), kind=kLoop, calls=%fused_computation.1 | loop fusion | bytes 1179652 | tf_op jit(solution)/shard_map/dynamic_slice | solution.py:444
  1.9 0.1 copy.20
  2.0 2.1 %collective-permute-start = (f32[2,16,4608]{2,1,0:T(8,128)S(1)}, f32[2,16,4608]{2,1,0:T(8,128)S(1)}, u32[]{:S(2)}, u32[]{:S(2)}) collective-permute-start(f32[2,16,4608]{2,1,0:T(8,128)S(1)} %bitcast.11), channel_id=1, source_target_pairs={{32,33},{48,49},{96,97},{112,113},{160,161},{176,177},{224,225},{2... | collective-permute-start | bytes 1769480 | tf_op jit(solution)/shard_map/ppermute | solution.py:417
  5.5 0.1 stack.17.info
  5.6 0.0 copy-start.1
  5.6 2.3 %copy-done.1 = f32[16,16,4608]{2,1,0:T(8,128)S(1)} copy-done((f32[16,16,4608]{2,1,0:T(8,128)S(1)}, f32[16,16,4608]{2,1,0:T(8,128)}, u32[]{:S(2)}) %copy-start.1) | copy-done | bytes 4718616
  7.9 4.0 %gather_rows.1 = (f32[2,20,36,8,128]{4,3,2,1,0:T(8,128)S(1)}, f32[2,2,36,8,128]{4,3,2,1,0:T(8,128)S(1)}) custom-call(s32[29]{0:T(128)S(1)} %stack.17.info, f32[256,4608]{1,0:T(8,128)S(1)} %bitcast.10), custom_call_target="tpu_custom_call" | custom-call | flops 34500000 | bytes 4096 | tf_op jit(solution)/shard_map/gather_rows/pallas_call | solution.py:227
  11.9 5.6 %collective-permute-start.1 = (f32[2,2,36,8,128]{4,3,2,1,0:T(8,128)S(1)}, f32[2,2,36,8,128]{4,3,2,1,0:T(8,128)S(1)}, u32[]{:S(2)}, u32[]{:S(2)}) collective-permute-start(f32[2,2,36,8,128]{4,3,2,1,0:T(8,128)S(1)} %get-tuple-element.41), channel_id=1, source_target_pairs={{0,1},{16,17},{64,65},{80,81},{128,129},{144,145},{192,193},{208,2... | collective-permute-start | bytes 1769480 | tf_op jit(solution)/shard_map/ppermute | solution.py:417
  17.5 3.1 %collective-permute-done.halo_ref = f32[2,16,4608]{2,1,0:T(8,128)S(1)} collective-permute-done((f32[2,16,4608]{2,1,0:T(8,128)S(1)}, f32[2,16,4608]{2,1,0:T(8,128)S(1)}, u32[]{:S(2)}, u32[]{:S(2)}) %collective-permute-start) | collective-permute-done | bytes 589856 | tf_op jit(solution)/shard_map/ppermute | solution.py:417
  20.6 3.1 %phase_filter.3 = (f32[2,20,36,8,128]{4,3,2,1,0:T(8,128)S(1)}, f32[1,2,36,8,128]{4,3,2,1,0:T(8,128)S(1)}, f32[1,2,36,8,128]{4,3,2,1,0:T(8,128)S(1)}, f32[1,2,36,...) custom-call(s32[29]{0:T(128)S(1)} %stack.17.info, ...), custom_call_target="tpu_custom_call", output_to_operand_aliasing={{0}: (2, {})} | custom-call | flops 57500000 | bytes 4096 | tf_op jit(solution)/shard_map/phase_filter/pallas_call | solution.py:277
  23.6 1.4 %collective-permute-start.2 = (f32[1,2,36,8,128]{4,3,2,1,0:T(8,128)S(1)}, f32[1,2,36,8,128]{4,3,2,1,0:T(8,128)S(1)}, u32[]{:S(2)}, u32[]{:S(2)}) collective-permute-start(f32[1,2,36,8,128]{4,3,2,1,0:T(8,128)S(1)} %get-tuple-element.43), channel_id=1, source_target_pairs={{0,64},{16,80},{32,96},{48,112},{64,128},{80,144},{96,160},{112,17... | collective-permute-start | bytes 884744 | tf_op jit(solution)/shard_map/ppermute | solution.py:402
  25.0 2.6 %collective-permute-start.3 = (f32[1,2,36,8,128]{4,3,2,1,0:T(8,128)S(1)}, f32[1,2,36,8,128]{4,3,2,1,0:T(8,128)S(1)}, u32[]{:S(2)}, u32[]{:S(2)}) collective-permute-start(f32[1,2,36,8,128]{4,3,2,1,0:T(8,128)S(1)} %get-tuple-element.44), channel_id=1, source_target_pairs={{0,128},{16,144},{32,160},{48,176},{64,192},{80,208},{96,224},{112... | collective-permute-start | bytes 884744 | tf_op jit(solution)/shard_map/ppermute | solution.py:402
  27.6 1.1 collective-permute-start.4
  28.7 3.1 %phase_filter.4 = (f32[2,20,36,8,128]{4,3,2,1,0:T(8,128)S(1)}, f32[1,2,36,8,128]{4,3,2,1,0:T(8,128)S(1)}, f32[1,2,36,8,128]{4,3,2,1,0:T(8,128)S(1)}, f32[1,2,36,...) custom-call(s32[29]{0:T(128)S(1)} %stack.17.info, ...), custom_call_target="tpu_custom_call", output_to_operand_aliasing={{0}: (2, {})} | custom-call | flops 57500000 | bytes 4096 | tf_op jit(solution)/shard_map/phase_filter/pallas_call | solution.py:277
  31.8 0.0 copy-start
  31.8 0.0 copy-start.2
  31.8 0.0 copy-start.3
  31.8 0.0 copy-start.4
  31.8 0.0 copy-start.5
  31.8 0.0 copy-start.6
  31.8 0.1 collective-permute-done.2.r1
  31.9 7.4 %collective-permute-done.3.r2 = f32[1,2,36,8,128]{4,3,2,1,0:T(8,128)S(1)} collective-permute-done((f32[1,2,36,8,128]{4,3,2,1,0:T(8,128)S(1)}, f32[1,2,36,8,128]{4,3,2,1,0:T(8,128)S(1)}, u32[]{:S(2)}, u32[]{:S(2)}) %collective-permute-start.3) | collective-permute-done | bytes 294944 | tf_op jit(solution)/shard_map/ppermute | solution.py:402
  39.4 0.4 collective-permute-done.4.r3
  39.7 0.9 stitch_pairs.3
  40.7 0.1 collective-permute-start.13
  40.8 10.4 %collective-permute-start.14 = (f32[2,1,61,8,128]{4,3,2,1,0:T(8,128)S(1)}, f32[2,1,61,8,128]{4,3,2,1,0:T(8,128)S(1)}, u32[]{:S(2)}, u32[]{:S(2)}) collective-permute-start(f32[2,1,61,8,128]{4,3,2,1,0:T(8,128)S(1)} %get-tuple-element.60), channel_id=1, source_target_pairs={{0,48},{16,32},{32,16},{48,0},{64,112},{80,96},{96,80},{112,64},{1... | collective-permute-start | bytes 1499144 | tf_op jit(solution)/shard_map/ppermute | solution.py:406
  51.2 1.4 %collective-permute-start.8 = (f32[1,2,36,8,128]{4,3,2,1,0:T(8,128)S(1)}, f32[1,2,36,8,128]{4,3,2,1,0:T(8,128)S(1)}, u32[]{:S(2)}, u32[]{:S(2)}) collective-permute-start(f32[1,2,36,8,128]{4,3,2,1,0:T(8,128)S(1)} %get-tuple-element.53), channel_id=1, source_target_pairs={{0,64},{16,80},{32,96},{48,112},{64,128},{80,144},{96,160},{112,17... | collective-permute-start | bytes 884744 | tf_op jit(solution)/shard_map/ppermute | solution.py:402
  52.6 1.8 %collective-permute-start.9 = (f32[1,2,36,8,128]{4,3,2,1,0:T(8,128)S(1)}, f32[1,2,36,8,128]{4,3,2,1,0:T(8,128)S(1)}, u32[]{:S(2)}, u32[]{:S(2)}) collective-permute-start(f32[1,2,36,8,128]{4,3,2,1,0:T(8,128)S(1)} %get-tuple-element.54), channel_id=1, source_target_pairs={{0,128},{16,144},{32,160},{48,176},{64,192},{80,208},{96,224},{112... | collective-permute-start | bytes 884744 | tf_op jit(solution)/shard_map/ppermute | solution.py:402
  54.4 0.0 collective-permute-done.1.halo_ref
  54.4 1.5 %collective-permute-start.10 = (f32[1,2,36,8,128]{4,3,2,1,0:T(8,128)S(1)}, f32[1,2,36,8,128]{4,3,2,1,0:T(8,128)S(1)}, u32[]{:S(2)}, u32[]{:S(2)}) collective-permute-start(f32[1,2,36,8,128]{4,3,2,1,0:T(8,128)S(1)} %get-tuple-element.55), channel_id=1, source_target_pairs={{0,192},{16,208},{32,224},{48,240},{64,0},{80,16},{96,32},{112,48}... | collective-permute-start | bytes 884744 | tf_op jit(solution)/shard_map/ppermute | solution.py:402
  55.9 5.6 %phase_filter.5 = (f32[2,20,36,8,128]{4,3,2,1,0:T(8,128)S(1)}, f32[2,2,36,8,128]{4,3,2,1,0:T(8,128)S(1)}, f32[2,2,36,8,128]{4,3,2,1,0:T(8,128)S(1)}, f32[2,2,36,...) custom-call(s32[29]{0:T(128)S(1)} %stack.17.info, ...), custom_call_target="tpu_custom_call", output_to_operand_aliasing={{0}: (2, {})} | custom-call | flops 57500000 | bytes 4096 | tf_op jit(solution)/shard_map/phase_filter/pallas_call | solution.py:277
  61.5 0.3 collective-permute-start.5
  61.7 5.9 %collective-permute-done.9.r2 = f32[1,2,36,8,128]{4,3,2,1,0:T(8,128)S(1)} collective-permute-done((f32[1,2,36,8,128]{4,3,2,1,0:T(8,128)S(1)}, f32[1,2,36,8,128]{4,3,2,1,0:T(8,128)S(1)}, u32[]{:S(2)}, u32[]{:S(2)}) %collective-permute-start.9) | collective-permute-done | bytes 294944 | tf_op jit(solution)/shard_map/ppermute | solution.py:402
  67.6 1.1 %collective-permute-start.6 = (f32[2,2,36,8,128]{4,3,2,1,0:T(8,128)S(1)}, f32[2,2,36,8,128]{4,3,2,1,0:T(8,128)S(1)}, u32[]{:S(2)}, u32[]{:S(2)}) collective-permute-start(f32[2,2,36,8,128]{4,3,2,1,0:T(8,128)S(1)} %get-tuple-element.50), channel_id=1, source_target_pairs={{0,128},{16,144},{32,160},{48,176},{64,192},{80,208},{96,224},{112... | collective-permute-start | bytes 1769480 | tf_op jit(solution)/shard_map/ppermute | solution.py:402
  68.7 2.8 %collective-permute-start.7 = (f32[2,2,36,8,128]{4,3,2,1,0:T(8,128)S(1)}, f32[2,2,36,8,128]{4,3,2,1,0:T(8,128)S(1)}, u32[]{:S(2)}, u32[]{:S(2)}) collective-permute-start(f32[2,2,36,8,128]{4,3,2,1,0:T(8,128)S(1)} %get-tuple-element.51), channel_id=1, source_target_pairs={{0,192},{16,208},{32,224},{48,240},{64,0},{80,16},{96,32},{112,48}... | collective-permute-start | bytes 1769480 | tf_op jit(solution)/shard_map/ppermute | solution.py:402
  71.5 0.9 stitch_pairs.4
  72.5 0.0 collective-permute-done.13.refs_0_
  72.5 0.8 collective-permute-start.11
  73.3 1.8 %collective-permute-start.12 = (f32[2,1,61,8,128]{4,3,2,1,0:T(8,128)S(1)}, f32[2,1,61,8,128]{4,3,2,1,0:T(8,128)S(1)}, u32[]{:S(2)}, u32[]{:S(2)}) collective-permute-start(f32[2,1,61,8,128]{4,3,2,1,0:T(8,128)S(1)} %get-tuple-element.58), channel_id=1, source_target_pairs={{0,48},{16,32},{32,16},{48,0},{64,112},{80,96},{96,80},{112,64},{1... | collective-permute-start | bytes 1499144 | tf_op jit(solution)/shard_map/ppermute | solution.py:406
  75.1 3.9 %ramp_filter.4 = (f32[2,2,2,2,8,8192]{5,4,3,2,1,0:T(8,128)}, f32[8,128]{1,0:T(8,128)}) custom-call(s32[29]{0:T(128)S(1)} %stack.17.info, f32[2,1,61,8,128]{4,3,2,1,0:T(8,128)S(1)} %collective-permute-done.13.refs_0_, f32[2,1,61,8,128]{4,3,2,1,0:T(8,128)S(1)} %collective-permute-done.14.refs_1_, f32[2,64,8,128]{3,2,1,0:T(8,128)S(1)} %copy-done, ...), custom_call_target="tpu_custom_call" | custom-call | flops 23000000 | bytes 4096 | tf_op jit(solution)/shard_map/ramp_filter/pallas_call | solution.py:379
  79.0 5.6 %collective-permute-done.11.refs_0_ = f32[2,1,61,8,128]{4,3,2,1,0:T(8,128)S(1)} collective-permute-done((f32[2,1,61,8,128]{4,3,2,1,0:T(8,128)S(1)}, f32[2,1,61,8,128]{4,3,2,1,0:T(8,128)S(1)}, u32[]{:S(2)}, u32[]{:S(2)}) %collective-permute-start.11) | collective-permute-done | bytes 499744 | tf_op jit(solution)/shard_map/ppermute | solution.py:406
  84.6 11.8 %collective-permute-done.12.refs_1_ = f32[2,1,61,8,128]{4,3,2,1,0:T(8,128)S(1)} collective-permute-done((f32[2,1,61,8,128]{4,3,2,1,0:T(8,128)S(1)}, f32[2,1,61,8,128]{4,3,2,1,0:T(8,128)S(1)}, u32[]{:S(2)}, u32[]{:S(2)}) %collective-permute-start.12) | collective-permute-done | bytes 499744 | tf_op jit(solution)/shard_map/ppermute | solution.py:406
  96.4 3.9 %ramp_filter.5 = (f32[2,2,2,2,8,8192]{5,4,3,2,1,0:T(8,128)}, f32[8,128]{1,0:T(8,128)S(1)}) custom-call(s32[29]{0:T(128)S(1)} %stack.17.info, f32[2,1,61,8,128]{4,3,2,1,0:T(8,128)S(1)} %collective-permute-done.11.refs_0_, f32[2,1,61,8,128]{4,3,2,1,0:T(8,128)S(1)} %collective-permute-done.12.refs_1_, ...), custom_call_target="tpu_custom_call", output_to_operand_aliasing={{0}: (9, {})} | custom-call | flops 23000000 | bytes 4096 | tf_op jit(solution)/shard_map/ramp_filter/pallas_call | solution.py:379
  100.3 0.0 collective-permute-done.5.r1
  100.3 0.0 collective-permute-done.6.r2
  100.3 2.1 %stitch_pairs.5 = (f32[2,2,61,8,128]{4,3,2,1,0:T(8,128)S(1)}, f32[2,2,61,8,128]{4,3,2,1,0:T(8,128)S(1)}, f32[8,128]{1,0:T(8,128)}) custom-call(s32[29]{0:T(128)S(1)} %stack.17.info, f32[2,2,36,8,128]{4,3,2,1,0:T(8,128)S(1)} %get-tuple-element.48.r0, f32[2,2,36,8,128]{4,3,2,1,0:T(8,128)S(1)} %collective-permute-done.5.r1, ...), custom_call_target="tpu_custom_call" | custom-call | flops 17250000 | bytes 4096 | tf_op jit(solution)/shard_map/stitch_pairs/pallas_call | solution.py:322
  102.4 3.9 %ramp_filter.6 = (f32[2,2,2,2,8,8192]{5,4,3,2,1,0:T(8,128)}, f32[8,128]{1,0:T(8,128)}) custom-call(s32[29]{0:T(128)S(1)} %stack.17.info, f32[2,2,61,8,128]{4,3,2,1,0:T(8,128)S(1)} %get-tuple-element.65.refs_0_, f32[2,64,8,128]{3,2,1,0:T(8,128)S(1)} %copy-done, f32[512,128]{1,0:T(8,128)S(1)} %copy-done.2, ...), custom_call_target="tpu_custom_call", output_to_operand_aliasing={{0}: (8, {})} | custom-call | flops 23000000 | bytes 4096 | tf_op jit(solution)/shard_map/ramp_filter/pallas_call | solution.py:379
  106.4 3.9 %ramp_filter.7 = (f32[2,2,2,2,8,8192]{5,4,3,2,1,0:T(8,128)}, f32[8,128]{1,0:T(8,128)}) custom-call(s32[29]{0:T(128)S(1)} %stack.17.info, f32[2,2,61,8,128]{4,3,2,1,0:T(8,128)S(1)} %collective-permute-done.15.refs_0_, f32[2,64,8,128]{3,2,1,0:T(8,128)S(1)} %copy-done, f32[512,128]{1,0:T(8,128)S(1)} %copy-done.2, ...), custom_call_target="tpu_custom_call", output_to_operand_aliasing={{0}: (8, {})} | custom-call | flops 23000000 | bytes 4096 | tf_op jit(solution)/shard_map/ramp_filter/pallas_call | solution.py:379
  (14 shorter events, 0.0 us)
Async XLA Ops:
  0.0 20.6 %copy-start.7 = (f32[5,5]{1,0:T(8,128)S(1)}, f32[5,5]{1,0:T(8,128)}, u32[]{:S(2)}) copy-start(f32[5,5]{1,0:T(8,128)} %taps_ref.5) | copy-start | bytes 304
  2.0 18.5 %collective-permute-start = (f32[2,16,4608]{2,1,0:T(8,128)S(1)}, f32[2,16,4608]{2,1,0:T(8,128)S(1)}, u32[]{:S(2)}, u32[]{:S(2)}) collective-permute-start(f32[2,16,4608]{2,1,0:T(8,128)S(1)} %bitcast.11), channel_id=1, source_target_pairs={{32,33},{48,49},{96,97},{112,113},{160,161},{176,177},{224,225},{2... | collective-permute-start | bytes 1769480 | tf_op jit(solution)/shard_map/ppermute | solution.py:417
  5.6 2.3 %copy-start.1 = (f32[16,16,4608]{2,1,0:T(8,128)S(1)}, f32[16,16,4608]{2,1,0:T(8,128)}, u32[]{:S(2)}) copy-start(f32[16,16,4608]{2,1,0:T(8,128)} %param.10) | copy-start | bytes 14155780
  11.9 42.5 %collective-permute-start.1 = (f32[2,2,36,8,128]{4,3,2,1,0:T(8,128)S(1)}, f32[2,2,36,8,128]{4,3,2,1,0:T(8,128)S(1)}, u32[]{:S(2)}, u32[]{:S(2)}) collective-permute-start(f32[2,2,36,8,128]{4,3,2,1,0:T(8,128)S(1)} %get-tuple-element.41), channel_id=1, source_target_pairs={{0,1},{16,17},{64,65},{80,81},{128,129},{144,145},{192,193},{208,2... | collective-permute-start | bytes 1769480 | tf_op jit(solution)/shard_map/ppermute | solution.py:417
  23.6 8.3 %collective-permute-start.2 = (f32[1,2,36,8,128]{4,3,2,1,0:T(8,128)S(1)}, f32[1,2,36,8,128]{4,3,2,1,0:T(8,128)S(1)}, u32[]{:S(2)}, u32[]{:S(2)}) collective-permute-start(f32[1,2,36,8,128]{4,3,2,1,0:T(8,128)S(1)} %get-tuple-element.43), channel_id=1, source_target_pairs={{0,64},{16,80},{32,96},{48,112},{64,128},{80,144},{96,160},{112,17... | collective-permute-start | bytes 884744 | tf_op jit(solution)/shard_map/ppermute | solution.py:402
  25.0 14.4 %collective-permute-start.3 = (f32[1,2,36,8,128]{4,3,2,1,0:T(8,128)S(1)}, f32[1,2,36,8,128]{4,3,2,1,0:T(8,128)S(1)}, u32[]{:S(2)}, u32[]{:S(2)}) collective-permute-start(f32[1,2,36,8,128]{4,3,2,1,0:T(8,128)S(1)} %get-tuple-element.44), channel_id=1, source_target_pairs={{0,128},{16,144},{32,160},{48,176},{64,192},{80,208},{96,224},{112... | collective-permute-start | bytes 884744 | tf_op jit(solution)/shard_map/ppermute | solution.py:402
  27.6 12.1 %collective-permute-start.4 = (f32[1,2,36,8,128]{4,3,2,1,0:T(8,128)S(1)}, f32[1,2,36,8,128]{4,3,2,1,0:T(8,128)S(1)}, u32[]{:S(2)}, u32[]{:S(2)}) collective-permute-start(f32[1,2,36,8,128]{4,3,2,1,0:T(8,128)S(1)} %get-tuple-element.45), channel_id=1, source_target_pairs={{0,192},{16,208},{32,224},{48,240},{64,0},{80,16},{96,32},{112,48}... | collective-permute-start | bytes 884744 | tf_op jit(solution)/shard_map/ppermute | solution.py:402
  31.8 43.3 %copy-start = (f32[2,64,8,128]{3,2,1,0:T(8,128)S(1)}, f32[2,64,8,128]{3,2,1,0:T(8,128)}, u32[]{:S(2)}) copy-start(f32[2,64,8,128]{3,2,1,0:T(8,128)} %constant.33.clone.refs_2_.refs_1_) | copy-start | bytes 1572868
  31.8 43.3 %copy-start.2 = (f32[512,128]{1,0:T(8,128)S(1)}, f32[512,128]{1,0:T(8,128)}, u32[]{:S(2)}) copy-start(f32[512,128]{1,0:T(8,128)} %constant.34.clone.refs_3_.refs_2_) | copy-start | bytes 786436
  31.8 43.3 %copy-start.3 = (bf16[256,256]{1,0:T(8,128)(2,1)S(1)}, bf16[256,256]{1,0:T(8,128)(2,1)}, u32[]{:S(2)}) copy-start(bf16[256,256]{1,0:T(8,128)(2,1)} %constant.38.clone.refs_7_.refs_6_) | copy-start | bytes 393220
  31.8 43.3 %copy-start.4 = (bf16[256,256]{1,0:T(8,128)(2,1)S(1)}, bf16[256,256]{1,0:T(8,128)(2,1)}, u32[]{:S(2)}) copy-start(bf16[256,256]{1,0:T(8,128)(2,1)} %constant.37.clone.refs_6_.refs_5_) | copy-start | bytes 393220
  31.8 43.3 %copy-start.5 = (bf16[256,256]{1,0:T(8,128)(2,1)S(1)}, bf16[256,256]{1,0:T(8,128)(2,1)}, u32[]{:S(2)}) copy-start(bf16[256,256]{1,0:T(8,128)(2,1)} %constant.36.clone.refs_5_.refs_4_) | copy-start | bytes 393220
  31.8 43.3 %copy-start.6 = (bf16[256,256]{1,0:T(8,128)(2,1)S(1)}, bf16[256,256]{1,0:T(8,128)(2,1)}, u32[]{:S(2)}) copy-start(bf16[256,256]{1,0:T(8,128)(2,1)} %constant.35.clone.refs_4_.refs_3_) | copy-start | bytes 393220
  40.7 31.8 %collective-permute-start.13 = (f32[2,1,61,8,128]{4,3,2,1,0:T(8,128)S(1)}, f32[2,1,61,8,128]{4,3,2,1,0:T(8,128)S(1)}, u32[]{:S(2)}, u32[]{:S(2)}) collective-permute-start(f32[2,1,61,8,128]{4,3,2,1,0:T(8,128)S(1)} %get-tuple-element.59), channel_id=1, source_target_pairs={{0,32},{16,48},{32,0},{48,16},{64,96},{80,112},{96,64},{112,80},{1... | collective-permute-start | bytes 1499144 | tf_op jit(solution)/shard_map/ppermute | solution.py:406
  40.8 32.5 %collective-permute-start.14 = (f32[2,1,61,8,128]{4,3,2,1,0:T(8,128)S(1)}, f32[2,1,61,8,128]{4,3,2,1,0:T(8,128)S(1)}, u32[]{:S(2)}, u32[]{:S(2)}) collective-permute-start(f32[2,1,61,8,128]{4,3,2,1,0:T(8,128)S(1)} %get-tuple-element.60), channel_id=1, source_target_pairs={{0,48},{16,32},{32,16},{48,0},{64,112},{80,96},{96,80},{112,64},{1... | collective-permute-start | bytes 1499144 | tf_op jit(solution)/shard_map/ppermute | solution.py:406
  51.2 10.3 %collective-permute-start.8 = (f32[1,2,36,8,128]{4,3,2,1,0:T(8,128)S(1)}, f32[1,2,36,8,128]{4,3,2,1,0:T(8,128)S(1)}, u32[]{:S(2)}, u32[]{:S(2)}) collective-permute-start(f32[1,2,36,8,128]{4,3,2,1,0:T(8,128)S(1)} %get-tuple-element.53), channel_id=1, source_target_pairs={{0,64},{16,80},{32,96},{48,112},{64,128},{80,144},{96,160},{112,17... | collective-permute-start | bytes 884744 | tf_op jit(solution)/shard_map/ppermute | solution.py:402
  52.6 15.0 %collective-permute-start.9 = (f32[1,2,36,8,128]{4,3,2,1,0:T(8,128)S(1)}, f32[1,2,36,8,128]{4,3,2,1,0:T(8,128)S(1)}, u32[]{:S(2)}, u32[]{:S(2)}) collective-permute-start(f32[1,2,36,8,128]{4,3,2,1,0:T(8,128)S(1)} %get-tuple-element.54), channel_id=1, source_target_pairs={{0,128},{16,144},{32,160},{48,176},{64,192},{80,208},{96,224},{112... | collective-permute-start | bytes 884744 | tf_op jit(solution)/shard_map/ppermute | solution.py:402
  54.4 14.3 %collective-permute-start.10 = (f32[1,2,36,8,128]{4,3,2,1,0:T(8,128)S(1)}, f32[1,2,36,8,128]{4,3,2,1,0:T(8,128)S(1)}, u32[]{:S(2)}, u32[]{:S(2)}) collective-permute-start(f32[1,2,36,8,128]{4,3,2,1,0:T(8,128)S(1)} %get-tuple-element.55), channel_id=1, source_target_pairs={{0,192},{16,208},{32,224},{48,240},{64,0},{80,16},{96,32},{112,48}... | collective-permute-start | bytes 884744 | tf_op jit(solution)/shard_map/ppermute | solution.py:402
  61.5 38.9 %collective-permute-start.5 = (f32[2,2,36,8,128]{4,3,2,1,0:T(8,128)S(1)}, f32[2,2,36,8,128]{4,3,2,1,0:T(8,128)S(1)}, u32[]{:S(2)}, u32[]{:S(2)}) collective-permute-start(f32[2,2,36,8,128]{4,3,2,1,0:T(8,128)S(1)} %get-tuple-element.49), channel_id=1, source_target_pairs={{0,64},{16,80},{32,96},{48,112},{64,128},{80,144},{96,160},{112,17... | collective-permute-start | bytes 1769480 | tf_op jit(solution)/shard_map/ppermute | solution.py:402
  67.6 32.7 %collective-permute-start.6 = (f32[2,2,36,8,128]{4,3,2,1,0:T(8,128)S(1)}, f32[2,2,36,8,128]{4,3,2,1,0:T(8,128)S(1)}, u32[]{:S(2)}, u32[]{:S(2)}) collective-permute-start(f32[2,2,36,8,128]{4,3,2,1,0:T(8,128)S(1)} %get-tuple-element.50), channel_id=1, source_target_pairs={{0,128},{16,144},{32,160},{48,176},{64,192},{80,208},{96,224},{112... | collective-permute-start | bytes 1769480 | tf_op jit(solution)/shard_map/ppermute | solution.py:402
  68.7 31.6 %collective-permute-start.7 = (f32[2,2,36,8,128]{4,3,2,1,0:T(8,128)S(1)}, f32[2,2,36,8,128]{4,3,2,1,0:T(8,128)S(1)}, u32[]{:S(2)}, u32[]{:S(2)}) collective-permute-start(f32[2,2,36,8,128]{4,3,2,1,0:T(8,128)S(1)} %get-tuple-element.51), channel_id=1, source_target_pairs={{0,192},{16,208},{32,224},{48,240},{64,0},{80,16},{96,32},{112,48}... | collective-permute-start | bytes 1769480 | tf_op jit(solution)/shard_map/ppermute | solution.py:402
  72.5 12.1 %collective-permute-start.11 = (f32[2,1,61,8,128]{4,3,2,1,0:T(8,128)S(1)}, f32[2,1,61,8,128]{4,3,2,1,0:T(8,128)S(1)}, u32[]{:S(2)}, u32[]{:S(2)}) collective-permute-start(f32[2,1,61,8,128]{4,3,2,1,0:T(8,128)S(1)} %get-tuple-element.57), channel_id=1, source_target_pairs={{0,32},{16,48},{32,0},{48,16},{64,96},{80,112},{96,64},{112,80},{1... | collective-permute-start | bytes 1499144 | tf_op jit(solution)/shard_map/ppermute | solution.py:406
  73.3 23.1 %collective-permute-start.12 = (f32[2,1,61,8,128]{4,3,2,1,0:T(8,128)S(1)}, f32[2,1,61,8,128]{4,3,2,1,0:T(8,128)S(1)}, u32[]{:S(2)}, u32[]{:S(2)}) collective-permute-start(f32[2,1,61,8,128]{4,3,2,1,0:T(8,128)S(1)} %get-tuple-element.58), channel_id=1, source_target_pairs={{0,48},{16,32},{32,16},{48,0},{64,112},{80,96},{96,80},{112,64},{1... | collective-permute-start | bytes 1499144 | tf_op jit(solution)/shard_map/ppermute | solution.py:406
  102.4 3.9 %collective-permute-start.15 = (f32[2,2,61,8,128]{4,3,2,1,0:T(8,128)S(1)}, f32[2,2,61,8,128]{4,3,2,1,0:T(8,128)S(1)}, u32[]{:S(2)}, u32[]{:S(2)}) collective-permute-start(f32[2,2,61,8,128]{4,3,2,1,0:T(8,128)S(1)} %get-tuple-element.64), channel_id=1, source_target_pairs={{0,16},{16,0},{32,48},{48,32},{64,80},{80,64},{96,112},{112,96},{1... | collective-permute-start | bytes 2998280 | tf_op jit(solution)/shard_map/ppermute | solution.py:406

commit v4 on v3

--- a/solution.py
+++ b/solution.py
@@ -201,7 +201,7 @@
 ROWS = (20, WT, SUB, LANES)
 
 
-def gather_kernel(info, x_hbm, out_ref, edge_ref, flat, sems):
+def gather_kernel(x_hbm, out_ref, flat, sems):
     octet = pl.program_id(0)
     first = pl.multiple_of(octet * 16 * SUB, 16 * SUB)
     copies = [
@@ -217,28 +217,24 @@
     for r in range(16):
         for t in range(WT):
             out_ref[0, r + 2, t] = flat[t, pl.ds(r, SUB, stride=16), :]
-    top = 14 * (1 - info[3])
-    for r in range(2):
-        for t in range(WT):
-            edge_ref[0, r, t] = flat[t, pl.ds(top + r, SUB, stride=16), :]
-
-
-def gather_rows(x, info):
+
+
+def gather_rows(x):
     return pl.pallas_call(
         gather_kernel,
-        out_shape=[jax.ShapeDtypeStruct((2, n) + ROWS[1:], f32) for n in (20, 2)],
+        out_shape=jax.ShapeDtypeStruct((2,) + ROWS, f32),
         grid=(2,),
-        in_specs=[SMEM, ANYWHERE],
-        out_specs=[pl.BlockSpec((1, n) + ROWS[1:], lambda o: (o, 0, 0, 0, 0)) for n in (20, 2)],
+        in_specs=[ANYWHERE],
+        out_specs=pl.BlockSpec((1,) + ROWS, lambda o: (o, 0, 0, 0, 0)),
         scratch_shapes=[pltpu.VMEM((WT, 16 * SUB, LANES), f32), pltpu.SemaphoreType.DMA((WT,))],
         compiler_params=limit(16),
         cost_estimate=cost(3.0),
         name="gather_rows",
-    )(info, x)
-
-
-def filter_kernel(octet, other, info, taps_ref, _, halo_ref, *rest):
-    rows, outs, token, weight = rest[-7], rest[-6:-2], rest[-2], rest[-1]
+    )(x)
+
+
+def filter_kernel(octet, other, edge_octets, info, taps_ref, _, halo_ref, *rest):
+    rows, outs, edges, token, weight = rest[-8], rest[-7:-3], rest[-3], rest[-2], rest[-1]
     step = pl.program_id(0)
     xs = rows.at[octet + step]
     for r in range(2):
@@ -249,6 +245,11 @@
                 value = halo_ref[0, r, t]
             xs[r, t] = value
             xs[18 + r, t] = value
+    top = 2 + 14 * (1 - info[3])
+    for n, edge_octet in enumerate(edge_octets):
+        for r in range(2):
+            for t in range(WT):
+                edges[n, r, t] = rows[edge_octet, top + r, t]
     taps = [taps_ref[i, j] for i in range(5) for j in range(5)]
     overlap = info[0].astype(f32)
     lane = lane_index().astype(f32) + 0.5
@@ -267,7 +268,7 @@
             filter_row(taps, weight, xs, r, store)
 
 
-def phase_filter(xt, halo, taps, info, octet, count, other, deps=()):
+def phase_filter(xt, halo, taps, info, octet, count, other, deps=(), edge_octets=()):
     tile = (WT, SUB, LANES)
     if other:
         halo_spec = pl.BlockSpec((2, SUB, W), lambda o: (0, octet + o, 0))
@@ -275,13 +276,13 @@
         halo_spec = pl.BlockSpec((1, 2) + tile, lambda o: (octet + o, 0, 0, 0, 0))
     local = pl.BlockSpec(memory_space=pltpu.VMEM)
     return pl.pallas_call(
-        functools.partial(filter_kernel, octet, other),
+        functools.partial(filter_kernel, octet, other, edge_octets),
         out_shape=[jax.ShapeDtypeStruct(xt.shape, f32)]
         + [jax.ShapeDtypeStruct((count, 2) + tile, f32)] * 4
-        + [TOKEN],
+        + [jax.ShapeDtypeStruct((max(len(edge_octets), 1), 2) + tile, f32), TOKEN],
         grid=(count,),
         in_specs=[SMEM, SMEM, local, halo_spec] + [ANYWHERE] * len(deps),
-        out_specs=[local] * 5 + [TOKEN_SPEC],
+        out_specs=[local] * 6 + [TOKEN_SPEC],
         scratch_shapes=[pltpu.VMEM(tile, f32)],
         input_output_aliases={2: 0},
         compiler_params=limit(8),
@@ -443,23 +444,22 @@
 
     edge = lax.dynamic_slice(projections, (0, 14 * x, 0), (16, 2, W))
     near = [row_step(jnp.swapaxes(edge, 0, 1), 1)] * 2
-    xt, edges = gather_rows(projections.reshape(256, W), info)
-    far = row_step(edges, 0)
-    xt, *sent_0, done = phase_filter(xt, near[0], phase_kernel, info, 0, 1, True)
+    xt = gather_rows(projections.reshape(256, W))
+    xt, *sent_0, edges_0, done = phase_filter(xt, near[0], phase_kernel, info, 0, 1, True, [], (0, 1))
+    far = row_step(edges_0, 0)
     parts_0 = y_exchange(sent_0)
-    xt, *sent_1, done = phase_filter(xt, near[1], phase_kernel, info, 1, 1, True, [done])
+    xt, *sent_1, edges_1, done = phase_filter(xt, near[1], phase_kernel, info, 1, 1, True, [done], ())
     parts_1 = y_exchange(sent_1)
     *rows_0, done = stitch_pairs(parts_0, info, [done])
     arrived_0 = send(rows_0)
-    xt, *sent_2, done = phase_filter(xt, far, phase_kernel, info, 0, 2, False, [done])
+    xt, *sent_2, _, done = phase_filter(xt, far, phase_kernel, info, 0, 2, False, [done])
     parts_2 = y_exchange(sent_2)
     *rows_1, done = stitch_pairs(parts_1, info, [done])
     arrived_1 = send(rows_1)
     result, done = ramp_filter(arrived_0, info, consts, 0, None, [done])
-    result, done = ramp_filter(arrived_1, info, consts, 2, result)
-    *rows_2, done = stitch_pairs(parts_2, info, [done])
+    *rows_2, done = stitch_pairs(parts_2, info, [done, arrived_1[0][0, 0, 0], arrived_1[1][0, 0, 0]])
     swapped = flip(rows_2[1], 1)
-    result, done = ramp_filter([rows_2[0]], info, consts, 4, result)
+    result, done = ramp_filter([*arrived_1, rows_2[0]], info, consts, 2, result)
     result, done = ramp_filter([swapped], info, consts, 6, result)
     return result.reshape(1, 128, S)
 

time: 110 us -> 107 us (0.973)
  the two profiles are of different devices: /device:TPU:197 before, /device:TPU:121 now
where the time goes in v4:
time: 107 us
  waiting for transfers between devices  36.9 us (34%)
  Pallas kernels  34.4 us (32%)
  starting transfers between devices  29.5 us (28%)
  local copies, waits for them, and re-layouts  4.46 us (4%)
  between operations  1.49 us (1%)
    ppermute x5, waiting for transfers between devices, flip(): return lax.ppermute(block, 'ang', [(i, i ^ bits) for i in range(16)])  25.5 us
    pallas_call x3, Pallas kernels, ramp_filter(): pl.pallas_call(functools.partial(ramp_kernel, len(rows)), out_shape=[jax....  14.4 us
    pallas_call x3, Pallas kernels, phase_filter(): pl.pallas_call(functools.partial(filter_kernel, octet, other, edge_octets...  12.9 us
    ppermute x9, starting transfers between devices, y_step(): return lax.ppermute(block, 'ang', route)  12.4 us
    ppermute x2, starting transfers between devices, row_step(): return lax.ppermute(block, ('ang', 'row'), route)  11 us
    ppermute x2, waiting for transfers between devices, row_step(): return lax.ppermute(block, ('ang', 'row'), route)  6.43 us
    ppermute x5, starting transfers between devices, flip(): return lax.ppermute(block, 'ang', [(i, i ^ bits) for i in range(16)])  6.11 us
    ppermute x9, waiting for transfers between devices, y_step(): return lax.ppermute(block, 'ang', route)  4.97 us
  transfers between devices with their start and end apart: 16, of which 4 were waited for; matrix products, arithmetic and copies ran while one was open for 0% of the time, Pallas kernels for 24%

profile of v4, /device:TPU:121, one launch (start us, length us, event | category | flops | bytes accessed | tf_op | source)
XLA Modules:
  0.0 106.7 jit_solution(7021099472194348548)
XLA Ops:
  0.0 1.9 %constant_dynamic-slice_fusion = f32[16,2,4608]{2,1,0:T(2,128)S(1)} fusion(f32[16,16,4608]{2,1,0:T(8,128)} %param.10, s32[]{:T(128)S(6)} %select_n.3), kind=kLoop, calls=%fused_computation.3 | loop fusion | bytes 1179652 | tf_op jit(solution)/shard_map/dynamic_slice | solution.py:445
  1.9 0.1 copy.19
  2.0 4.2 %collective-permute-start = (f32[2,16,4608]{2,1,0:T(8,128)S(1)}, f32[2,16,4608]{2,1,0:T(8,128)S(1)}, u32[]{:S(2)}, u32[]{:S(2)}) collective-permute-start(f32[2,16,4608]{2,1,0:T(8,128)S(1)} %bitcast.15), channel_id=1, source_target_pairs={{32,33},{48,49},{96,97},{112,113},{160,161},{176,177},{224,225},{2... | collective-permute-start | bytes 1769480 | tf_op jit(solution)/shard_map/ppermute | solution.py:418
  7.5 0.1 stack.17.info
  7.6 0.0 copy-start
  7.6 2.3 %copy-done = f32[16,16,4608]{2,1,0:T(8,128)S(1)} copy-done((f32[16,16,4608]{2,1,0:T(8,128)S(1)}, f32[16,16,4608]{2,1,0:T(8,128)}, u32[]{:S(2)}) %copy-start) | copy-done | bytes 4718616
  10.0 3.2 %gather_rows.1._ = f32[2,20,36,8,128]{4,3,2,1,0:T(8,128)S(1)} custom-call(f32[256,4608]{1,0:T(8,128)S(1)} %bitcast.14), custom_call_target="tpu_custom_call" | custom-call | flops 34500000 | bytes 4096 | tf_op jit(solution)/shard_map/gather_rows/pallas_call | solution.py:223
  13.2 6.4 %collective-permute-done.halo_ref = f32[2,16,4608]{2,1,0:T(8,128)S(1)} collective-permute-done((f32[2,16,4608]{2,1,0:T(8,128)S(1)}, f32[2,16,4608]{2,1,0:T(8,128)S(1)}, u32[]{:S(2)}, u32[]{:S(2)}) %collective-permute-start) | collective-permute-done | bytes 589856 | tf_op jit(solution)/shard_map/ppermute | solution.py:418
  19.6 3.1 %phase_filter.3 = (f32[2,20,36,8,128]{4,3,2,1,0:T(8,128)S(1)}, f32[1,2,36,8,128]{4,3,2,1,0:T(8,128)S(1)}, f32[1,2,36,8,128]{4,3,2,1,0:T(8,128)S(1)}, f32[1,2,36,...) custom-call(s32[29]{0:T(128)S(1)} %stack.17.info, ...), custom_call_target="tpu_custom_call", output_to_operand_aliasing={{0}: (2, {})} | custom-call | flops 57500000 | bytes 4096 | tf_op jit(solution)/shard_map/phase_filter/pallas_call | solution.py:278
  22.7 6.8 %collective-permute-start.1 = (f32[2,2,36,8,128]{4,3,2,1,0:T(8,128)S(1)}, f32[2,2,36,8,128]{4,3,2,1,0:T(8,128)S(1)}, u32[]{:S(2)}, u32[]{:S(2)}) collective-permute-start(f32[2,2,36,8,128]{4,3,2,1,0:T(8,128)S(1)} %get-tuple-element.38), channel_id=1, source_target_pairs={{0,1},{16,17},{64,65},{80,81},{128,129},{144,145},{192,193},{208,2... | collective-permute-start | bytes 1769480 | tf_op jit(solution)/shard_map/ppermute | solution.py:418
  29.5 0.1 collective-permute-start.2
  29.6 2.2 %collective-permute-start.3 = (f32[1,2,36,8,128]{4,3,2,1,0:T(8,128)S(1)}, f32[1,2,36,8,128]{4,3,2,1,0:T(8,128)S(1)}, u32[]{:S(2)}, u32[]{:S(2)}) collective-permute-start(f32[1,2,36,8,128]{4,3,2,1,0:T(8,128)S(1)} %get-tuple-element.41), channel_id=1, source_target_pairs={{0,128},{16,144},{32,160},{48,176},{64,192},{80,208},{96,224},{112... | collective-permute-start | bytes 884744 | tf_op jit(solution)/shard_map/ppermute | solution.py:403
  31.8 0.0 collective-permute-start.4
  31.8 3.5 %phase_filter.4 = (f32[2,20,36,8,128]{4,3,2,1,0:T(8,128)S(1)}, f32[1,2,36,8,128]{4,3,2,1,0:T(8,128)S(1)}, f32[1,2,36,8,128]{4,3,2,1,0:T(8,128)S(1)}, f32[1,2,36,...) custom-call(s32[29]{0:T(128)S(1)} %stack.17.info, ...), custom_call_target="tpu_custom_call", output_to_operand_aliasing={{0}: (2, {})} | custom-call | flops 57500000 | bytes 4096 | tf_op jit(solution)/shard_map/phase_filter/pallas_call | solution.py:278
  35.3 0.0 copy-start.5
  35.3 0.0 copy-start.6
  35.3 2.8 %collective-permute-start.10 = (f32[1,2,36,8,128]{4,3,2,1,0:T(8,128)S(1)}, f32[1,2,36,8,128]{4,3,2,1,0:T(8,128)S(1)}, u32[]{:S(2)}, u32[]{:S(2)}) collective-permute-start(f32[1,2,36,8,128]{4,3,2,1,0:T(8,128)S(1)} %get-tuple-element.52), channel_id=1, source_target_pairs={{0,64},{16,80},{32,96},{48,112},{64,128},{80,144},{96,160},{112,17... | collective-permute-start | bytes 884744 | tf_op jit(solution)/shard_map/ppermute | solution.py:403
  38.1 0.0 collective-permute-done.2.r1
  38.1 0.2 collective-permute-start.11
  38.3 0.0 collective-permute-done.3.r2
  38.3 4.6 %collective-permute-start.12 = (f32[1,2,36,8,128]{4,3,2,1,0:T(8,128)S(1)}, f32[1,2,36,8,128]{4,3,2,1,0:T(8,128)S(1)}, u32[]{:S(2)}, u32[]{:S(2)}) collective-permute-start(f32[1,2,36,8,128]{4,3,2,1,0:T(8,128)S(1)} %get-tuple-element.54), channel_id=1, source_target_pairs={{0,192},{16,208},{32,224},{48,240},{64,0},{80,16},{96,32},{112,48}... | collective-permute-start | bytes 884744 | tf_op jit(solution)/shard_map/ppermute | solution.py:403
  42.9 4.9 %collective-permute-done.4.r3 = f32[1,2,36,8,128]{4,3,2,1,0:T(8,128)S(1)} collective-permute-done((f32[1,2,36,8,128]{4,3,2,1,0:T(8,128)S(1)}, f32[1,2,36,8,128]{4,3,2,1,0:T(8,128)S(1)}, u32[]{:S(2)}, u32[]{:S(2)}) %collective-permute-start.4) | collective-permute-done | bytes 294944 | tf_op jit(solution)/shard_map/ppermute | solution.py:403
  47.9 0.9 stitch_pairs.3
  48.8 0.1 collective-permute-start.8
  48.9 0.0 collective-permute-done.1.halo_ref
  48.9 5.4 %collective-permute-start.9 = (f32[2,1,61,8,128]{4,3,2,1,0:T(8,128)S(1)}, f32[2,1,61,8,128]{4,3,2,1,0:T(8,128)S(1)}, u32[]{:S(2)}, u32[]{:S(2)}) collective-permute-start(f32[2,1,61,8,128]{4,3,2,1,0:T(8,128)S(1)} %get-tuple-element.50), channel_id=1, source_target_pairs={{0,48},{16,32},{32,16},{48,0},{64,112},{80,96},{96,80},{112,64},{1... | collective-permute-start | bytes 1499144 | tf_op jit(solution)/shard_map/ppermute | solution.py:407
  54.3 6.3 %phase_filter.5 = (f32[2,20,36,8,128]{4,3,2,1,0:T(8,128)S(1)}, f32[2,2,36,8,128]{4,3,2,1,0:T(8,128)S(1)}, f32[2,2,36,8,128]{4,3,2,1,0:T(8,128)S(1)}, f32[2,2,36,...) custom-call(s32[29]{0:T(128)S(1)} %stack.17.info, ...), custom_call_target="tpu_custom_call", output_to_operand_aliasing={{0}: (2, {})} | custom-call | flops 57500000 | bytes 4096 | tf_op jit(solution)/shard_map/phase_filter/pallas_call | solution.py:278
  60.6 0.0 collective-permute-done.10.r1
  60.6 0.0 collective-permute-done.11.r2
  60.6 0.0 collective-permute-done.12.r3
  60.6 0.9 stitch_pairs.4
  61.6 0.1 collective-permute-start.13
  61.7 0.5 collective-permute-start.14
  62.2 0.8 collective-permute-start.5
  63.0 0.0 collective-permute-done.8.refs_0_
  63.0 1.7 %collective-permute-start.6 = (f32[2,2,36,8,128]{4,3,2,1,0:T(8,128)S(1)}, f32[2,2,36,8,128]{4,3,2,1,0:T(8,128)S(1)}, u32[]{:S(2)}, u32[]{:S(2)}) collective-permute-start(f32[2,2,36,8,128]{4,3,2,1,0:T(8,128)S(1)} %get-tuple-element.47), channel_id=1, source_target_pairs={{0,128},{16,144},{32,160},{48,176},{64,192},{80,208},{96,224},{112... | collective-permute-start | bytes 1769480 | tf_op jit(solution)/shard_map/ppermute | solution.py:403
  64.7 12.6 %collective-permute-done.9.refs_1_ = f32[2,1,61,8,128]{4,3,2,1,0:T(8,128)S(1)} collective-permute-done((f32[2,1,61,8,128]{4,3,2,1,0:T(8,128)S(1)}, f32[2,1,61,8,128]{4,3,2,1,0:T(8,128)S(1)}, u32[]{:S(2)}, u32[]{:S(2)}) %collective-permute-start.9) | collective-permute-done | bytes 499744 | tf_op jit(solution)/shard_map/ppermute | solution.py:407
  77.3 0.0 collective-permute-start.7
  77.4 3.9 %ramp_filter.3 = (f32[2,2,2,2,8,8192]{5,4,3,2,1,0:T(8,128)}, f32[8,128]{1,0:T(8,128)S(1)}) custom-call(s32[29]{0:T(128)S(1)} %stack.17.info, f32[2,1,61,8,128]{4,3,2,1,0:T(8,128)S(1)} %collective-permute-done.8.refs_0_, f32[2,1,61,8,128]{4,3,2,1,0:T(8,128)S(1)} %collective-permute-done.9.refs_1_, f32[2,64,8,128]{3,2,1,0:T(8,128)S(1)} %copy-done.1, ...), custom_call_target="tpu_custom_call" | custom-call | flops 23000000 | bytes 4096 | tf_op jit(solution)/shard_map/ramp_filter/pallas_call | solution.py:380
  81.3 0.0 collective-permute-done.13.refs_0_
  81.3 12.8 %collective-permute-done.14.refs_1_ = f32[2,1,61,8,128]{4,3,2,1,0:T(8,128)S(1)} collective-permute-done((f32[2,1,61,8,128]{4,3,2,1,0:T(8,128)S(1)}, f32[2,1,61,8,128]{4,3,2,1,0:T(8,128)S(1)}, u32[]{:S(2)}, u32[]{:S(2)}) %collective-permute-start.14) | collective-permute-done | bytes 499744 | tf_op jit(solution)/shard_map/ppermute | solution.py:407
  94.2 0.0 collective-permute-done.5.r1
  94.2 0.0 collective-permute-done.6.r2
  94.2 2.1 %stitch_pairs.5 = (f32[2,2,61,8,128]{4,3,2,1,0:T(8,128)S(1)}, f32[2,2,61,8,128]{4,3,2,1,0:T(8,128)S(1)}, f32[8,128]{1,0:T(8,128)}) custom-call(s32[29]{0:T(128)S(1)} %stack.17.info, f32[2,2,36,8,128]{4,3,2,1,0:T(8,128)S(1)} %get-tuple-element.45.r0, f32[2,2,36,8,128]{4,3,2,1,0:T(8,128)S(1)} %collective-permute-done.5.r1, ...), custom_call_target="tpu_custom_call" | custom-call | flops 17250000 | bytes 4096 | tf_op jit(solution)/shard_map/stitch_pairs/pallas_call | solution.py:323
  96.3 0.0 collective-permute-start.15
  96.3 6.5 %ramp_filter.4 = (f32[2,2,2,2,8,8192]{5,4,3,2,1,0:T(8,128)}, f32[8,128]{1,0:T(8,128)}) custom-call(s32[29]{0:T(128)S(1)} %stack.17.info, f32[2,1,61,8,128]{4,3,2,1,0:T(8,128)S(1)} %collective-permute-done.13.refs_0_, f32[2,1,61,8,128]{4,3,2,1,0:T(8,128)S(1)} %collective-permute-done.14.refs_1_, ...), custom_call_target="tpu_custom_call", output_to_operand_aliasing={{0}: (10, {})} | custom-call | flops 23000000 | bytes 4096 | tf_op jit(solution)/shard_map/ramp_filter/pallas_call | solution.py:380
  102.8 0.0 collective-permute-done.15.refs_0_
  102.8 3.9 %ramp_filter.5 = (f32[2,2,2,2,8,8192]{5,4,3,2,1,0:T(8,128)}, f32[8,128]{1,0:T(8,128)}) custom-call(s32[29]{0:T(128)S(1)} %stack.17.info, f32[2,2,61,8,128]{4,3,2,1,0:T(8,128)S(1)} %collective-permute-done.15.refs_0_, f32[2,64,8,128]{3,2,1,0:T(8,128)S(1)} %copy-done.1, f32[512,128]{1,0:T(8,128)S(1)} %copy-done.2, ...), custom_call_target="tpu_custom_call", output_to_operand_aliasing={{0}: (8, {})} | custom-call | flops 23000000 | bytes 4096 | tf_op jit(solution)/shard_map/ramp_filter/pallas_call | solution.py:380
  (15 shorter events, 0.0 us)
Async XLA Ops:
  2.0 17.6 %collective-permute-start = (f32[2,16,4608]{2,1,0:T(8,128)S(1)}, f32[2,16,4608]{2,1,0:T(8,128)S(1)}, u32[]{:S(2)}, u32[]{:S(2)}) collective-permute-start(f32[2,16,4608]{2,1,0:T(8,128)S(1)} %bitcast.15), channel_id=1, source_target_pairs={{32,33},{48,49},{96,97},{112,113},{160,161},{176,177},{224,225},{2... | collective-permute-start | bytes 1769480 | tf_op jit(solution)/shard_map/ppermute | solution.py:418
  7.6 2.3 %copy-start = (f32[16,16,4608]{2,1,0:T(8,128)S(1)}, f32[16,16,4608]{2,1,0:T(8,128)}, u32[]{:S(2)}) copy-start(f32[16,16,4608]{2,1,0:T(8,128)} %param.10) | copy-start | bytes 14155780
  10.0 9.6 %copy-start.7 = (f32[5,5]{1,0:T(8,128)S(1)}, f32[5,5]{1,0:T(8,128)}, u32[]{:S(2)}) copy-start(f32[5,5]{1,0:T(8,128)} %taps_ref.5) | copy-start | bytes 304
  22.7 26.2 %collective-permute-start.1 = (f32[2,2,36,8,128]{4,3,2,1,0:T(8,128)S(1)}, f32[2,2,36,8,128]{4,3,2,1,0:T(8,128)S(1)}, u32[]{:S(2)}, u32[]{:S(2)}) collective-permute-start(f32[2,2,36,8,128]{4,3,2,1,0:T(8,128)S(1)} %get-tuple-element.38), channel_id=1, source_target_pairs={{0,1},{16,17},{64,65},{80,81},{128,129},{144,145},{192,193},{208,2... | collective-permute-start | bytes 1769480 | tf_op jit(solution)/shard_map/ppermute | solution.py:418
  29.5 8.6 %collective-permute-start.2 = (f32[1,2,36,8,128]{4,3,2,1,0:T(8,128)S(1)}, f32[1,2,36,8,128]{4,3,2,1,0:T(8,128)S(1)}, u32[]{:S(2)}, u32[]{:S(2)}) collective-permute-start(f32[1,2,36,8,128]{4,3,2,1,0:T(8,128)S(1)} %get-tuple-element.40), channel_id=1, source_target_pairs={{0,64},{16,80},{32,96},{48,112},{64,128},{80,144},{96,160},{112,17... | collective-permute-start | bytes 884744 | tf_op jit(solution)/shard_map/ppermute | solution.py:403
  29.6 8.7 %collective-permute-start.3 = (f32[1,2,36,8,128]{4,3,2,1,0:T(8,128)S(1)}, f32[1,2,36,8,128]{4,3,2,1,0:T(8,128)S(1)}, u32[]{:S(2)}, u32[]{:S(2)}) collective-permute-start(f32[1,2,36,8,128]{4,3,2,1,0:T(8,128)S(1)} %get-tuple-element.41), channel_id=1, source_target_pairs={{0,128},{16,144},{32,160},{48,176},{64,192},{80,208},{96,224},{112... | collective-permute-start | bytes 884744 | tf_op jit(solution)/shard_map/ppermute | solution.py:403
  31.8 16.1 %collective-permute-start.4 = (f32[1,2,36,8,128]{4,3,2,1,0:T(8,128)S(1)}, f32[1,2,36,8,128]{4,3,2,1,0:T(8,128)S(1)}, u32[]{:S(2)}, u32[]{:S(2)}) collective-permute-start(f32[1,2,36,8,128]{4,3,2,1,0:T(8,128)S(1)} %get-tuple-element.42), channel_id=1, source_target_pairs={{0,192},{16,208},{32,224},{48,240},{64,0},{80,16},{96,32},{112,48}... | collective-permute-start | bytes 884744 | tf_op jit(solution)/shard_map/ppermute | solution.py:403
  35.3 42.1 %copy-start.1 = (f32[2,64,8,128]{3,2,1,0:T(8,128)S(1)}, f32[2,64,8,128]{3,2,1,0:T(8,128)}, u32[]{:S(2)}) copy-start(f32[2,64,8,128]{3,2,1,0:T(8,128)} %constant.33.clone.refs_2_.refs_3_.refs_1_) | copy-start | bytes 1572868
  35.3 42.1 %copy-start.2 = (f32[512,128]{1,0:T(8,128)S(1)}, f32[512,128]{1,0:T(8,128)}, u32[]{:S(2)}) copy-start(f32[512,128]{1,0:T(8,128)} %constant.34.clone.refs_3_.refs_4_.refs_2_) | copy-start | bytes 786436
  35.3 42.1 %copy-start.3 = (bf16[256,256]{1,0:T(8,128)(2,1)S(1)}, bf16[256,256]{1,0:T(8,128)(2,1)}, u32[]{:S(2)}) copy-start(bf16[256,256]{1,0:T(8,128)(2,1)} %constant.38.clone.refs_7_.refs_8_.refs_6_) | copy-start | bytes 393220
  35.3 42.1 %copy-start.4 = (bf16[256,256]{1,0:T(8,128)(2,1)S(1)}, bf16[256,256]{1,0:T(8,128)(2,1)}, u32[]{:S(2)}) copy-start(bf16[256,256]{1,0:T(8,128)(2,1)} %constant.37.clone.refs_6_.refs_7_.refs_5_) | copy-start | bytes 393220
  35.3 42.1 %copy-start.5 = (bf16[256,256]{1,0:T(8,128)(2,1)S(1)}, bf16[256,256]{1,0:T(8,128)(2,1)}, u32[]{:S(2)}) copy-start(bf16[256,256]{1,0:T(8,128)(2,1)} %constant.36.clone.refs_5_.refs_6_.refs_4_) | copy-start | bytes 393220
  35.3 42.1 %copy-start.6 = (bf16[256,256]{1,0:T(8,128)(2,1)S(1)}, bf16[256,256]{1,0:T(8,128)(2,1)}, u32[]{:S(2)}) copy-start(bf16[256,256]{1,0:T(8,128)(2,1)} %constant.35.clone.refs_4_.refs_5_.refs_3_) | copy-start | bytes 393220
  35.3 25.3 %collective-permute-start.10 = (f32[1,2,36,8,128]{4,3,2,1,0:T(8,128)S(1)}, f32[1,2,36,8,128]{4,3,2,1,0:T(8,128)S(1)}, u32[]{:S(2)}, u32[]{:S(2)}) collective-permute-start(f32[1,2,36,8,128]{4,3,2,1,0:T(8,128)S(1)} %get-tuple-element.52), channel_id=1, source_target_pairs={{0,64},{16,80},{32,96},{48,112},{64,128},{80,144},{96,160},{112,17... | collective-permute-start | bytes 884744 | tf_op jit(solution)/shard_map/ppermute | solution.py:403
  38.1 22.5 %collective-permute-start.11 = (f32[1,2,36,8,128]{4,3,2,1,0:T(8,128)S(1)}, f32[1,2,36,8,128]{4,3,2,1,0:T(8,128)S(1)}, u32[]{:S(2)}, u32[]{:S(2)}) collective-permute-start(f32[1,2,36,8,128]{4,3,2,1,0:T(8,128)S(1)} %get-tuple-element.53), channel_id=1, source_target_pairs={{0,128},{16,144},{32,160},{48,176},{64,192},{80,208},{96,224},{112... | collective-permute-start | bytes 884744 | tf_op jit(solution)/shard_map/ppermute | solution.py:403
  38.3 22.3 %collective-permute-start.12 = (f32[1,2,36,8,128]{4,3,2,1,0:T(8,128)S(1)}, f32[1,2,36,8,128]{4,3,2,1,0:T(8,128)S(1)}, u32[]{:S(2)}, u32[]{:S(2)}) collective-permute-start(f32[1,2,36,8,128]{4,3,2,1,0:T(8,128)S(1)} %get-tuple-element.54), channel_id=1, source_target_pairs={{0,192},{16,208},{32,224},{48,240},{64,0},{80,16},{96,32},{112,48}... | collective-permute-start | bytes 884744 | tf_op jit(solution)/shard_map/ppermute | solution.py:403
  48.8 14.2 %collective-permute-start.8 = (f32[2,1,61,8,128]{4,3,2,1,0:T(8,128)S(1)}, f32[2,1,61,8,128]{4,3,2,1,0:T(8,128)S(1)}, u32[]{:S(2)}, u32[]{:S(2)}) collective-permute-start(f32[2,1,61,8,128]{4,3,2,1,0:T(8,128)S(1)} %get-tuple-element.49), channel_id=1, source_target_pairs={{0,32},{16,48},{32,0},{48,16},{64,96},{80,112},{96,64},{112,80},{1... | collective-permute-start | bytes 1499144 | tf_op jit(solution)/shard_map/ppermute | solution.py:407
  48.9 28.4 %collective-permute-start.9 = (f32[2,1,61,8,128]{4,3,2,1,0:T(8,128)S(1)}, f32[2,1,61,8,128]{4,3,2,1,0:T(8,128)S(1)}, u32[]{:S(2)}, u32[]{:S(2)}) collective-permute-start(f32[2,1,61,8,128]{4,3,2,1,0:T(8,128)S(1)} %get-tuple-element.50), channel_id=1, source_target_pairs={{0,48},{16,32},{32,16},{48,0},{64,112},{80,96},{96,80},{112,64},{1... | collective-permute-start | bytes 1499144 | tf_op jit(solution)/shard_map/ppermute | solution.py:407
  61.6 19.8 %collective-permute-start.13 = (f32[2,1,61,8,128]{4,3,2,1,0:T(8,128)S(1)}, f32[2,1,61,8,128]{4,3,2,1,0:T(8,128)S(1)}, u32[]{:S(2)}, u32[]{:S(2)}) collective-permute-start(f32[2,1,61,8,128]{4,3,2,1,0:T(8,128)S(1)} %get-tuple-element.58), channel_id=1, source_target_pairs={{0,32},{16,48},{32,0},{48,16},{64,96},{80,112},{96,64},{112,80},{1... | collective-permute-start | bytes 1499144 | tf_op jit(solution)/shard_map/ppermute | solution.py:407
  61.7 32.5 %collective-permute-start.14 = (f32[2,1,61,8,128]{4,3,2,1,0:T(8,128)S(1)}, f32[2,1,61,8,128]{4,3,2,1,0:T(8,128)S(1)}, u32[]{:S(2)}, u32[]{:S(2)}) collective-permute-start(f32[2,1,61,8,128]{4,3,2,1,0:T(8,128)S(1)} %get-tuple-element.59), channel_id=1, source_target_pairs={{0,48},{16,32},{32,16},{48,0},{64,112},{80,96},{96,80},{112,64},{1... | collective-permute-start | bytes 1499144 | tf_op jit(solution)/shard_map/ppermute | solution.py:407
  62.2 32.0 %collective-permute-start.5 = (f32[2,2,36,8,128]{4,3,2,1,0:T(8,128)S(1)}, f32[2,2,36,8,128]{4,3,2,1,0:T(8,128)S(1)}, u32[]{:S(2)}, u32[]{:S(2)}) collective-permute-start(f32[2,2,36,8,128]{4,3,2,1,0:T(8,128)S(1)} %get-tuple-element.46), channel_id=1, source_target_pairs={{0,64},{16,80},{32,96},{48,112},{64,128},{80,144},{96,160},{112,17... | collective-permute-start | bytes 1769480 | tf_op jit(solution)/shard_map/ppermute | solution.py:403
  63.0 31.1 %collective-permute-start.6 = (f32[2,2,36,8,128]{4,3,2,1,0:T(8,128)S(1)}, f32[2,2,36,8,128]{4,3,2,1,0:T(8,128)S(1)}, u32[]{:S(2)}, u32[]{:S(2)}) collective-permute-start(f32[2,2,36,8,128]{4,3,2,1,0:T(8,128)S(1)} %get-tuple-element.47), channel_id=1, source_target_pairs={{0,128},{16,144},{32,160},{48,176},{64,192},{80,208},{96,224},{112... | collective-permute-start | bytes 1769480 | tf_op jit(solution)/shard_map/ppermute | solution.py:403
  77.3 16.8 %collective-permute-start.7 = (f32[2,2,36,8,128]{4,3,2,1,0:T(8,128)S(1)}, f32[2,2,36,8,128]{4,3,2,1,0:T(8,128)S(1)}, u32[]{:S(2)}, u32[]{:S(2)}) collective-permute-start(f32[2,2,36,8,128]{4,3,2,1,0:T(8,128)S(1)} %get-tuple-element.48), channel_id=1, source_target_pairs={{0,192},{16,208},{32,224},{48,240},{64,0},{80,16},{96,32},{112,48}... | collective-permute-start | bytes 1769480 | tf_op jit(solution)/shard_map/ppermute | solution.py:403
  96.3 6.5 %collective-permute-start.15 = (f32[2,2,61,8,128]{4,3,2,1,0:T(8,128)S(1)}, f32[2,2,61,8,128]{4,3,2,1,0:T(8,128)S(1)}, u32[]{:S(2)}, u32[]{:S(2)}) collective-permute-start(f32[2,2,61,8,128]{4,3,2,1,0:T(8,128)S(1)} %get-tuple-element.60), channel_id=1, source_target_pairs={{0,16},{16,0},{32,48},{48,32},{64,80},{80,64},{96,112},{112,96},{1... | collective-permute-start | bytes 2998280 | tf_op jit(solution)/shard_map/ppermute | solution.py:407

commit v5 on v4

--- a/solution.py
+++ b/solution.py
@@ -456,10 +456,10 @@
     parts_2 = y_exchange(sent_2)
     *rows_1, done = stitch_pairs(parts_1, info, [done])
     arrived_1 = send(rows_1)
-    result, done = ramp_filter(arrived_0, info, consts, 0, None, [done])
+    result, done = ramp_filter([*arrived_0, arrived_1[0]], info, consts, 0, None, [done])
     *rows_2, done = stitch_pairs(parts_2, info, [done, arrived_1[0][0, 0, 0], arrived_1[1][0, 0, 0]])
     swapped = flip(rows_2[1], 1)
-    result, done = ramp_filter([*arrived_1, rows_2[0]], info, consts, 2, result)
+    result, done = ramp_filter([arrived_1[1], rows_2[0]], info, consts, 3, result)
     result, done = ramp_filter([swapped], info, consts, 6, result)
     return result.reshape(1, 128, S)
 

time: 107 us -> 106 us (level)
  waiting for transfers between devices: 36.9 us -> 35.6 us
    ppermute x5, waiting for transfers between devices: 25.5 us -> 24.2 us  [flip(): return lax.ppermute(block, 'ang', [(i, i ^ bits) for i in range(16)])]
  transfers between devices with their start and end apart: 16 -> 16, of which waited for: 4 -> 5; matrix products, arithmetic and copies ran while one was open for 0% -> 0% of each run, Pallas kernels for 24% -> 24%
where the time goes in v5:
time: 106 us; the launch traced here: 105 us
  waiting for transfers between devices  35.6 us (34%)
  Pallas kernels  34.4 us (32%)
  starting transfers between devices  29.5 us (28%)
  local copies, waits for them, and re-layouts  4.46 us (4%)
  between operations  1.49 us (1%)
    ppermute x5, waiting for transfers between devices, flip(): return lax.ppermute(block, 'ang', [(i, i ^ bits) for i in range(16)])  24.2 us
    pallas_call x3, Pallas kernels, ramp_filter(): pl.pallas_call(functools.partial(ramp_kernel, len(rows)), out_shape=[jax....  14.4 us
    pallas_call x3, Pallas kernels, phase_filter(): pl.pallas_call(functools.partial(filter_kernel, octet, other, edge_octets...  12.9 us
    ppermute x9, starting transfers between devices, y_step(): return lax.ppermute(block, 'ang', route)  12.4 us
    ppermute x2, starting transfers between devices, row_step(): return lax.ppermute(block, ('ang', 'row'), route)  11 us
    ppermute x2, waiting for transfers between devices, row_step(): return lax.ppermute(block, ('ang', 'row'), route)  6.43 us
    ppermute x5, starting transfers between devices, flip(): return lax.ppermute(block, 'ang', [(i, i ^ bits) for i in range(16)])  6.11 us
    ppermute x9, waiting for transfers between devices, y_step(): return lax.ppermute(block, 'ang', route)  4.97 us
  transfers between devices with their start and end apart: 16, of which 5 were waited for; matrix products, arithmetic and copies ran while one was open for 0% of the time, Pallas kernels for 24%

profile of v5, /device:TPU:121, one launch (start us, length us, event | category | flops | bytes accessed | tf_op | source)
XLA Modules:
  0.0 105.4 jit_solution(14060780298558764266)
XLA Ops:
  0.0 1.9 %constant_dynamic-slice_fusion = f32[16,2,4608]{2,1,0:T(2,128)S(1)} fusion(f32[16,16,4608]{2,1,0:T(8,128)} %param.10, s32[]{:T(128)S(6)} %select_n.3), kind=kLoop, calls=%fused_computation.3 | loop fusion | bytes 1179652 | tf_op jit(solution)/shard_map/dynamic_slice | solution.py:445
  1.9 0.1 copy.19
  2.0 4.2 %collective-permute-start = (f32[2,16,4608]{2,1,0:T(8,128)S(1)}, f32[2,16,4608]{2,1,0:T(8,128)S(1)}, u32[]{:S(2)}, u32[]{:S(2)}) collective-permute-start(f32[2,16,4608]{2,1,0:T(8,128)S(1)} %bitcast.15), channel_id=1, source_target_pairs={{32,33},{48,49},{96,97},{112,113},{160,161},{176,177},{224,225},{2... | collective-permute-start | bytes 1769480 | tf_op jit(solution)/shard_map/ppermute | solution.py:418
  7.5 0.1 stack.17.info
  7.6 0.0 copy-start
  7.6 2.3 %copy-done = f32[16,16,4608]{2,1,0:T(8,128)S(1)} copy-done((f32[16,16,4608]{2,1,0:T(8,128)S(1)}, f32[16,16,4608]{2,1,0:T(8,128)}, u32[]{:S(2)}) %copy-start) | copy-done | bytes 4718616
  10.0 3.2 %gather_rows.1._ = f32[2,20,36,8,128]{4,3,2,1,0:T(8,128)S(1)} custom-call(f32[256,4608]{1,0:T(8,128)S(1)} %bitcast.14), custom_call_target="tpu_custom_call" | custom-call | flops 34500000 | bytes 4096 | tf_op jit(solution)/shard_map/gather_rows/pallas_call | solution.py:223
  13.2 6.4 %collective-permute-done.halo_ref = f32[2,16,4608]{2,1,0:T(8,128)S(1)} collective-permute-done((f32[2,16,4608]{2,1,0:T(8,128)S(1)}, f32[2,16,4608]{2,1,0:T(8,128)S(1)}, u32[]{:S(2)}, u32[]{:S(2)}) %collective-permute-start) | collective-permute-done | bytes 589856 | tf_op jit(solution)/shard_map/ppermute | solution.py:418
  19.6 3.1 %phase_filter.3 = (f32[2,20,36,8,128]{4,3,2,1,0:T(8,128)S(1)}, f32[1,2,36,8,128]{4,3,2,1,0:T(8,128)S(1)}, f32[1,2,36,8,128]{4,3,2,1,0:T(8,128)S(1)}, f32[1,2,36,...) custom-call(s32[29]{0:T(128)S(1)} %stack.17.info, ...), custom_call_target="tpu_custom_call", output_to_operand_aliasing={{0}: (2, {})} | custom-call | flops 57500000 | bytes 4096 | tf_op jit(solution)/shard_map/phase_filter/pallas_call | solution.py:278
  22.7 6.8 %collective-permute-start.1 = (f32[2,2,36,8,128]{4,3,2,1,0:T(8,128)S(1)}, f32[2,2,36,8,128]{4,3,2,1,0:T(8,128)S(1)}, u32[]{:S(2)}, u32[]{:S(2)}) collective-permute-start(f32[2,2,36,8,128]{4,3,2,1,0:T(8,128)S(1)} %get-tuple-element.38), channel_id=1, source_target_pairs={{0,1},{16,17},{64,65},{80,81},{128,129},{144,145},{192,193},{208,2... | collective-permute-start | bytes 1769480 | tf_op jit(solution)/shard_map/ppermute | solution.py:418
  29.5 0.1 collective-permute-start.2
  29.6 2.2 %collective-permute-start.3 = (f32[1,2,36,8,128]{4,3,2,1,0:T(8,128)S(1)}, f32[1,2,36,8,128]{4,3,2,1,0:T(8,128)S(1)}, u32[]{:S(2)}, u32[]{:S(2)}) collective-permute-start(f32[1,2,36,8,128]{4,3,2,1,0:T(8,128)S(1)} %get-tuple-element.41), channel_id=1, source_target_pairs={{0,128},{16,144},{32,160},{48,176},{64,192},{80,208},{96,224},{112... | collective-permute-start | bytes 884744 | tf_op jit(solution)/shard_map/ppermute | solution.py:403
  31.8 0.0 collective-permute-start.4
  31.8 3.5 %phase_filter.4 = (f32[2,20,36,8,128]{4,3,2,1,0:T(8,128)S(1)}, f32[1,2,36,8,128]{4,3,2,1,0:T(8,128)S(1)}, f32[1,2,36,8,128]{4,3,2,1,0:T(8,128)S(1)}, f32[1,2,36,...) custom-call(s32[29]{0:T(128)S(1)} %stack.17.info, ...), custom_call_target="tpu_custom_call", output_to_operand_aliasing={{0}: (2, {})} | custom-call | flops 57500000 | bytes 4096 | tf_op jit(solution)/shard_map/phase_filter/pallas_call | solution.py:278
  35.3 0.0 copy-start.5
  35.3 0.0 copy-start.6
  35.3 2.8 %collective-permute-start.10 = (f32[1,2,36,8,128]{4,3,2,1,0:T(8,128)S(1)}, f32[1,2,36,8,128]{4,3,2,1,0:T(8,128)S(1)}, u32[]{:S(2)}, u32[]{:S(2)}) collective-permute-start(f32[1,2,36,8,128]{4,3,2,1,0:T(8,128)S(1)} %get-tuple-element.52), channel_id=1, source_target_pairs={{0,64},{16,80},{32,96},{48,112},{64,128},{80,144},{96,160},{112,17... | collective-permute-start | bytes 884744 | tf_op jit(solution)/shard_map/ppermute | solution.py:403
  38.1 0.0 collective-permute-done.2.r1
  38.1 0.2 collective-permute-start.11
  38.3 0.0 collective-permute-done.3.r2
  38.3 4.6 %collective-permute-start.12 = (f32[1,2,36,8,128]{4,3,2,1,0:T(8,128)S(1)}, f32[1,2,36,8,128]{4,3,2,1,0:T(8,128)S(1)}, u32[]{:S(2)}, u32[]{:S(2)}) collective-permute-start(f32[1,2,36,8,128]{4,3,2,1,0:T(8,128)S(1)} %get-tuple-element.54), channel_id=1, source_target_pairs={{0,192},{16,208},{32,224},{48,240},{64,0},{80,16},{96,32},{112,48}... | collective-permute-start | bytes 884744 | tf_op jit(solution)/shard_map/ppermute | solution.py:403
  42.9 4.9 %collective-permute-done.4.r3 = f32[1,2,36,8,128]{4,3,2,1,0:T(8,128)S(1)} collective-permute-done((f32[1,2,36,8,128]{4,3,2,1,0:T(8,128)S(1)}, f32[1,2,36,8,128]{4,3,2,1,0:T(8,128)S(1)}, u32[]{:S(2)}, u32[]{:S(2)}) %collective-permute-start.4) | collective-permute-done | bytes 294944 | tf_op jit(solution)/shard_map/ppermute | solution.py:403
  47.9 0.9 stitch_pairs.3
  48.8 0.1 collective-permute-start.8
  48.9 0.0 collective-permute-done.1.halo_ref
  48.9 5.4 %collective-permute-start.9 = (f32[2,1,61,8,128]{4,3,2,1,0:T(8,128)S(1)}, f32[2,1,61,8,128]{4,3,2,1,0:T(8,128)S(1)}, u32[]{:S(2)}, u32[]{:S(2)}) collective-permute-start(f32[2,1,61,8,128]{4,3,2,1,0:T(8,128)S(1)} %get-tuple-element.50), channel_id=1, source_target_pairs={{0,48},{16,32},{32,16},{48,0},{64,112},{80,96},{96,80},{112,64},{1... | collective-permute-start | bytes 1499144 | tf_op jit(solution)/shard_map/ppermute | solution.py:407
  54.3 6.3 %phase_filter.5 = (f32[2,20,36,8,128]{4,3,2,1,0:T(8,128)S(1)}, f32[2,2,36,8,128]{4,3,2,1,0:T(8,128)S(1)}, f32[2,2,36,8,128]{4,3,2,1,0:T(8,128)S(1)}, f32[2,2,36,...) custom-call(s32[29]{0:T(128)S(1)} %stack.17.info, ...), custom_call_target="tpu_custom_call", output_to_operand_aliasing={{0}: (2, {})} | custom-call | flops 57500000 | bytes 4096 | tf_op jit(solution)/shard_map/phase_filter/pallas_call | solution.py:278
  60.6 0.0 collective-permute-done.10.r1
  60.6 0.0 collective-permute-done.11.r2
  60.6 0.0 collective-permute-done.12.r3
  60.6 0.9 stitch_pairs.4
  61.6 0.1 collective-permute-start.13
  61.7 0.5 collective-permute-start.14
  62.2 0.8 collective-permute-start.5
  63.0 0.0 collective-permute-done.8.refs_0_
  63.0 1.7 %collective-permute-start.6 = (f32[2,2,36,8,128]{4,3,2,1,0:T(8,128)S(1)}, f32[2,2,36,8,128]{4,3,2,1,0:T(8,128)S(1)}, u32[]{:S(2)}, u32[]{:S(2)}) collective-permute-start(f32[2,2,36,8,128]{4,3,2,1,0:T(8,128)S(1)} %get-tuple-element.47), channel_id=1, source_target_pairs={{0,128},{16,144},{32,160},{48,176},{64,192},{80,208},{96,224},{112... | collective-permute-start | bytes 1769480 | tf_op jit(solution)/shard_map/ppermute | solution.py:403
  64.7 12.6 %collective-permute-done.9.refs_1_ = f32[2,1,61,8,128]{4,3,2,1,0:T(8,128)S(1)} collective-permute-done((f32[2,1,61,8,128]{4,3,2,1,0:T(8,128)S(1)}, f32[2,1,61,8,128]{4,3,2,1,0:T(8,128)S(1)}, u32[]{:S(2)}, u32[]{:S(2)}) %collective-permute-start.9) | collective-permute-done | bytes 499744 | tf_op jit(solution)/shard_map/ppermute | solution.py:407
  77.3 0.0 collective-permute-start.7
  77.4 2.1 %collective-permute-done.13.refs_2_ = f32[2,1,61,8,128]{4,3,2,1,0:T(8,128)S(1)} collective-permute-done((f32[2,1,61,8,128]{4,3,2,1,0:T(8,128)S(1)}, f32[2,1,61,8,128]{4,3,2,1,0:T(8,128)S(1)}, u32[]{:S(2)}, u32[]{:S(2)}) %collective-permute-start.13) | collective-permute-done | bytes 499744 | tf_op jit(solution)/shard_map/ppermute | solution.py:407
  79.5 5.2 %ramp_filter.3 = (f32[2,2,2,2,8,8192]{5,4,3,2,1,0:T(8,128)}, f32[8,128]{1,0:T(8,128)S(1)}) custom-call(s32[29]{0:T(128)S(1)} %stack.17.info, f32[2,1,61,8,128]{4,3,2,1,0:T(8,128)S(1)} %collective-permute-done.8.refs_0_, f32[2,1,61,8,128]{4,3,2,1,0:T(8,128)S(1)} %collective-permute-done.9.refs_1_, f32[2,1,61,8,128]{4,3,2,1,0:T(8,128)S(1)} %collective-permute-done.13.refs_2_, ...), custom_call_target="tpu_custom_call" | custom-call | flops 23000000 | bytes 4096 | tf_op jit(solution)/shard_map/ramp_filter/pallas_call | solution.py:380
  84.7 9.5 %collective-permute-done.14.refs_0_ = f32[2,1,61,8,128]{4,3,2,1,0:T(8,128)S(1)} collective-permute-done((f32[2,1,61,8,128]{4,3,2,1,0:T(8,128)S(1)}, f32[2,1,61,8,128]{4,3,2,1,0:T(8,128)S(1)}, u32[]{:S(2)}, u32[]{:S(2)}) %collective-permute-start.14) | collective-permute-done | bytes 499744 | tf_op jit(solution)/shard_map/ppermute | solution.py:407
  94.2 0.0 collective-permute-done.5.r1
  94.2 0.0 collective-permute-done.7.r3
  94.2 2.1 %stitch_pairs.5 = (f32[2,2,61,8,128]{4,3,2,1,0:T(8,128)S(1)}, f32[2,2,61,8,128]{4,3,2,1,0:T(8,128)S(1)}, f32[8,128]{1,0:T(8,128)}) custom-call(s32[29]{0:T(128)S(1)} %stack.17.info, f32[2,2,36,8,128]{4,3,2,1,0:T(8,128)S(1)} %get-tuple-element.45.r0, f32[2,2,36,8,128]{4,3,2,1,0:T(8,128)S(1)} %collective-permute-done.5.r1, ...), custom_call_target="tpu_custom_call" | custom-call | flops 17250000 | bytes 4096 | tf_op jit(solution)/shard_map/stitch_pairs/pallas_call | solution.py:323
  96.2 0.0 collective-permute-start.15
  96.2 5.2 %ramp_filter.4 = (f32[2,2,2,2,8,8192]{5,4,3,2,1,0:T(8,128)}, f32[8,128]{1,0:T(8,128)}) custom-call(s32[29]{0:T(128)S(1)} %stack.17.info, f32[2,1,61,8,128]{4,3,2,1,0:T(8,128)S(1)} %collective-permute-done.14.refs_0_, f32[2,2,61,8,128]{4,3,2,1,0:T(8,128)S(1)} %get-tuple-element.61.refs_1_, ...), custom_call_target="tpu_custom_call", output_to_operand_aliasing={{0}: (9, {})} | custom-call | flops 23000000 | bytes 4096 | tf_op jit(solution)/shard_map/ramp_filter/pallas_call | solution.py:380
  101.5 0.0 collective-permute-done.15.refs_0_
  101.5 3.9 %ramp_filter.5 = (f32[2,2,2,2,8,8192]{5,4,3,2,1,0:T(8,128)}, f32[8,128]{1,0:T(8,128)}) custom-call(s32[29]{0:T(128)S(1)} %stack.17.info, f32[2,2,61,8,128]{4,3,2,1,0:T(8,128)S(1)} %collective-permute-done.15.refs_0_, f32[2,64,8,128]{3,2,1,0:T(8,128)S(1)} %copy-done.1, f32[512,128]{1,0:T(8,128)S(1)} %copy-done.2, ...), custom_call_target="tpu_custom_call", output_to_operand_aliasing={{0}: (8, {})} | custom-call | flops 23000000 | bytes 4096 | tf_op jit(solution)/shard_map/ramp_filter/pallas_call | solution.py:380
  (15 shorter events, 0.0 us)
Async XLA Ops:
  2.0 17.6 %collective-permute-start = (f32[2,16,4608]{2,1,0:T(8,128)S(1)}, f32[2,16,4608]{2,1,0:T(8,128)S(1)}, u32[]{:S(2)}, u32[]{:S(2)}) collective-permute-start(f32[2,16,4608]{2,1,0:T(8,128)S(1)} %bitcast.15), channel_id=1, source_target_pairs={{32,33},{48,49},{96,97},{112,113},{160,161},{176,177},{224,225},{2... | collective-permute-start | bytes 1769480 | tf_op jit(solution)/shard_map/ppermute | solution.py:418
  7.6 2.3 %copy-start = (f32[16,16,4608]{2,1,0:T(8,128)S(1)}, f32[16,16,4608]{2,1,0:T(8,128)}, u32[]{:S(2)}) copy-start(f32[16,16,4608]{2,1,0:T(8,128)} %param.10) | copy-start | bytes 14155780
  10.0 9.6 %copy-start.7 = (f32[5,5]{1,0:T(8,128)S(1)}, f32[5,5]{1,0:T(8,128)}, u32[]{:S(2)}) copy-start(f32[5,5]{1,0:T(8,128)} %taps_ref.5) | copy-start | bytes 304
  22.7 26.2 %collective-permute-start.1 = (f32[2,2,36,8,128]{4,3,2,1,0:T(8,128)S(1)}, f32[2,2,36,8,128]{4,3,2,1,0:T(8,128)S(1)}, u32[]{:S(2)}, u32[]{:S(2)}) collective-permute-start(f32[2,2,36,8,128]{4,3,2,1,0:T(8,128)S(1)} %get-tuple-element.38), channel_id=1, source_target_pairs={{0,1},{16,17},{64,65},{80,81},{128,129},{144,145},{192,193},{208,2... | collective-permute-start | bytes 1769480 | tf_op jit(solution)/shard_map/ppermute | solution.py:418
  29.5 8.6 %collective-permute-start.2 = (f32[1,2,36,8,128]{4,3,2,1,0:T(8,128)S(1)}, f32[1,2,36,8,128]{4,3,2,1,0:T(8,128)S(1)}, u32[]{:S(2)}, u32[]{:S(2)}) collective-permute-start(f32[1,2,36,8,128]{4,3,2,1,0:T(8,128)S(1)} %get-tuple-element.40), channel_id=1, source_target_pairs={{0,64},{16,80},{32,96},{48,112},{64,128},{80,144},{96,160},{112,17... | collective-permute-start | bytes 884744 | tf_op jit(solution)/shard_map/ppermute | solution.py:403
  29.6 8.7 %collective-permute-start.3 = (f32[1,2,36,8,128]{4,3,2,1,0:T(8,128)S(1)}, f32[1,2,36,8,128]{4,3,2,1,0:T(8,128)S(1)}, u32[]{:S(2)}, u32[]{:S(2)}) collective-permute-start(f32[1,2,36,8,128]{4,3,2,1,0:T(8,128)S(1)} %get-tuple-element.41), channel_id=1, source_target_pairs={{0,128},{16,144},{32,160},{48,176},{64,192},{80,208},{96,224},{112... | collective-permute-start | bytes 884744 | tf_op jit(solution)/shard_map/ppermute | solution.py:403
  31.8 16.1 %collective-permute-start.4 = (f32[1,2,36,8,128]{4,3,2,1,0:T(8,128)S(1)}, f32[1,2,36,8,128]{4,3,2,1,0:T(8,128)S(1)}, u32[]{:S(2)}, u32[]{:S(2)}) collective-permute-start(f32[1,2,36,8,128]{4,3,2,1,0:T(8,128)S(1)} %get-tuple-element.42), channel_id=1, source_target_pairs={{0,192},{16,208},{32,224},{48,240},{64,0},{80,16},{96,32},{112,48}... | collective-permute-start | bytes 884744 | tf_op jit(solution)/shard_map/ppermute | solution.py:403
  35.3 44.1 %copy-start.1 = (f32[2,64,8,128]{3,2,1,0:T(8,128)S(1)}, f32[2,64,8,128]{3,2,1,0:T(8,128)}, u32[]{:S(2)}) copy-start(f32[2,64,8,128]{3,2,1,0:T(8,128)} %constant.33.clone.refs_3_.refs_2_.refs_1_) | copy-start | bytes 1572868
  35.3 44.1 %copy-start.2 = (f32[512,128]{1,0:T(8,128)S(1)}, f32[512,128]{1,0:T(8,128)}, u32[]{:S(2)}) copy-start(f32[512,128]{1,0:T(8,128)} %constant.34.clone.refs_4_.refs_3_.refs_2_) | copy-start | bytes 786436
  35.3 44.1 %copy-start.3 = (bf16[256,256]{1,0:T(8,128)(2,1)S(1)}, bf16[256,256]{1,0:T(8,128)(2,1)}, u32[]{:S(2)}) copy-start(bf16[256,256]{1,0:T(8,128)(2,1)} %constant.38.clone.refs_8_.refs_7_.refs_6_) | copy-start | bytes 393220
  35.3 44.1 %copy-start.4 = (bf16[256,256]{1,0:T(8,128)(2,1)S(1)}, bf16[256,256]{1,0:T(8,128)(2,1)}, u32[]{:S(2)}) copy-start(bf16[256,256]{1,0:T(8,128)(2,1)} %constant.37.clone.refs_7_.refs_6_.refs_5_) | copy-start | bytes 393220
  35.3 44.1 %copy-start.5 = (bf16[256,256]{1,0:T(8,128)(2,1)S(1)}, bf16[256,256]{1,0:T(8,128)(2,1)}, u32[]{:S(2)}) copy-start(bf16[256,256]{1,0:T(8,128)(2,1)} %constant.36.clone.refs_6_.refs_5_.refs_4_) | copy-start | bytes 393220
  35.3 44.1 %copy-start.6 = (bf16[256,256]{1,0:T(8,128)(2,1)S(1)}, bf16[256,256]{1,0:T(8,128)(2,1)}, u32[]{:S(2)}) copy-start(bf16[256,256]{1,0:T(8,128)(2,1)} %constant.35.clone.refs_5_.refs_4_.refs_3_) | copy-start | bytes 393220
  35.3 25.3 %collective-permute-start.10 = (f32[1,2,36,8,128]{4,3,2,1,0:T(8,128)S(1)}, f32[1,2,36,8,128]{4,3,2,1,0:T(8,128)S(1)}, u32[]{:S(2)}, u32[]{:S(2)}) collective-permute-start(f32[1,2,36,8,128]{4,3,2,1,0:T(8,128)S(1)} %get-tuple-element.52), channel_id=1, source_target_pairs={{0,64},{16,80},{32,96},{48,112},{64,128},{80,144},{96,160},{112,17... | collective-permute-start | bytes 884744 | tf_op jit(solution)/shard_map/ppermute | solution.py:403
  38.1 22.5 %collective-permute-start.11 = (f32[1,2,36,8,128]{4,3,2,1,0:T(8,128)S(1)}, f32[1,2,36,8,128]{4,3,2,1,0:T(8,128)S(1)}, u32[]{:S(2)}, u32[]{:S(2)}) collective-permute-start(f32[1,2,36,8,128]{4,3,2,1,0:T(8,128)S(1)} %get-tuple-element.53), channel_id=1, source_target_pairs={{0,128},{16,144},{32,160},{48,176},{64,192},{80,208},{96,224},{112... | collective-permute-start | bytes 884744 | tf_op jit(solution)/shard_map/ppermute | solution.py:403
  38.3 22.3 %collective-permute-start.12 = (f32[1,2,36,8,128]{4,3,2,1,0:T(8,128)S(1)}, f32[1,2,36,8,128]{4,3,2,1,0:T(8,128)S(1)}, u32[]{:S(2)}, u32[]{:S(2)}) collective-permute-start(f32[1,2,36,8,128]{4,3,2,1,0:T(8,128)S(1)} %get-tuple-element.54), channel_id=1, source_target_pairs={{0,192},{16,208},{32,224},{48,240},{64,0},{80,16},{96,32},{112,48}... | collective-permute-start | bytes 884744 | tf_op jit(solution)/shard_map/ppermute | solution.py:403
  48.8 14.2 %collective-permute-start.8 = (f32[2,1,61,8,128]{4,3,2,1,0:T(8,128)S(1)}, f32[2,1,61,8,128]{4,3,2,1,0:T(8,128)S(1)}, u32[]{:S(2)}, u32[]{:S(2)}) collective-permute-start(f32[2,1,61,8,128]{4,3,2,1,0:T(8,128)S(1)} %get-tuple-element.49), channel_id=1, source_target_pairs={{0,32},{16,48},{32,0},{48,16},{64,96},{80,112},{96,64},{112,80},{1... | collective-permute-start | bytes 1499144 | tf_op jit(solution)/shard_map/ppermute | solution.py:407
  48.9 28.4 %collective-permute-start.9 = (f32[2,1,61,8,128]{4,3,2,1,0:T(8,128)S(1)}, f32[2,1,61,8,128]{4,3,2,1,0:T(8,128)S(1)}, u32[]{:S(2)}, u32[]{:S(2)}) collective-permute-start(f32[2,1,61,8,128]{4,3,2,1,0:T(8,128)S(1)} %get-tuple-element.50), channel_id=1, source_target_pairs={{0,48},{16,32},{32,16},{48,0},{64,112},{80,96},{96,80},{112,64},{1... | collective-permute-start | bytes 1499144 | tf_op jit(solution)/shard_map/ppermute | solution.py:407
  61.6 17.9 %collective-permute-start.13 = (f32[2,1,61,8,128]{4,3,2,1,0:T(8,128)S(1)}, f32[2,1,61,8,128]{4,3,2,1,0:T(8,128)S(1)}, u32[]{:S(2)}, u32[]{:S(2)}) collective-permute-start(f32[2,1,61,8,128]{4,3,2,1,0:T(8,128)S(1)} %get-tuple-element.56), channel_id=1, source_target_pairs={{0,32},{16,48},{32,0},{48,16},{64,96},{80,112},{96,64},{112,80},{1... | collective-permute-start | bytes 1499144 | tf_op jit(solution)/shard_map/ppermute | solution.py:407
  61.7 32.5 %collective-permute-start.14 = (f32[2,1,61,8,128]{4,3,2,1,0:T(8,128)S(1)}, f32[2,1,61,8,128]{4,3,2,1,0:T(8,128)S(1)}, u32[]{:S(2)}, u32[]{:S(2)}) collective-permute-start(f32[2,1,61,8,128]{4,3,2,1,0:T(8,128)S(1)} %get-tuple-element.59), channel_id=1, source_target_pairs={{0,48},{16,32},{32,16},{48,0},{64,112},{80,96},{96,80},{112,64},{1... | collective-permute-start | bytes 1499144 | tf_op jit(solution)/shard_map/ppermute | solution.py:407
  62.2 32.0 %collective-permute-start.5 = (f32[2,2,36,8,128]{4,3,2,1,0:T(8,128)S(1)}, f32[2,2,36,8,128]{4,3,2,1,0:T(8,128)S(1)}, u32[]{:S(2)}, u32[]{:S(2)}) collective-permute-start(f32[2,2,36,8,128]{4,3,2,1,0:T(8,128)S(1)} %get-tuple-element.46), channel_id=1, source_target_pairs={{0,64},{16,80},{32,96},{48,112},{64,128},{80,144},{96,160},{112,17... | collective-permute-start | bytes 1769480 | tf_op jit(solution)/shard_map/ppermute | solution.py:403
  63.0 31.1 %collective-permute-start.6 = (f32[2,2,36,8,128]{4,3,2,1,0:T(8,128)S(1)}, f32[2,2,36,8,128]{4,3,2,1,0:T(8,128)S(1)}, u32[]{:S(2)}, u32[]{:S(2)}) collective-permute-start(f32[2,2,36,8,128]{4,3,2,1,0:T(8,128)S(1)} %get-tuple-element.47), channel_id=1, source_target_pairs={{0,128},{16,144},{32,160},{48,176},{64,192},{80,208},{96,224},{112... | collective-permute-start | bytes 1769480 | tf_op jit(solution)/shard_map/ppermute | solution.py:403
  77.3 16.8 %collective-permute-start.7 = (f32[2,2,36,8,128]{4,3,2,1,0:T(8,128)S(1)}, f32[2,2,36,8,128]{4,3,2,1,0:T(8,128)S(1)}, u32[]{:S(2)}, u32[]{:S(2)}) collective-permute-start(f32[2,2,36,8,128]{4,3,2,1,0:T(8,128)S(1)} %get-tuple-element.48), channel_id=1, source_target_pairs={{0,192},{16,208},{32,224},{48,240},{64,0},{80,16},{96,32},{112,48}... | collective-permute-start | bytes 1769480 | tf_op jit(solution)/shard_map/ppermute | solution.py:403
  96.2 5.2 %collective-permute-start.15 = (f32[2,2,61,8,128]{4,3,2,1,0:T(8,128)S(1)}, f32[2,2,61,8,128]{4,3,2,1,0:T(8,128)S(1)}, u32[]{:S(2)}, u32[]{:S(2)}) collective-permute-start(f32[2,2,61,8,128]{4,3,2,1,0:T(8,128)S(1)} %get-tuple-element.60), channel_id=1, source_target_pairs={{0,16},{16,0},{32,48},{48,32},{64,80},{80,64},{96,112},{112,96},{1... | collective-permute-start | bytes 2998280 | tf_op jit(solution)/shard_map/ppermute | solution.py:407
